TPU v7x, 32 devices: a whole 2x2x4 slice. The times are simulated.
32 devices in a mesh: pb: 4 (over y, x), db: 8 (over z, core).
Axes of the slice: x: 2, y: 2, z: 4, core: 2. Of those that a mesh axis runs over, the one named last changes fastest.
Arguments:
- database: bfloat16 [2048, 768], P('db')
- neighbours: int32 [2048, 16], P('db'), may hold values from 0 to 2047, as said below
- valid_count: int32 [2048], P('db'), may hold values from 9 to 16, as said below
- queries: bfloat16 [65536, 768], P('pb'), may hold values from -6 to 6
Outputs:
- augmented: bfloat16 [2048, 768], P('db')
- best_score: float32 [65536], P('pb')
Inputs may be any that keep to these rules, and one draw needn't show every extreme that they name: `neighbours`: every entry is a row number of the whole database, also in slots at or past valid_count (those carry no weight). The owner of row r is r // 256. In each aligned block of 64 rows, at most 256 of its 1024 entries name rows of one owner, and in every block some owner is named by exactly 256 entries. `valid_count`: every aligned block of 64 rows holds a row with 16 valid slots.
All inputs are finite; a program needn't handle non-finite values.
Results may differ from a plain program's by a relative error of at most 0.0028.
Values may be sent and summed in bfloat16 or wider, within the bound.
No kernel may reach another device: no remote copies, remote signals or barrier semaphores. Data moves between devices by JAX's collectives and lax.ppermute only.
A program may use at most 128 MiB of HBM per device.

v0:
```python
import functools

import jax
import jax.numpy as jnp
from jax import lax
from jax.experimental import pallas as pl
from jax.experimental.pallas import tpu as pltpu
from jax.sharding import PartitionSpec as P

epsilon = 1e-06
MIB = 1 << 20


def column_inverse(values):
    squares = jnp.sum(values * values, axis=-1, keepdims=True)
    return lax.rsqrt(squares + epsilon)


def as_row(column):
    wide = jnp.broadcast_to(column, (column.shape[0], 128))
    return wide.T[0:1, :]


def position_of():
    owner = lax.axis_index("db")
    return lax.axis_index("pb"), owner // 2, owner % 2


def fetch_queries(queries_ref, held_ref, part, sem):
    rows = held_ref.shape[0]
    half = queries_ref.shape[0] // 2
    start = pl.multiple_of(position_of()[2] * half + part * rows, rows)
    return pltpu.make_async_copy(queries_ref.at[pl.ds(start, rows), :], held_ref, sem)


def count_kernel(
    planes, twin_ref, own_ref, database_ref, queries_ref, adjacent_ref, far_ref, *rest
):
    count_refs = rest[:-7]
    copy_ref, held_ref, near_ref, tiles_ref, lows_ref, sem, queries_sem = rest[-7:]
    rows = copy_ref.shape[0]
    fanout = own_ref.shape[0] * 128 // rows
    quarter = rows // 4
    span = (planes - 1) * quarter
    starts = [0]
    for count_ref in count_refs:
        starts.append(starts[-1] + count_ref.shape[1])
    copy = pltpu.make_async_copy(database_ref, copy_ref, sem)
    copy.start()
    queries = fetch_queries(queries_ref, held_ref, 0, queries_sem)
    queries.start()
    near_ref[...] = adjacent_ref[: near_ref.shape[0], :]
    me, plane, core = position_of()
    bits = rows.bit_length() - 1
    lines = own_ref.shape[0]
    for number, wanted_ref in enumerate((twin_ref, own_ref)):
        wanted = wanted_ref[...]
        owner = wanted >> bits
        side = owner & 1
        row = wanted & (rows - 1)
        cross = (row >> (bits - 2)) ^ me
        inner = row & (quarter - 1)
        away = (owner >> 1) ^ plane
        straight = (away - 1) * quarter + inner
        start = jnp.where(cross == 3, starts[3], starts[3] + span)
        start = jnp.where(cross == 1 + core, starts[2], start)
        position = jnp.where(cross == 0, starts[1], start) + straight
        position = jnp.where(away == 0, row, position)
        position = jnp.where((wanted >= 0) & (side == core), position, -1)
        tiles_ref[number * lines : (number + 1) * lines, :] = position >> 7
        lows_ref[number * lines : (number + 1) * lines, :] = position & 127

    group = 16
    height = starts[-1] // 128 * group
    width = group * fanout
    at_row = lax.broadcasted_iota(jnp.int32, (height, width), 0)
    at_lane = lax.broadcasted_iota(jnp.int32, (height, width), 1)
    target = jnp.where(at_lane // fanout == at_row % group, at_row // group, -2)
    low_of = lax.broadcasted_iota(jnp.int32, (128, width), 0)
    each = width // 128

    def flat(ref, at):
        return jnp.concatenate([ref[pl.ds(at * each + i, 1), :] for i in range(each)], axis=1)

    def body(at, carry):
        tile = jnp.broadcast_to(flat(tiles_ref, at), (height, width))
        low = jnp.broadcast_to(flat(lows_ref, at), (128, width))
        left = jnp.where(tile == target, 1.0, 0.0).astype(jnp.bfloat16)
        right = jnp.where(low == low_of, 1.0, 0.0).astype(jnp.bfloat16)
        counts = lax.dot_general(
            left, right, (((1,), (1,)), ((), ())), preferred_element_type=jnp.float32
        ).astype(jnp.bfloat16)
        start = pl.ds(pl.multiple_of(at * group, group), group)
        tile = 0
        for count_ref in count_refs:
            for t in range(count_ref.shape[1] // 128):
                count_ref[start, t * 128 : (t + 1) * 128] = counts[tile * group : (tile + 1) * group, :]
                tile += 1
        return carry

    lax.fori_loop(0, 2 * rows // group, body, 0, unroll=4)
    copy.wait()
    queries.wait()


def join_kernel(pieces, *rest):
    out_ref = rest[-1]
    quarter = out_ref.shape[0] // pieces
    for i in range(pieces):
        out_ref[i * quarter : (i + 1) * quarter, :] = rest[i][...]


def spread_terms(dest, dest_inverse, block, far, counts):
    products = lax.dot_general(
        dest, block, (((1,), (1,)), ((), ())), preferred_element_type=jnp.float32
    )
    cosine = products * dest_inverse * far
    halfway = (1.0 + cosine) * 0.5
    weight = halfway * halfway * halfway
    coefficient = (weight * far).astype(jnp.bfloat16).astype(jnp.float32)
    spread = coefficient * counts.astype(jnp.float32)
    high = spread.astype(jnp.bfloat16)
    low = (spread - high.astype(jnp.float32)).astype(jnp.bfloat16)
    return jnp.dot(high, block, preferred_element_type=jnp.float32) + jnp.dot(
        low, block, preferred_element_type=jnp.float32
    )


def sums_kernel(blocks, twin_ref, own_ref, counts_ref, *rest):
    block_refs, rest = rest[:blocks], rest[blocks:]
    *before_ref, out_ref = rest
    rows = own_ref.shape[0]
    block = jnp.concatenate([ref[...] for ref in block_refs], axis=0) if blocks > 1 else block_refs[0][...]
    far = as_row(column_inverse(block.astype(jnp.float32)))
    for number, dest_ref in enumerate((twin_ref, own_ref)):
        lines = slice(number * rows, (number + 1) * rows)
        dest = dest_ref[...]
        values = dest.astype(jnp.float32)
        dest_inverse = column_inverse(values)
        terms = spread_terms(dest, dest_inverse, block, far, counts_ref[lines, : block.shape[0]])
        if before_ref:
            terms = before_ref[0][lines, :] + terms
        elif number == 1:
            terms = terms + values * dest_inverse
        out_ref[lines, :] = terms


def late_kernel(number, dest_ref, early_ref, counts_ref, *rest):
    out_ref = rest[-1]
    rows = dest_ref.shape[0]
    lines = slice(number * rows, (number + 1) * rows)
    block = jnp.concatenate([ref[...] for ref in rest[:-1]], axis=0)
    far = as_row(column_inverse(block.astype(jnp.float32)))
    dest = dest_ref[...]
    dest_inverse = column_inverse(dest.astype(jnp.float32))
    terms = spread_terms(dest, dest_inverse, block, far, counts_ref[lines, : block.shape[0]])
    out_ref[...] = early_ref[lines, :] + terms


def score_kernel(own_a_ref, own_b_ref, twin_a_ref, twin_b_ref, first_ref, queries_ref, augmented_ref, best_ref, rows_ref, held_ref, sems):
    rows = own_a_ref.shape[0]
    size = held_ref.shape[0] // sems.shape[0]
    fetched = lambda i: held_ref.at[pl.ds(i * size, size), :]
    ahead = first_ref.shape[0] // size
    fetches = [
        fetch_queries(queries_ref, fetched(i), ahead + i, sems.at[i]) for i in range(sems.shape[0])
    ]
    for fetch in fetches:
        fetch.start()
    for number, (a_ref, b_ref) in enumerate(((own_a_ref, own_b_ref), (twin_a_ref, twin_b_ref))):
        summed = a_ref[...] + b_ref[...]
        augmented = (summed * column_inverse(summed)).astype(jnp.bfloat16)
        if number == 0:
            augmented_ref[...] = augmented
        rows_ref[number * rows : (number + 1) * rows, :] = augmented

    line_of = 0
    for part in range(1 + sems.shape[0]):
        if part == 0:
            block_ref = first_ref
        else:
            fetches[part - 1].wait()
            block_ref = fetched(part - 1)
        height = block_ref.shape[0]
        step = min(1024, height)
        tile = min(2048, height)
        before = line_of
        line_of += height // 128

        @pl.loop(0, height // tile)
        def _(i):
            at = pl.multiple_of(i * tile, tile)
            line = pl.multiple_of(before + i * (tile // 128), tile // 128)
            found = []
            for first in range(0, tile, step):
                scores = lax.dot_general(
                    rows_ref[...],
                    block_ref[pl.ds(at + first, step), :],
                    (((1,), (1,)), ((), ())),
                    preferred_element_type=jnp.float32,
                )
                best = jnp.max(scores, axis=0, keepdims=True)
                found += [best[:, part : part + 128] for part in range(0, step, 128)]
            best_ref[pl.ds(line, tile // 128), :] = jnp.concatenate(found, axis=0)


def local(database, neighbours, valid_count, queries):
    rows, features = database.shape
    fanout = neighbours.shape[1]
    count = queries.shape[0]
    owners = lax.axis_size("db")
    panels = lax.axis_size("pb")
    assert panels == 4 and owners % 4 == 0 and owners & (owners - 1) == 0
    planes = owners // 2
    quarter = rows // panels
    me = lax.axis_index("pb")
    core = lax.axis_index("db") % 2

    def along(value, apart):
        pairs = [(i, ((i // 2) ^ apart) * 2 + i % 2) for i in range(owners)]
        return lax.ppermute(value, "db", pairs)

    def along_all(value, adjacent):
        pieces = {0: value}
        apart = planes // 2
        while apart:
            for other in sorted(pieces):
                joined = apart == 1 and other == 0
                pieces[other ^ apart] = adjacent if joined else along(pieces[other], apart)
            apart //= 2
        return [pieces[apart] for apart in range(1, planes)]

    def swap(value):
        return lax.ppermute(value, "db", [(i, i ^ 1) for i in range(owners)])

    def cross(value, bits):
        pairs = []
        for panel in range(panels):
            for i in range(owners):
                pairs.append((panel * owners + i, (panel ^ bits[i % 2]) * owners + i))
        return lax.ppermute(value, ("pb", "db"), pairs)

    mine = lax.dynamic_slice_in_dim(database, me * quarter, quarter, 0)
    other = lax.dynamic_slice_in_dim(database, (me ^ 3) * quarter, quarter, 0)
    adjacent = along(jnp.concatenate([mine, other], axis=0), 1)
    near = along_all(mine, adjacent[:quarter])
    across = along_all(other, adjacent[quarter:])
    twin = swap(database)
    vmem = pl.BlockSpec(memory_space=pltpu.VMEM)
    slots = jnp.arange(fanout, dtype=jnp.int32)[None, :]
    wanted = jnp.where(slots < valid_count[:, None], neighbours, -1).reshape(-1, 128)
    twin_wanted = swap(wanted)
    padded = lambda size: (size + 127) // 128 * 128
    span = (planes - 1) * quarter
    widths = (rows, span, span, 2 * span)
    *counts, own, first_queries, near_first = pl.pallas_call(
        functools.partial(count_kernel, planes),
        out_shape=[
            jax.ShapeDtypeStruct((2 * rows, padded(width)), jnp.bfloat16) for width in widths
        ]
        + [
            jax.ShapeDtypeStruct((rows, features), jnp.bfloat16),
            jax.ShapeDtypeStruct((count // 8, features), jnp.bfloat16),
            jax.ShapeDtypeStruct((quarter, features), jnp.bfloat16),
        ],
        in_specs=[vmem, vmem] + [pl.BlockSpec(memory_space=pltpu.HBM)] * 2 + [vmem] * 2,
        out_specs=[vmem] * 7,
        scratch_shapes=[
            pltpu.VMEM((2 * wanted.shape[0], 128), jnp.int32),
            pltpu.VMEM((2 * wanted.shape[0], 128), jnp.int32),
            pltpu.SemaphoreType.DMA(()),
            pltpu.SemaphoreType.DMA(()),
        ],
        compiler_params=pltpu.CompilerParams(vmem_limit_bytes=30 * MIB),
        cost_estimate=pl.CostEstimate(flops=1<<30, bytes_accessed=4 * rows * rows, transcendentals=0),
        name="counts",
    )(twin_wanted, wanted, database, queries, adjacent, near[planes // 2 - 1])
    near = pl.pallas_call(
        functools.partial(join_kernel, planes - 1),
        out_shape=jax.ShapeDtypeStruct((span, features), jnp.bfloat16),
        in_specs=[vmem] * planes,
        out_specs=vmem,
        compiler_params=pltpu.CompilerParams(vmem_limit_bytes=8 * MIB),
        name="join",
    )(near_first, *near[1:], across[planes // 2 - 1])
    beside = cross(near, (1, 2))
    behind = cross(near, (2, 1))

    def sums(name, counts, blocks, before=None):
        out = [jax.ShapeDtypeStruct((2 * rows, features), jnp.float32)]
        operands = [twin, own, counts, *blocks]
        specs = [vmem] * len(operands)
        if before is not None:
            operands.append(before)
            specs.append(vmem)
        return pl.pallas_call(
            functools.partial(sums_kernel, len(blocks)),
            out_shape=out,
            in_specs=specs,
            out_specs=[vmem] * len(out),
            compiler_params=pltpu.CompilerParams(vmem_limit_bytes=30 * MIB),
            cost_estimate=pl.CostEstimate(flops=1<<26, bytes_accessed=4 * rows * rows, transcendentals=0),
            name=name,
        )(*operands)

    (total,) = sums("own_sums", counts[0], [own])
    (total,) = sums("near_sums", counts[1], [near], total)
    (total,) = sums("beside_sums", counts[2], [beside], total)

    def late(number, dest):
        return pl.pallas_call(
            functools.partial(late_kernel, number),
            out_shape=jax.ShapeDtypeStruct((rows, features), jnp.float32),
            in_specs=[vmem] * (4 + len(across)),
            out_specs=vmem,
            compiler_params=pltpu.CompilerParams(vmem_limit_bytes=30 * MIB),
            name="late_sums",
        )(dest, total, counts[3], *across, behind)

    twin_a = late(0, twin)
    own_b = swap(twin_a)
    own_a = late(1, own)
    twin_b = swap(own_a)

    half = count // 2
    augmented, best = pl.pallas_call(
        score_kernel,
        out_shape=[
            jax.ShapeDtypeStruct((rows, features), jnp.bfloat16),
            jax.ShapeDtypeStruct((half // 128, 128), jnp.float32),
        ],
        in_specs=[vmem] * 5 + [pl.BlockSpec(memory_space=pltpu.HBM)],
        out_specs=[vmem, vmem],
        scratch_shapes=[
            pltpu.VMEM((2 * rows, features), jnp.bfloat16),
            pltpu.VMEM((count // 8 * 3, features), jnp.bfloat16),
            pltpu.SemaphoreType.DMA((3,)),
        ],
        compiler_params=pltpu.CompilerParams(vmem_limit_bytes=40 * MIB),
        cost_estimate=pl.CostEstimate(
            flops=2 * count * rows * features, bytes_accessed=count * features, transcendentals=0
        ),
        name="scores",
    )(own_a, own_b, twin_a, twin_b, first_queries, queries)

    received = [along(best, apart) for apart in range(planes - 1, 0, -1)]
    for value in received:
        best = jnp.maximum(best, value)
    other_half = swap(best)
    first = jnp.where(core == 0, best, other_half)
    second = jnp.where(core == 0, other_half, best)
    return augmented, jnp.concatenate([first, second], axis=0).reshape(count)


def solution(mesh):
    return jax.shard_map(
        local,
        mesh=mesh,
        in_specs=(P("db", None), P("db", None), P("db"), P("pb", None)),
        out_specs=(P("db", None), P("pb")),
        check_vma=False,
    )
```

profile of v0, /device:TPU:0, one launch (start us, length us, event | category | flops | bytes accessed | tf_op | source)
XLA Modules:
  0.0 51.2 jit_solution(2562745055128599031)
XLA Ops:
  0.6 1.0 %constant_dynamic-slice_fusion.1 = (bf16[64,768]{1,0:T(8,128)(2,1)S(1)}, bf16[64,768]{1,0:T(8,128)(2,1)S(1)}) fusion(bf16[256,768]{1,0:T(8,128)(2,1)} %database_ref.1, s32[]{:T(128)S(6)} %select_n.30, s32[]{:T(128)S(6)} %select_n.31), kind=kLoop, calls=%fused_computation.8 | loop fusion | bytes 393224 | tf_op jit(solution)/shard_map/dynamic_slice | solution.py:243
  1.6 4.1 %collective-permute-start.2 = (bf16[64,768]{1,0:T(8,128)(2,1)S(1)}, bf16[64,768]{1,0:T(8,128)(2,1)S(1)}, u32[]{:S(2)}, u32[]{:S(2)}) collective-permute-start(bf16[64,768]{1,0:T(8,128)(2,1)S(1)} %get-tuple-element.20), channel_id=1, source_target_pairs={{0,4},{1,5},{2,6},{3,7},{4,0},{5,1},{6,2},{7,3},{8,12},{9,13},{10,... | collective-permute-start | bytes 294920 | tf_op jit(solution)/shard_map/ppermute | solution.py:221
  5.7 1.6 %collective-permute-start.1 = (bf16[128,768]{1,0:T(8,128)(2,1)S(1)}, bf16[128,768]{1,0:T(8,128)(2,1)S(1)}, u32[]{:S(2)}, u32[]{:S(2)}) collective-permute-start(bf16[128,768]{1,0:T(8,128)(2,1)S(1)} %pad_maximum_fusion), channel_id=1, source_target_pairs={{0,2},{1,3},{2,0},{3,1},{4,6},{5,7},{6,4},{7,5},{8,10},{9,11},{10,... | collective-permute-start | bytes 589832 | tf_op jit(solution)/shard_map/ppermute | solution.py:221
  7.4 0.7 %fusion = s32[256,16]{0,1:T(8,128)S(1)} fusion(s32[256,16]{0,1:T(8,128)} %param.5, s32[256]{0:T(256)} %param.6), kind=kLoop, calls=%fused_computation.4 | loop fusion | flops 8192 | bytes 33792 | tf_op jit(solution)/shard_map/jit(_where)/select_n | solution.py:251
  8.1 0.1 copy.7
  8.2 0.1 reshape.11.own_ref
  8.4 0.5 collective-permute-start.3
  8.9 0.3 collective-permute-start.5
  9.2 1.3 %collective-permute-done.2.far_ref.rest_1_ = bf16[64,768]{1,0:T(8,128)(2,1)S(1)} collective-permute-done((bf16[64,768]{1,0:T(8,128)(2,1)S(1)}, bf16[64,768]{1,0:T(8,128)(2,1)S(1)}, u32[]{:S(2)}, u32[]{:S(2)}) %collective-permute-start.2) | collective-permute-done | bytes 98336 | tf_op jit(solution)/shard_map/ppermute | solution.py:221
  10.5 1.0 %collective-permute-start.4 = (bf16[64,768]{1,0:T(8,128)(2,1)S(1)}, bf16[64,768]{1,0:T(8,128)(2,1)S(1)}, u32[]{:S(2)}, u32[]{:S(2)}) collective-permute-start(bf16[64,768]{1,0:T(8,128)(2,1)S(1)} %collective-permute-done.2.far_ref.rest_1_), channel_id=1, source_target_pairs={{0,2},{1,3},{2,0},{3,1},{4,6},{5,7},{6,4},{7,5},{8,10},{9,11},{10,... | collective-permute-start | bytes 294920 | tf_op jit(solution)/shard_map/ppermute | solution.py:221
  11.5 4.0 %collective-permute-done.1.adjacent_ref = bf16[128,768]{1,0:T(8,128)(2,1)S(1)} collective-permute-done((bf16[128,768]{1,0:T(8,128)(2,1)S(1)}, bf16[128,768]{1,0:T(8,128)(2,1)S(1)}, u32[]{:S(2)}, u32[]{:S(2)}) %collective-permute-start.1) | collective-permute-done | bytes 196640 | tf_op jit(solution)/shard_map/ppermute | solution.py:221
  15.5 1.0 %copy-done = bf16[256,768]{1,0:T(8,128)(2,1)S(1)} copy-done((bf16[256,768]{1,0:T(8,128)(2,1)S(1)}, bf16[256,768]{1,0:T(8,128)(2,1)}, u32[]{:S(2)}) %copy-start) | copy-done | bytes 393240
  16.5 2.3 %counts.1 = (bf16[512,256]{1,0:T(8,128)(2,1)S(1)}, bf16[512,256]{1,0:T(8,128)(2,1)S(1)}, bf16[512,256]{1,0:T(8,128)(2,1)S(1)}, bf16[512,384]{1,0:T(8,128)(2,1)S(...) custom-call(s32[32,128]{1,0:T(8,128)S(1)} %collective-permute-done.twin_ref, ...), custom_call_target="tpu_custom_call" | custom-call | flops 1073741824 | bytes 262144 | tf_op jit(solution)/shard_map/counts/pallas_call | solution.py:256
  18.8 1.8 %collective-permute-start.6 = (bf16[192,768]{1,0:T(8,128)(2,1)S(1)}, bf16[192,768]{1,0:T(8,128)(2,1)S(1)}, u32[]{:S(2)}, u32[]{:S(2)}) collective-permute-start(bf16[192,768]{1,0:T(8,128)(2,1)S(1)} %join.1.rest_0_), channel_id=1, source_target_pairs={{0,8},{1,17},{2,10},{3,19},{4,12},{5,21},{6,14},{7,23},{8,0},{9,25... | collective-permute-start | bytes 884744 | tf_op jit(solution)/shard_map/ppermute | solution.py:241
  20.6 1.5 %collective-permute-start.8 = (bf16[192,768]{1,0:T(8,128)(2,1)S(1)}, bf16[192,768]{1,0:T(8,128)(2,1)S(1)}, u32[]{:S(2)}, u32[]{:S(2)}) collective-permute-start(bf16[192,768]{1,0:T(8,128)(2,1)S(1)} %join.1.rest_0_), channel_id=1, source_target_pairs={{0,16},{1,9},{2,18},{3,11},{4,20},{5,13},{6,22},{7,15},{8,24},{9,1... | collective-permute-start | bytes 884744 | tf_op jit(solution)/shard_map/ppermute | solution.py:241
  22.1 1.1 %own_sums.1.rest_1_ = f32[512,768]{1,0:T(8,128)S(1)} custom-call(bf16[256,768]{1,0:T(8,128)(2,1)S(1)} %collective-permute-done.3.twin_ref.dest_ref, bf16[256,768]{1,0:T(8,128)(2,1)S(1)} %get-tuple-element.11.own_ref.rest_0_.dest_ref, bf16[512,256]{1,0:T(8,128)(2,1)S(1)} %get-tuple-element.15.counts_ref, ...), custom_call_target="tpu_custom_call" | custom-call | flops 67108864 | bytes 262144 | tf_op jit(solution)/shard_map/own_sums/pallas_call | solution.py:296
  23.3 1.1 %near_sums.1.rest_1_ = f32[512,768]{1,0:T(8,128)S(1)} custom-call(bf16[256,768]{1,0:T(8,128)(2,1)S(1)} %collective-permute-done.3.twin_ref.dest_ref, bf16[256,768]{1,0:T(8,128)(2,1)S(1)} %get-tuple-element.11.own_ref.rest_0_.dest_ref, bf16[512,256]{1,0:T(8,128)(2,1)S(1)} %get-tuple-element.14.counts_ref, bf16[192,768]{1,0:T(8,128)(2,1)S(1)} %join.1.rest_0_, ...), custom_call_target="tpu_custom_call" | custom-call | flops 67108864 | bytes 262144 | tf_op jit(solution)/shard_map/near_sums/pallas_call | solution.py:296
  24.4 2.2 %collective-permute-done.6.rest_0_ = bf16[192,768]{1,0:T(8,128)(2,1)S(1)} collective-permute-done((bf16[192,768]{1,0:T(8,128)(2,1)S(1)}, bf16[192,768]{1,0:T(8,128)(2,1)S(1)}, u32[]{:S(2)}, u32[]{:S(2)}) %collective-permute-start.6) | collective-permute-done | bytes 294944 | tf_op jit(solution)/shard_map/ppermute | solution.py:241
  26.6 1.1 %beside_sums.1.early_ref = f32[512,768]{1,0:T(8,128)S(1)} custom-call(bf16[256,768]{1,0:T(8,128)(2,1)S(1)} %collective-permute-done.3.twin_ref.dest_ref, bf16[256,768]{1,0:T(8,128)(2,1)S(1)} %get-tuple-element.11.own_ref.rest_0_.dest_ref, bf16[512,256]{1,0:T(8,128)(2,1)S(1)} %get-tuple-element.12.counts_ref, ...), custom_call_target="tpu_custom_call" | custom-call | flops 67108864 | bytes 262144 | tf_op jit(solution)/shard_map/beside_sums/pallas_call | solution.py:296
  27.8 1.1 %late_sums.3.twin_a_ref = f32[256,768]{1,0:T(8,128)S(1)} custom-call(bf16[256,768]{1,0:T(8,128)(2,1)S(1)} %collective-permute-done.3.twin_ref.dest_ref, f32[512,768]{1,0:T(8,128)S(1)} %beside_sums.1.early_ref, bf16[512,384]{1,0:T(8,128)(2,1)S(1)} %get-tuple-element.16.counts_ref, bf16[64,768]{1,0:T(8,128)(2,1)S(1)} %slice.4.rest_0_, ...), custom_call_target="tpu_custom_call" | custom-call | tf_op jit(solution)/shard_map/late_sums/pallas_call | solution.py:311
  28.9 1.1 %late_sums.2.own_a_ref = f32[256,768]{1,0:T(8,128)S(1)} custom-call(bf16[256,768]{1,0:T(8,128)(2,1)S(1)} %get-tuple-element.11.own_ref.rest_0_.dest_ref, f32[512,768]{1,0:T(8,128)S(1)} %beside_sums.1.early_ref, bf16[512,384]{1,0:T(8,128)(2,1)S(1)} %get-tuple-element.16.counts_ref, bf16[64,768]{1,0:T(8,128)(2,1)S(1)} %slice.4.rest_0_, ...), custom_call_target="tpu_custom_call" | custom-call | tf_op jit(solution)/shard_map/late_sums/pallas_call | solution.py:311
  30.0 0.6 %collective-permute-start.10 = (f32[256,768]{1,0:T(8,128)S(1)}, f32[256,768]{1,0:T(8,128)S(1)}, u32[]{:S(2)}, u32[]{:S(2)}) collective-permute-start(f32[256,768]{1,0:T(8,128)S(1)} %late_sums.2.own_a_ref), channel_id=1, source_target_pairs={{0,1},{1,0},{2,3},{3,2},{4,5},{5,4},{6,7},{7,6},{8,9},{9,8},{10,11... | collective-permute-start | bytes 2359304 | tf_op jit(solution)/shard_map/ppermute | solution.py:234
  30.5 0.6 %collective-permute-done.9.own_b_ref = f32[256,768]{1,0:T(8,128)S(1)} collective-permute-done((f32[256,768]{1,0:T(8,128)S(1)}, f32[256,768]{1,0:T(8,128)S(1)}, u32[]{:S(2)}, u32[]{:S(2)}) %collective-permute-start.9) | collective-permute-done | bytes 786464 | tf_op jit(solution)/shard_map/ppermute | solution.py:234
  31.2 1.3 %collective-permute-done.10.twin_b_ref = f32[256,768]{1,0:T(8,128)S(1)} collective-permute-done((f32[256,768]{1,0:T(8,128)S(1)}, f32[256,768]{1,0:T(8,128)S(1)}, u32[]{:S(2)}, u32[]{:S(2)}) %collective-permute-start.10) | collective-permute-done | bytes 786464 | tf_op jit(solution)/shard_map/ppermute | solution.py:234
  32.5 9.0 %scores.1 = (bf16[256,768]{1,0:T(8,128)(2,1)}, f32[64,128]{1,0:T(8,128)S(1)}) custom-call(f32[256,768]{1,0:T(8,128)S(1)} %late_sums.2.own_a_ref, f32[256,768]{1,0:T(8,128)S(1)} %collective-permute-done.9.own_b_ref, f32[256,768]{1,0:T(8,128)S(1)} %late_sums.3.twin_a_ref, f32[256,768]{1,0:T(8,128)S(1)} %collective-permute-done.10.twin_b_ref, ...), custom_call_target="tpu_custom_call" | custom-call | flops 6442450944 | bytes 12582912 | tf_op jit(solution)/shard_map/scores/pallas_call | solution.py:326
  41.5 2.9 %collective-permute-start.11 = (f32[64,128]{1,0:T(8,128)S(1)}, f32[64,128]{1,0:T(8,128)S(1)}, u32[]{:S(2)}, u32[]{:S(2)}) collective-permute-start(f32[64,128]{1,0:T(8,128)S(1)} %get-tuple-element.19), channel_id=1, source_target_pairs={{0,6},{1,7},{2,4},{3,5},{4,2},{5,3},{6,0},{7,1},{8,14},{9,15},{10,... | collective-permute-start | bytes 98312 | tf_op jit(solution)/shard_map/ppermute | solution.py:221
  44.4 0.3 collective-permute-start.12
  44.7 1.2 %collective-permute-start.13 = (f32[64,128]{1,0:T(8,128)S(1)}, f32[64,128]{1,0:T(8,128)S(1)}, u32[]{:S(2)}, u32[]{:S(2)}) collective-permute-start(f32[64,128]{1,0:T(8,128)S(1)} %get-tuple-element.19), channel_id=1, source_target_pairs={{0,2},{1,3},{2,0},{3,1},{4,6},{5,7},{6,4},{7,5},{8,10},{9,11},{10,... | collective-permute-start | bytes 98312 | tf_op jit(solution)/shard_map/ppermute | solution.py:221
  46.0 1.6 %collective-permute-done.11 = f32[64,128]{1,0:T(8,128)S(1)} collective-permute-done((f32[64,128]{1,0:T(8,128)S(1)}, f32[64,128]{1,0:T(8,128)S(1)}, u32[]{:S(2)}, u32[]{:S(2)}) %collective-permute-start.11) | collective-permute-done | bytes 32800 | tf_op jit(solution)/shard_map/ppermute | solution.py:221
  47.6 1.6 %collective-permute-done.12 = f32[64,128]{1,0:T(8,128)S(1)} collective-permute-done((f32[64,128]{1,0:T(8,128)S(1)}, f32[64,128]{1,0:T(8,128)S(1)}, u32[]{:S(2)}, u32[]{:S(2)}) %collective-permute-start.12) | collective-permute-done | bytes 32800 | tf_op jit(solution)/shard_map/ppermute | solution.py:221
  49.3 1.2 %collective-permute-done.14 = f32[64,128]{1,0:T(8,128)S(1)} collective-permute-done((f32[64,128]{1,0:T(8,128)S(1)}, f32[64,128]{1,0:T(8,128)S(1)}, u32[]{:S(2)}, u32[]{:S(2)}) %collective-permute-start.14) | collective-permute-done | bytes 32800 | tf_op jit(solution)/shard_map/ppermute | solution.py:234
  50.5 0.6 %maximum_bitcast_fusion = f32[16384]{0:T(1024)} fusion(f32[64,128]{1,0:T(8,128)S(1)} %get-tuple-element.23, f32[64,128]{1,0:T(8,128)S(1)} %get-tuple-element.22), kind=kLoop, calls=%fused_computation.1 | loop fusion | flops 16384 | bytes 131072 | tf_op jit(solution)/shard_map/reshape | solution.py:352
  (17 shorter events, 0.3 us)
Async XLA Ops:
  1.6 8.9 %collective-permute-start.2 = (bf16[64,768]{1,0:T(8,128)(2,1)S(1)}, bf16[64,768]{1,0:T(8,128)(2,1)S(1)}, u32[]{:S(2)}, u32[]{:S(2)}) collective-permute-start(bf16[64,768]{1,0:T(8,128)(2,1)S(1)} %get-tuple-element.20), channel_id=1, source_target_pairs={{0,4},{1,5},{2,6},{3,7},{4,0},{5,1},{6,2},{7,3},{8,12},{9,13},{10,... | collective-permute-start | bytes 294920 | tf_op jit(solution)/shard_map/ppermute | solution.py:221
  5.7 9.7 %collective-permute-start.1 = (bf16[128,768]{1,0:T(8,128)(2,1)S(1)}, bf16[128,768]{1,0:T(8,128)(2,1)S(1)}, u32[]{:S(2)}, u32[]{:S(2)}) collective-permute-start(bf16[128,768]{1,0:T(8,128)(2,1)S(1)} %pad_maximum_fusion), channel_id=1, source_target_pairs={{0,2},{1,3},{2,0},{3,1},{4,6},{5,7},{6,4},{7,5},{8,10},{9,11},{10,... | collective-permute-start | bytes 589832 | tf_op jit(solution)/shard_map/ppermute | solution.py:221
  8.3 3.2 %collective-permute-start = (s32[32,128]{1,0:T(8,128)S(1)}, s32[32,128]{1,0:T(8,128)S(1)}, u32[]{:S(2)}, u32[]{:S(2)}) collective-permute-start(s32[32,128]{1,0:T(8,128)S(1)} %reshape.11.own_ref), channel_id=1, source_target_pairs={{0,1},{1,0},{2,3},{3,2},{4,5},{5,4},{6,7},{7,6},{8,9},{9,8},{10,11... | collective-permute-start | bytes 49160 | tf_op jit(solution)/shard_map/ppermute | solution.py:234
  8.4 13.7 %collective-permute-start.3 = (bf16[256,768]{1,0:T(8,128)(2,1)}, bf16[256,768]{1,0:T(8,128)(2,1)S(1)}, u32[]{:S(2)}, u32[]{:S(2)}) collective-permute-start(bf16[256,768]{1,0:T(8,128)(2,1)} %database_ref.1), channel_id=1, source_target_pairs={{0,1},{1,0},{2,3},{3,2},{4,5},{5,4},{6,7},{7,6},{8,9},{9,8},{10,11... | collective-permute-start | bytes 1179656 | tf_op jit(solution)/shard_map/ppermute | solution.py:234
  8.9 9.9 %collective-permute-start.5 = (bf16[64,768]{1,0:T(8,128)(2,1)S(1)}, bf16[64,768]{1,0:T(8,128)(2,1)S(1)}, u32[]{:S(2)}, u32[]{:S(2)}) collective-permute-start(bf16[64,768]{1,0:T(8,128)(2,1)S(1)} %get-tuple-element.21), channel_id=1, source_target_pairs={{0,4},{1,5},{2,6},{3,7},{4,0},{5,1},{6,2},{7,3},{8,12},{9,13},{10,... | collective-permute-start | bytes 294920 | tf_op jit(solution)/shard_map/ppermute | solution.py:221
  10.5 8.3 %collective-permute-start.4 = (bf16[64,768]{1,0:T(8,128)(2,1)S(1)}, bf16[64,768]{1,0:T(8,128)(2,1)S(1)}, u32[]{:S(2)}, u32[]{:S(2)}) collective-permute-start(bf16[64,768]{1,0:T(8,128)(2,1)S(1)} %collective-permute-done.2.far_ref.rest_1_), channel_id=1, source_target_pairs={{0,2},{1,3},{2,0},{3,1},{4,6},{5,7},{6,4},{7,5},{8,10},{9,11},{10,... | collective-permute-start | bytes 294920 | tf_op jit(solution)/shard_map/ppermute | solution.py:221
  15.5 1.0 %copy-start = (bf16[256,768]{1,0:T(8,128)(2,1)S(1)}, bf16[256,768]{1,0:T(8,128)(2,1)}, u32[]{:S(2)}) copy-start(bf16[256,768]{1,0:T(8,128)(2,1)} %database_ref.1) | copy-start | bytes 1179652
  18.8 7.8 %collective-permute-start.6 = (bf16[192,768]{1,0:T(8,128)(2,1)S(1)}, bf16[192,768]{1,0:T(8,128)(2,1)S(1)}, u32[]{:S(2)}, u32[]{:S(2)}) collective-permute-start(bf16[192,768]{1,0:T(8,128)(2,1)S(1)} %join.1.rest_0_), channel_id=1, source_target_pairs={{0,8},{1,17},{2,10},{3,19},{4,12},{5,21},{6,14},{7,23},{8,0},{9,25... | collective-permute-start | bytes 884744 | tf_op jit(solution)/shard_map/ppermute | solution.py:241
  20.6 7.2 %collective-permute-start.8 = (bf16[192,768]{1,0:T(8,128)(2,1)S(1)}, bf16[192,768]{1,0:T(8,128)(2,1)S(1)}, u32[]{:S(2)}, u32[]{:S(2)}) collective-permute-start(bf16[192,768]{1,0:T(8,128)(2,1)S(1)} %join.1.rest_0_), channel_id=1, source_target_pairs={{0,16},{1,9},{2,18},{3,11},{4,20},{5,13},{6,22},{7,15},{8,24},{9,1... | collective-permute-start | bytes 884744 | tf_op jit(solution)/shard_map/ppermute | solution.py:241
  22.1 5.7 %collective-permute-start.7 = (bf16[64,768]{1,0:T(8,128)(2,1)S(1)}, bf16[64,768]{1,0:T(8,128)(2,1)S(1)}, u32[]{:S(2)}, u32[]{:S(2)}) collective-permute-start(bf16[64,768]{1,0:T(8,128)(2,1)S(1)} %collective-permute-done.5.rest_3_.rest_1_), channel_id=1, source_target_pairs={{0,2},{1,3},{2,0},{3,1},{4,6},{5,7},{6,4},{7,5},{8,10},{9,11},{10,... | collective-permute-start | bytes 294920 | tf_op jit(solution)/shard_map/ppermute | solution.py:221
  28.8 2.4 %collective-permute-start.9 = (f32[256,768]{1,0:T(8,128)S(1)}, f32[256,768]{1,0:T(8,128)S(1)}, u32[]{:S(2)}, u32[]{:S(2)}) collective-permute-start(f32[256,768]{1,0:T(8,128)S(1)} %late_sums.3.twin_a_ref), channel_id=1, source_target_pairs={{0,1},{1,0},{2,3},{3,2},{4,5},{5,4},{6,7},{7,6},{8,9},{9,8},{10,11... | collective-permute-start | bytes 2359304 | tf_op jit(solution)/shard_map/ppermute | solution.py:234
  30.0 2.5 %collective-permute-start.10 = (f32[256,768]{1,0:T(8,128)S(1)}, f32[256,768]{1,0:T(8,128)S(1)}, u32[]{:S(2)}, u32[]{:S(2)}) collective-permute-start(f32[256,768]{1,0:T(8,128)S(1)} %late_sums.2.own_a_ref), channel_id=1, source_target_pairs={{0,1},{1,0},{2,3},{3,2},{4,5},{5,4},{6,7},{7,6},{8,9},{9,8},{10,11... | collective-permute-start | bytes 2359304 | tf_op jit(solution)/shard_map/ppermute | solution.py:234
  41.5 6.1 %collective-permute-start.11 = (f32[64,128]{1,0:T(8,128)S(1)}, f32[64,128]{1,0:T(8,128)S(1)}, u32[]{:S(2)}, u32[]{:S(2)}) collective-permute-start(f32[64,128]{1,0:T(8,128)S(1)} %get-tuple-element.19), channel_id=1, source_target_pairs={{0,6},{1,7},{2,4},{3,5},{4,2},{5,3},{6,0},{7,1},{8,14},{9,15},{10,... | collective-permute-start | bytes 98312 | tf_op jit(solution)/shard_map/ppermute | solution.py:221
  44.4 4.8 %collective-permute-start.12 = (f32[64,128]{1,0:T(8,128)S(1)}, f32[64,128]{1,0:T(8,128)S(1)}, u32[]{:S(2)}, u32[]{:S(2)}) collective-permute-start(f32[64,128]{1,0:T(8,128)S(1)} %get-tuple-element.19), channel_id=1, source_target_pairs={{0,4},{1,5},{2,6},{3,7},{4,0},{5,1},{6,2},{7,3},{8,12},{9,13},{10,... | collective-permute-start | bytes 98312 | tf_op jit(solution)/shard_map/ppermute | solution.py:221
  44.7 4.5 %collective-permute-start.13 = (f32[64,128]{1,0:T(8,128)S(1)}, f32[64,128]{1,0:T(8,128)S(1)}, u32[]{:S(2)}, u32[]{:S(2)}) collective-permute-start(f32[64,128]{1,0:T(8,128)S(1)} %get-tuple-element.19), channel_id=1, source_target_pairs={{0,2},{1,3},{2,0},{3,1},{4,6},{5,7},{6,4},{7,5},{8,10},{9,11},{10,... | collective-permute-start | bytes 98312 | tf_op jit(solution)/shard_map/ppermute | solution.py:221
  49.2 1.3 %collective-permute-start.14 = (f32[64,128]{1,0:T(8,128)S(1)}, f32[64,128]{1,0:T(8,128)S(1)}, u32[]{:S(2)}, u32[]{:S(2)}) collective-permute-start(f32[64,128]{1,0:T(8,128)S(1)} %maximum_maximum_fusion), channel_id=1, source_target_pairs={{0,1},{1,0},{2,3},{3,2},{4,5},{5,4},{6,7},{7,6},{8,9},{9,8},{10,11... | collective-permute-start | bytes 98312 | tf_op jit(solution)/shard_map/ppermute | solution.py:234
where the time goes:
time: 51.4 us; the launch traced here: 51.2 us
  Pallas kernels  16.8 us (33%)
  starting transfers between devices  16.1 us (31%)
  waiting for transfers between devices  13.9 us (27%)
  local copies, waits for them, and re-layouts  2.16 us (4%)
  other arithmetic  1.39 us (3%)
  between operations  0.81 us (2%)
    ppermute x8, starting transfers between devices, along(): return lax.ppermute(value, 'db', pairs)  11.5 us
    pallas_call x1, Pallas kernels, local(): pl.pallas_call(score_kernel, out_shape=[jax.ShapeDtypeStruct((rows, featu...  9.04 us
    ppermute x8, waiting for transfers between devices, along(): return lax.ppermute(value, 'db', pairs)  8.54 us
    pallas_call x3, Pallas kernels, sums(): pl.pallas_call(functools.partial(sums_kernel, len(blocks)), out_shape=out...  3.37 us
    ppermute x2, starting transfers between devices, cross(): return lax.ppermute(value, ('pb', 'db'), pairs)  3.29 us
    ppermute x5, waiting for transfers between devices, swap(): return lax.ppermute(value, 'db', [(i, i ^ 1) for i in range(owners)])  3.1 us
    pallas_call x1, Pallas kernels, local(): pl.pallas_call(functools.partial(count_kernel, planes), out_shape=[jax.Sh...  2.28 us
    ppermute x2, waiting for transfers between devices, cross(): return lax.ppermute(value, ('pb', 'db'), pairs)  2.24 us
  transfers between devices with their start and end apart: 15, of which 8 were waited for; matrix products, arithmetic and copies ran while one was open for 2% of the time, Pallas kernels for 13%

commit v1 on v0

--- a/solution.py
+++ b/solution.py
@@ -49,7 +49,7 @@
     copy.start()
     queries = fetch_queries(queries_ref, held_ref, 0, queries_sem)
     queries.start()
-    near_ref[...] = adjacent_ref[: near_ref.shape[0], :]
+    near_ref[...] = adjacent_ref[...]
     me, plane, core = position_of()
     bits = rows.bit_length() - 1
     lines = own_ref.shape[0]
@@ -62,9 +62,11 @@
         inner = row & (quarter - 1)
         away = (owner >> 1) ^ plane
         straight = (away - 1) * quarter + inner
-        start = jnp.where(cross == 3, starts[3], starts[3] + span)
-        start = jnp.where(cross == 1 + core, starts[2], start)
-        position = jnp.where(cross == 0, starts[1], start) + straight
+        half = away >> 1
+        relayed = jnp.where(away & 1 == 1, planes // 2 - 1 + half, half - 1) * quarter + inner
+        position = starts[3] + jnp.where(cross == 3, relayed, span + straight)
+        position = jnp.where(cross == 1 + core, starts[2] + straight, position)
+        position = jnp.where(cross == 0, starts[1] + straight, position)
         position = jnp.where(away == 0, row, position)
         position = jnp.where((wanted >= 0) & (side == core), position, -1)
         tiles_ref[number * lines : (number + 1) * lines, :] = position >> 7
@@ -104,10 +106,11 @@
 
 
 def join_kernel(pieces, *rest):
-    out_ref = rest[-1]
-    quarter = out_ref.shape[0] // pieces
-    for i in range(pieces):
-        out_ref[i * quarter : (i + 1) * quarter, :] = rest[i][...]
+    *pieces_refs, near_ref, across_ref = rest
+    quarter = near_ref.shape[0] // pieces
+    for i, ref in enumerate(pieces_refs):
+        out_ref, at = (near_ref, i) if i < pieces else (across_ref, i - pieces)
+        out_ref[at * quarter : (at + 1) * quarter, :] = ref[...]
 
 
 def spread_terms(dest, dest_inverse, block, far, counts):
@@ -220,15 +223,14 @@
         pairs = [(i, ((i // 2) ^ apart) * 2 + i % 2) for i in range(owners)]
         return lax.ppermute(value, "db", pairs)
 
-    def along_all(value, adjacent):
+    def along_all(value, smallest):
         pieces = {0: value}
         apart = planes // 2
-        while apart:
+        while apart >= smallest:
             for other in sorted(pieces):
-                joined = apart == 1 and other == 0
-                pieces[other ^ apart] = adjacent if joined else along(pieces[other], apart)
+                pieces[other ^ apart] = along(pieces[other], apart)
             apart //= 2
-        return [pieces[apart] for apart in range(1, planes)]
+        return [pieces[apart] for apart in sorted(pieces)]
 
     def swap(value):
         return lax.ppermute(value, "db", [(i, i ^ 1) for i in range(owners)])
@@ -242,9 +244,8 @@
 
     mine = lax.dynamic_slice_in_dim(database, me * quarter, quarter, 0)
     other = lax.dynamic_slice_in_dim(database, (me ^ 3) * quarter, quarter, 0)
-    adjacent = along(jnp.concatenate([mine, other], axis=0), 1)
-    near = along_all(mine, adjacent[:quarter])
-    across = along_all(other, adjacent[quarter:])
+    near = along_all(mine, 1)[1:]
+    across = along_all(other, 2)
     twin = swap(database)
     vmem = pl.BlockSpec(memory_space=pltpu.VMEM)
     slots = jnp.arange(fanout, dtype=jnp.int32)[None, :]
@@ -260,7 +261,7 @@
         ]
         + [
             jax.ShapeDtypeStruct((rows, features), jnp.bfloat16),
-            jax.ShapeDtypeStruct((count // 8, features), jnp.bfloat16),
+            jax.ShapeDtypeStruct((count // 4, features), jnp.bfloat16),
             jax.ShapeDtypeStruct((quarter, features), jnp.bfloat16),
         ],
         in_specs=[vmem, vmem] + [pl.BlockSpec(memory_space=pltpu.HBM)] * 2 + [vmem] * 2,
@@ -274,15 +275,19 @@
         compiler_params=pltpu.CompilerParams(vmem_limit_bytes=30 * MIB),
         cost_estimate=pl.CostEstimate(flops=1<<30, bytes_accessed=4 * rows * rows, transcendentals=0),
         name="counts",
-    )(twin_wanted, wanted, database, queries, adjacent, near[planes // 2 - 1])
-    near = pl.pallas_call(
+    )(twin_wanted, wanted, database, queries, near[0], near[planes // 2 - 1])
+    near, message = pl.pallas_call(
         functools.partial(join_kernel, planes - 1),
-        out_shape=jax.ShapeDtypeStruct((span, features), jnp.bfloat16),
-        in_specs=[vmem] * planes,
-        out_specs=vmem,
+        out_shape=[
+            jax.ShapeDtypeStruct((span, features), jnp.bfloat16),
+            jax.ShapeDtypeStruct((planes // 2 * quarter, features), jnp.bfloat16),
+        ],
+        in_specs=[vmem] * (planes - 1 + planes // 2),
+        out_specs=[vmem] * 2,
         compiler_params=pltpu.CompilerParams(vmem_limit_bytes=8 * MIB),
         name="join",
-    )(near_first, *near[1:], across[planes // 2 - 1])
+    )(near_first, *near[1:], *across)
+    across = across[1:] + [along(message, 1)]
     beside = cross(near, (1, 2))
     behind = cross(near, (2, 1))
 
@@ -333,8 +338,8 @@
         out_specs=[vmem, vmem],
         scratch_shapes=[
             pltpu.VMEM((2 * rows, features), jnp.bfloat16),
-            pltpu.VMEM((count // 8 * 3, features), jnp.bfloat16),
-            pltpu.SemaphoreType.DMA((3,)),
+            pltpu.VMEM((count // 4, features), jnp.bfloat16),
+            pltpu.SemaphoreType.DMA((2,)),
         ],
         compiler_params=pltpu.CompilerParams(vmem_limit_bytes=40 * MIB),
         cost_estimate=pl.CostEstimate(

time: 51.4 us -> 50.7 us (0.986)
  Pallas kernels: 16.8 us -> 16.1 us
    ppermute x8, waiting for transfers between devices: 8.54 us -> 6.62 us  [along(): return lax.ppermute(value, 'db', pairs)]
    ppermute x2, waiting for transfers between devices: 2.24 us -> 4.03 us  [cross(): return lax.ppermute(value, ('pb', 'db'), pairs)]
    pallas_call x1, Pallas kernels: 9.04 us -> 7.64 us  [local(): pl.pallas_call(score_kernel, out_shape=[jax.ShapeDtypeStruct((rows, featu...]
    pallas_call x1, Pallas kernels: 2.28 us -> 3 us  [local(): pl.pallas_call(functools.partial(count_kernel, planes), out_shape=[jax.Sh...]
  transfers between devices with their start and end apart: 15 -> 15, of which waited for: 8 -> 9; matrix products, arithmetic and copies ran while one was open for 2% -> 2% of each run, Pallas kernels for 13% -> 15%
where the time goes in v1:
time: 50.7 us; the launch traced here: 50.5 us
  starting transfers between devices  16.3 us (32%)
  Pallas kernels  16.1 us (32%)
  waiting for transfers between devices  13.8 us (27%)
  local copies, waits for them, and re-layouts  2.16 us (4%)
  other arithmetic  1.38 us (3%)
  between operations  0.78 us (2%)
    ppermute x8, starting transfers between devices, along(): return lax.ppermute(value, 'db', pairs)  11.6 us
    pallas_call x1, Pallas kernels, local(): pl.pallas_call(score_kernel, out_shape=[jax.ShapeDtypeStruct((rows, featu...  7.64 us
    ppermute x8, waiting for transfers between devices, along(): return lax.ppermute(value, 'db', pairs)  6.62 us
    ppermute x2, waiting for transfers between devices, cross(): return lax.ppermute(value, ('pb', 'db'), pairs)  4.03 us
    pallas_call x3, Pallas kernels, sums(): pl.pallas_call(functools.partial(sums_kernel, len(blocks)), out_shape=out...  3.36 us
    ppermute x2, starting transfers between devices, cross(): return lax.ppermute(value, ('pb', 'db'), pairs)  3.33 us
    ppermute x5, waiting for transfers between devices, swap(): return lax.ppermute(value, 'db', [(i, i ^ 1) for i in range(owners)])  3.1 us
    pallas_call x1, Pallas kernels, local(): pl.pallas_call(functools.partial(count_kernel, planes), out_shape=[jax.Sh...  3 us
  transfers between devices with their start and end apart: 15, of which 9 were waited for; matrix products, arithmetic and copies ran while one was open for 2% of the time, Pallas kernels for 15%

profile of v1, /device:TPU:0, one launch (start us, length us, event | category | flops | bytes accessed | tf_op | source)
XLA Modules:
  0.0 50.5 jit_solution(9227024744156976577)
XLA Ops:
  0.6 1.0 %constant_dynamic-slice_fusion = (bf16[64,768]{1,0:T(8,128)(2,1)S(1)}, bf16[64,768]{1,0:T(8,128)(2,1)S(1)}) fusion(bf16[256,768]{1,0:T(8,128)(2,1)} %database_ref.1, s32[]{:T(128)S(6)} %select_n.31, s32[]{:T(128)S(6)} %select_n.30), kind=kLoop, calls=%fused_computation.6 | loop fusion | bytes 393224 | tf_op jit(solution)/shard_map/dynamic_slice | solution.py:246
  1.6 4.1 %collective-permute-start.2 = (bf16[64,768]{1,0:T(8,128)(2,1)S(1)}, bf16[64,768]{1,0:T(8,128)(2,1)S(1)}, u32[]{:S(2)}, u32[]{:S(2)}) collective-permute-start(bf16[64,768]{1,0:T(8,128)(2,1)S(1)} %get-tuple-element.25), channel_id=1, source_target_pairs={{0,4},{1,5},{2,6},{3,7},{4,0},{5,1},{6,2},{7,3},{8,12},{9,13},{10,... | collective-permute-start | bytes 294920 | tf_op jit(solution)/shard_map/ppermute | solution.py:224
  5.7 1.6 %collective-permute-start.1 = (bf16[64,768]{1,0:T(8,128)(2,1)S(1)}, bf16[64,768]{1,0:T(8,128)(2,1)S(1)}, u32[]{:S(2)}, u32[]{:S(2)}) collective-permute-start(bf16[64,768]{1,0:T(8,128)(2,1)S(1)} %get-tuple-element.25), channel_id=1, source_target_pairs={{0,2},{1,3},{2,0},{3,1},{4,6},{5,7},{6,4},{7,5},{8,10},{9,11},{10,... | collective-permute-start | bytes 294920 | tf_op jit(solution)/shard_map/ppermute | solution.py:224
  7.3 0.7 %fusion = s32[256,16]{0,1:T(8,128)S(1)} fusion(s32[256,16]{0,1:T(8,128)} %param.5, s32[256]{0:T(256)} %param.6), kind=kLoop, calls=%fused_computation.3 | loop fusion | flops 8192 | bytes 33792 | tf_op jit(solution)/shard_map/jit(_where)/select_n | solution.py:252
  8.0 0.1 copy.7
  8.1 0.1 reshape.11.own_ref
  8.3 0.5 collective-permute-start.3
  8.8 0.3 collective-permute-start.5
  9.1 1.4 %collective-permute-done.2.far_ref.rest_1_ = bf16[64,768]{1,0:T(8,128)(2,1)S(1)} collective-permute-done((bf16[64,768]{1,0:T(8,128)(2,1)S(1)}, bf16[64,768]{1,0:T(8,128)(2,1)S(1)}, u32[]{:S(2)}, u32[]{:S(2)}) %collective-permute-start.2) | collective-permute-done | bytes 98336 | tf_op jit(solution)/shard_map/ppermute | solution.py:224
  10.5 1.2 %collective-permute-start.4 = (bf16[64,768]{1,0:T(8,128)(2,1)S(1)}, bf16[64,768]{1,0:T(8,128)(2,1)S(1)}, u32[]{:S(2)}, u32[]{:S(2)}) collective-permute-start(bf16[64,768]{1,0:T(8,128)(2,1)S(1)} %collective-permute-done.2.far_ref.rest_1_), channel_id=1, source_target_pairs={{0,2},{1,3},{2,0},{3,1},{4,6},{5,7},{6,4},{7,5},{8,10},{9,11},{10,... | collective-permute-start | bytes 294920 | tf_op jit(solution)/shard_map/ppermute | solution.py:224
  11.7 1.0 %copy-done = bf16[256,768]{1,0:T(8,128)(2,1)S(1)} copy-done((bf16[256,768]{1,0:T(8,128)(2,1)S(1)}, bf16[256,768]{1,0:T(8,128)(2,1)}, u32[]{:S(2)}) %copy-start) | copy-done | bytes 393240
  12.7 3.0 %counts.1 = (bf16[512,256]{1,0:T(8,128)(2,1)S(1)}, bf16[512,256]{1,0:T(8,128)(2,1)S(1)}, bf16[512,256]{1,0:T(8,128)(2,1)S(1)}, bf16[512,384]{1,0:T(8,128)(2,1)S(...) custom-call(s32[32,128]{1,0:T(8,128)S(1)} %collective-permute-done.twin_ref, ...), custom_call_target="tpu_custom_call" | custom-call | flops 1073741824 | bytes 262144 | tf_op jit(solution)/shard_map/counts/pallas_call | solution.py:257
  15.7 0.9 %collective-permute-done.5.rest_4_.rest_0_ = bf16[64,768]{1,0:T(8,128)(2,1)S(1)} collective-permute-done((bf16[64,768]{1,0:T(8,128)(2,1)S(1)}, bf16[64,768]{1,0:T(8,128)(2,1)S(1)}, u32[]{:S(2)}, u32[]{:S(2)}) %collective-permute-start.5) | collective-permute-done | bytes 98336 | tf_op jit(solution)/shard_map/ppermute | solution.py:224
  16.6 0.6 %collective-permute-done.4.rest_2_ = bf16[64,768]{1,0:T(8,128)(2,1)S(1)} collective-permute-done((bf16[64,768]{1,0:T(8,128)(2,1)S(1)}, bf16[64,768]{1,0:T(8,128)(2,1)S(1)}, u32[]{:S(2)}, u32[]{:S(2)}) %collective-permute-start.4) | collective-permute-done | bytes 98336 | tf_op jit(solution)/shard_map/ppermute | solution.py:224
  17.2 1.8 %collective-permute-start.6 = (bf16[192,768]{1,0:T(8,128)(2,1)S(1)}, bf16[192,768]{1,0:T(8,128)(2,1)S(1)}, u32[]{:S(2)}, u32[]{:S(2)}) collective-permute-start(bf16[192,768]{1,0:T(8,128)(2,1)S(1)} %get-tuple-element.16.rest_0_), channel_id=1, source_target_pairs={{0,8},{1,17},{2,10},{3,19},{4,12},{5,21},{6,14},{7,23},{8,0},{9,25... | collective-permute-start | bytes 884744 | tf_op jit(solution)/shard_map/ppermute | solution.py:243
  19.0 1.5 %collective-permute-start.8 = (bf16[192,768]{1,0:T(8,128)(2,1)S(1)}, bf16[192,768]{1,0:T(8,128)(2,1)S(1)}, u32[]{:S(2)}, u32[]{:S(2)}) collective-permute-start(bf16[192,768]{1,0:T(8,128)(2,1)S(1)} %get-tuple-element.16.rest_0_), channel_id=1, source_target_pairs={{0,16},{1,9},{2,18},{3,11},{4,20},{5,13},{6,22},{7,15},{8,24},{9,1... | collective-permute-start | bytes 884744 | tf_op jit(solution)/shard_map/ppermute | solution.py:243
  20.5 1.1 %own_sums.1.rest_1_ = f32[512,768]{1,0:T(8,128)S(1)} custom-call(bf16[256,768]{1,0:T(8,128)(2,1)S(1)} %collective-permute-done.3.twin_ref.dest_ref, bf16[256,768]{1,0:T(8,128)(2,1)S(1)} %get-tuple-element.13.own_ref.rest_0_.dest_ref, bf16[512,256]{1,0:T(8,128)(2,1)S(1)} %get-tuple-element.18.counts_ref, ...), custom_call_target="tpu_custom_call" | custom-call | flops 67108864 | bytes 262144 | tf_op jit(solution)/shard_map/own_sums/pallas_call | solution.py:301
  21.6 1.1 %near_sums.1.rest_1_ = f32[512,768]{1,0:T(8,128)S(1)} custom-call(bf16[256,768]{1,0:T(8,128)(2,1)S(1)} %collective-permute-done.3.twin_ref.dest_ref, bf16[256,768]{1,0:T(8,128)(2,1)S(1)} %get-tuple-element.13.own_ref.rest_0_.dest_ref, bf16[512,256]{1,0:T(8,128)(2,1)S(1)} %get-tuple-element.17.counts_ref, bf16[192,768]{1,0:T(8,128)(2,1)S(1)} %get-tuple-element.16.rest_0_, ...), custom_call_target="tpu_custom_call" | custom-call | flops 67108864 | bytes 262144 | tf_op jit(solution)/shard_map/near_sums/pallas_call | solution.py:301
  22.8 4.0 %collective-permute-done.6.rest_0_ = bf16[192,768]{1,0:T(8,128)(2,1)S(1)} collective-permute-done((bf16[192,768]{1,0:T(8,128)(2,1)S(1)}, bf16[192,768]{1,0:T(8,128)(2,1)S(1)}, u32[]{:S(2)}, u32[]{:S(2)}) %collective-permute-start.6) | collective-permute-done | bytes 294944 | tf_op jit(solution)/shard_map/ppermute | solution.py:243
  26.8 1.1 %beside_sums.1.early_ref = f32[512,768]{1,0:T(8,128)S(1)} custom-call(bf16[256,768]{1,0:T(8,128)(2,1)S(1)} %collective-permute-done.3.twin_ref.dest_ref, bf16[256,768]{1,0:T(8,128)(2,1)S(1)} %get-tuple-element.13.own_ref.rest_0_.dest_ref, bf16[512,256]{1,0:T(8,128)(2,1)S(1)} %get-tuple-element.14.counts_ref, ...), custom_call_target="tpu_custom_call" | custom-call | flops 67108864 | bytes 262144 | tf_op jit(solution)/shard_map/beside_sums/pallas_call | solution.py:301
  27.9 1.1 %late_sums.3.twin_a_ref = f32[256,768]{1,0:T(8,128)S(1)} custom-call(bf16[256,768]{1,0:T(8,128)(2,1)S(1)} %collective-permute-done.3.twin_ref.dest_ref, f32[512,768]{1,0:T(8,128)S(1)} %beside_sums.1.early_ref, bf16[512,384]{1,0:T(8,128)(2,1)S(1)} %get-tuple-element.19.counts_ref, bf16[64,768]{1,0:T(8,128)(2,1)S(1)} %collective-permute-done.5.rest_4_.rest_0_, ...), custom_call_target="tpu_custom_call" | custom-call | tf_op jit(solution)/shard_map/late_sums/pallas_call | solution.py:316
  29.1 1.1 %late_sums.2.own_a_ref = f32[256,768]{1,0:T(8,128)S(1)} custom-call(bf16[256,768]{1,0:T(8,128)(2,1)S(1)} %get-tuple-element.13.own_ref.rest_0_.dest_ref, f32[512,768]{1,0:T(8,128)S(1)} %beside_sums.1.early_ref, bf16[512,384]{1,0:T(8,128)(2,1)S(1)} %get-tuple-element.19.counts_ref, bf16[64,768]{1,0:T(8,128)(2,1)S(1)} %collective-permute-done.5.rest_4_.rest_0_, ...), custom_call_target="tpu_custom_call" | custom-call | tf_op jit(solution)/shard_map/late_sums/pallas_call | solution.py:316
  30.1 0.6 %collective-permute-start.10 = (f32[256,768]{1,0:T(8,128)S(1)}, f32[256,768]{1,0:T(8,128)S(1)}, u32[]{:S(2)}, u32[]{:S(2)}) collective-permute-start(f32[256,768]{1,0:T(8,128)S(1)} %late_sums.2.own_a_ref), channel_id=1, source_target_pairs={{0,1},{1,0},{2,3},{3,2},{4,5},{5,4},{6,7},{7,6},{8,9},{9,8},{10,11... | collective-permute-start | bytes 2359304 | tf_op jit(solution)/shard_map/ppermute | solution.py:236
  30.7 0.6 %collective-permute-done.9.own_b_ref = f32[256,768]{1,0:T(8,128)S(1)} collective-permute-done((f32[256,768]{1,0:T(8,128)S(1)}, f32[256,768]{1,0:T(8,128)S(1)}, u32[]{:S(2)}, u32[]{:S(2)}) %collective-permute-start.9) | collective-permute-done | bytes 786464 | tf_op jit(solution)/shard_map/ppermute | solution.py:236
  31.4 1.3 %collective-permute-done.10.twin_b_ref = f32[256,768]{1,0:T(8,128)S(1)} collective-permute-done((f32[256,768]{1,0:T(8,128)S(1)}, f32[256,768]{1,0:T(8,128)S(1)}, u32[]{:S(2)}, u32[]{:S(2)}) %collective-permute-start.10) | collective-permute-done | bytes 786464 | tf_op jit(solution)/shard_map/ppermute | solution.py:236
  32.6 7.6 %scores.1 = (bf16[256,768]{1,0:T(8,128)(2,1)}, f32[64,128]{1,0:T(8,128)S(1)}) custom-call(f32[256,768]{1,0:T(8,128)S(1)} %late_sums.2.own_a_ref, f32[256,768]{1,0:T(8,128)S(1)} %collective-permute-done.9.own_b_ref, f32[256,768]{1,0:T(8,128)S(1)} %late_sums.3.twin_a_ref, f32[256,768]{1,0:T(8,128)S(1)} %collective-permute-done.10.twin_b_ref, ...), custom_call_target="tpu_custom_call" | custom-call | flops 6442450944 | bytes 12582912 | tf_op jit(solution)/shard_map/scores/pallas_call | solution.py:331
  40.3 3.4 %collective-permute-start.11 = (f32[64,128]{1,0:T(8,128)S(1)}, f32[64,128]{1,0:T(8,128)S(1)}, u32[]{:S(2)}, u32[]{:S(2)}) collective-permute-start(f32[64,128]{1,0:T(8,128)S(1)} %get-tuple-element.23), channel_id=1, source_target_pairs={{0,6},{1,7},{2,4},{3,5},{4,2},{5,3},{6,0},{7,1},{8,14},{9,15},{10,... | collective-permute-start | bytes 98312 | tf_op jit(solution)/shard_map/ppermute | solution.py:224
  43.7 1.0 %collective-permute-start.13 = (f32[64,128]{1,0:T(8,128)S(1)}, f32[64,128]{1,0:T(8,128)S(1)}, u32[]{:S(2)}, u32[]{:S(2)}) collective-permute-start(f32[64,128]{1,0:T(8,128)S(1)} %get-tuple-element.23), channel_id=1, source_target_pairs={{0,2},{1,3},{2,0},{3,1},{4,6},{5,7},{6,4},{7,5},{8,10},{9,11},{10,... | collective-permute-start | bytes 98312 | tf_op jit(solution)/shard_map/ppermute | solution.py:224
  44.7 1.3 %collective-permute-done.11 = f32[64,128]{1,0:T(8,128)S(1)} collective-permute-done((f32[64,128]{1,0:T(8,128)S(1)}, f32[64,128]{1,0:T(8,128)S(1)}, u32[]{:S(2)}, u32[]{:S(2)}) %collective-permute-start.11) | collective-permute-done | bytes 32800 | tf_op jit(solution)/shard_map/ppermute | solution.py:224
  46.1 2.5 %collective-permute-done.12 = f32[64,128]{1,0:T(8,128)S(1)} collective-permute-done((f32[64,128]{1,0:T(8,128)S(1)}, f32[64,128]{1,0:T(8,128)S(1)}, u32[]{:S(2)}, u32[]{:S(2)}) %collective-permute-start.12) | collective-permute-done | bytes 32800 | tf_op jit(solution)/shard_map/ppermute | solution.py:224
  48.6 1.2 %collective-permute-done.14 = f32[64,128]{1,0:T(8,128)S(1)} collective-permute-done((f32[64,128]{1,0:T(8,128)S(1)}, f32[64,128]{1,0:T(8,128)S(1)}, u32[]{:S(2)}, u32[]{:S(2)}) %collective-permute-start.14) | collective-permute-done | bytes 32800 | tf_op jit(solution)/shard_map/ppermute | solution.py:236
  49.8 0.6 %maximum_bitcast_fusion = f32[16384]{0:T(1024)} fusion(f32[64,128]{1,0:T(8,128)S(1)} %get-tuple-element.27, f32[64,128]{1,0:T(8,128)S(1)} %get-tuple-element.26), kind=kLoop, calls=%fused_computation | loop fusion | flops 16384 | bytes 131072 | tf_op jit(solution)/shard_map/reshape | solution.py:357
  (15 shorter events, 0.3 us)
Async XLA Ops:
  1.6 8.9 %collective-permute-start.2 = (bf16[64,768]{1,0:T(8,128)(2,1)S(1)}, bf16[64,768]{1,0:T(8,128)(2,1)S(1)}, u32[]{:S(2)}, u32[]{:S(2)}) collective-permute-start(bf16[64,768]{1,0:T(8,128)(2,1)S(1)} %get-tuple-element.25), channel_id=1, source_target_pairs={{0,4},{1,5},{2,6},{3,7},{4,0},{5,1},{6,2},{7,3},{8,12},{9,13},{10,... | collective-permute-start | bytes 294920 | tf_op jit(solution)/shard_map/ppermute | solution.py:224
  5.7 6.0 %collective-permute-start.1 = (bf16[64,768]{1,0:T(8,128)(2,1)S(1)}, bf16[64,768]{1,0:T(8,128)(2,1)S(1)}, u32[]{:S(2)}, u32[]{:S(2)}) collective-permute-start(bf16[64,768]{1,0:T(8,128)(2,1)S(1)} %get-tuple-element.25), channel_id=1, source_target_pairs={{0,2},{1,3},{2,0},{3,1},{4,6},{5,7},{6,4},{7,5},{8,10},{9,11},{10,... | collective-permute-start | bytes 294920 | tf_op jit(solution)/shard_map/ppermute | solution.py:224
  8.2 3.5 %collective-permute-start = (s32[32,128]{1,0:T(8,128)S(1)}, s32[32,128]{1,0:T(8,128)S(1)}, u32[]{:S(2)}, u32[]{:S(2)}) collective-permute-start(s32[32,128]{1,0:T(8,128)S(1)} %reshape.11.own_ref), channel_id=1, source_target_pairs={{0,1},{1,0},{2,3},{3,2},{4,5},{5,4},{6,7},{7,6},{8,9},{9,8},{10,11... | collective-permute-start | bytes 49160 | tf_op jit(solution)/shard_map/ppermute | solution.py:236
  8.3 12.2 %collective-permute-start.3 = (bf16[256,768]{1,0:T(8,128)(2,1)}, bf16[256,768]{1,0:T(8,128)(2,1)S(1)}, u32[]{:S(2)}, u32[]{:S(2)}) collective-permute-start(bf16[256,768]{1,0:T(8,128)(2,1)} %database_ref.1), channel_id=1, source_target_pairs={{0,1},{1,0},{2,3},{3,2},{4,5},{5,4},{6,7},{7,6},{8,9},{9,8},{10,11... | collective-permute-start | bytes 1179656 | tf_op jit(solution)/shard_map/ppermute | solution.py:236
  8.8 7.8 %collective-permute-start.5 = (bf16[64,768]{1,0:T(8,128)(2,1)S(1)}, bf16[64,768]{1,0:T(8,128)(2,1)S(1)}, u32[]{:S(2)}, u32[]{:S(2)}) collective-permute-start(bf16[64,768]{1,0:T(8,128)(2,1)S(1)} %get-tuple-element.24.rest_3_), channel_id=1, source_target_pairs={{0,4},{1,5},{2,6},{3,7},{4,0},{5,1},{6,2},{7,3},{8,12},{9,13},{10,... | collective-permute-start | bytes 294920 | tf_op jit(solution)/shard_map/ppermute | solution.py:224
  10.5 6.6 %collective-permute-start.4 = (bf16[64,768]{1,0:T(8,128)(2,1)S(1)}, bf16[64,768]{1,0:T(8,128)(2,1)S(1)}, u32[]{:S(2)}, u32[]{:S(2)}) collective-permute-start(bf16[64,768]{1,0:T(8,128)(2,1)S(1)} %collective-permute-done.2.far_ref.rest_1_), channel_id=1, source_target_pairs={{0,2},{1,3},{2,0},{3,1},{4,6},{5,7},{6,4},{7,5},{8,10},{9,11},{10,... | collective-permute-start | bytes 294920 | tf_op jit(solution)/shard_map/ppermute | solution.py:224
  11.7 1.0 %copy-start = (bf16[256,768]{1,0:T(8,128)(2,1)S(1)}, bf16[256,768]{1,0:T(8,128)(2,1)}, u32[]{:S(2)}) copy-start(bf16[256,768]{1,0:T(8,128)(2,1)} %database_ref.1) | copy-start | bytes 1179652
  17.2 9.6 %collective-permute-start.6 = (bf16[192,768]{1,0:T(8,128)(2,1)S(1)}, bf16[192,768]{1,0:T(8,128)(2,1)S(1)}, u32[]{:S(2)}, u32[]{:S(2)}) collective-permute-start(bf16[192,768]{1,0:T(8,128)(2,1)S(1)} %get-tuple-element.16.rest_0_), channel_id=1, source_target_pairs={{0,8},{1,17},{2,10},{3,19},{4,12},{5,21},{6,14},{7,23},{8,0},{9,25... | collective-permute-start | bytes 884744 | tf_op jit(solution)/shard_map/ppermute | solution.py:243
  19.0 9.0 %collective-permute-start.8 = (bf16[192,768]{1,0:T(8,128)(2,1)S(1)}, bf16[192,768]{1,0:T(8,128)(2,1)S(1)}, u32[]{:S(2)}, u32[]{:S(2)}) collective-permute-start(bf16[192,768]{1,0:T(8,128)(2,1)S(1)} %get-tuple-element.16.rest_0_), channel_id=1, source_target_pairs={{0,16},{1,9},{2,18},{3,11},{4,20},{5,13},{6,22},{7,15},{8,24},{9,1... | collective-permute-start | bytes 884744 | tf_op jit(solution)/shard_map/ppermute | solution.py:243
  20.5 7.4 %collective-permute-start.7 = (bf16[128,768]{1,0:T(8,128)(2,1)S(1)}, bf16[128,768]{1,0:T(8,128)(2,1)S(1)}, u32[]{:S(2)}, u32[]{:S(2)}) collective-permute-start(bf16[128,768]{1,0:T(8,128)(2,1)S(1)} %get-tuple-element.20), channel_id=1, source_target_pairs={{0,2},{1,3},{2,0},{3,1},{4,6},{5,7},{6,4},{7,5},{8,10},{9,11},{10,... | collective-permute-start | bytes 589832 | tf_op jit(solution)/shard_map/ppermute | solution.py:224
  29.0 2.4 %collective-permute-start.9 = (f32[256,768]{1,0:T(8,128)S(1)}, f32[256,768]{1,0:T(8,128)S(1)}, u32[]{:S(2)}, u32[]{:S(2)}) collective-permute-start(f32[256,768]{1,0:T(8,128)S(1)} %late_sums.3.twin_a_ref), channel_id=1, source_target_pairs={{0,1},{1,0},{2,3},{3,2},{4,5},{5,4},{6,7},{7,6},{8,9},{9,8},{10,11... | collective-permute-start | bytes 2359304 | tf_op jit(solution)/shard_map/ppermute | solution.py:236
  30.1 2.5 %collective-permute-start.10 = (f32[256,768]{1,0:T(8,128)S(1)}, f32[256,768]{1,0:T(8,128)S(1)}, u32[]{:S(2)}, u32[]{:S(2)}) collective-permute-start(f32[256,768]{1,0:T(8,128)S(1)} %late_sums.2.own_a_ref), channel_id=1, source_target_pairs={{0,1},{1,0},{2,3},{3,2},{4,5},{5,4},{6,7},{7,6},{8,9},{9,8},{10,11... | collective-permute-start | bytes 2359304 | tf_op jit(solution)/shard_map/ppermute | solution.py:236
  40.3 5.8 %collective-permute-start.11 = (f32[64,128]{1,0:T(8,128)S(1)}, f32[64,128]{1,0:T(8,128)S(1)}, u32[]{:S(2)}, u32[]{:S(2)}) collective-permute-start(f32[64,128]{1,0:T(8,128)S(1)} %get-tuple-element.23), channel_id=1, source_target_pairs={{0,6},{1,7},{2,4},{3,5},{4,2},{5,3},{6,0},{7,1},{8,14},{9,15},{10,... | collective-permute-start | bytes 98312 | tf_op jit(solution)/shard_map/ppermute | solution.py:224
  43.7 4.8 %collective-permute-start.12 = (f32[64,128]{1,0:T(8,128)S(1)}, f32[64,128]{1,0:T(8,128)S(1)}, u32[]{:S(2)}, u32[]{:S(2)}) collective-permute-start(f32[64,128]{1,0:T(8,128)S(1)} %get-tuple-element.23), channel_id=1, source_target_pairs={{0,4},{1,5},{2,6},{3,7},{4,0},{5,1},{6,2},{7,3},{8,12},{9,13},{10,... | collective-permute-start | bytes 98312 | tf_op jit(solution)/shard_map/ppermute | solution.py:224
  43.7 4.8 %collective-permute-start.13 = (f32[64,128]{1,0:T(8,128)S(1)}, f32[64,128]{1,0:T(8,128)S(1)}, u32[]{:S(2)}, u32[]{:S(2)}) collective-permute-start(f32[64,128]{1,0:T(8,128)S(1)} %get-tuple-element.23), channel_id=1, source_target_pairs={{0,2},{1,3},{2,0},{3,1},{4,6},{5,7},{6,4},{7,5},{8,10},{9,11},{10,... | collective-permute-start | bytes 98312 | tf_op jit(solution)/shard_map/ppermute | solution.py:224
  48.5 1.3 %collective-permute-start.14 = (f32[64,128]{1,0:T(8,128)S(1)}, f32[64,128]{1,0:T(8,128)S(1)}, u32[]{:S(2)}, u32[]{:S(2)}) collective-permute-start(f32[64,128]{1,0:T(8,128)S(1)} %maximum_maximum_fusion), channel_id=1, source_target_pairs={{0,1},{1,0},{2,3},{3,2},{4,5},{5,4},{6,7},{7,6},{8,9},{9,8},{10,11... | collective-permute-start | bytes 98312 | tf_op jit(solution)/shard_map/ppermute | solution.py:236

commit v2 on v1

--- a/solution.py
+++ b/solution.py
@@ -64,8 +64,12 @@
         straight = (away - 1) * quarter + inner
         half = away >> 1
         relayed = jnp.where(away & 1 == 1, planes // 2 - 1 + half, half - 1) * quarter + inner
-        position = starts[3] + jnp.where(cross == 3, relayed, span + straight)
-        position = jnp.where(cross == 1 + core, starts[2] + straight, position)
+        second = jnp.where(cross == 1 + core, 0, 1)
+        first = span - quarter
+        early = starts[1] + span + second * first + straight
+        late = starts[2] + span + second * quarter + straight - first
+        position = jnp.where(straight < first, early, late)
+        position = jnp.where(cross == 3, starts[2] + relayed, position)
         position = jnp.where(cross == 0, starts[1] + straight, position)
         position = jnp.where(away == 0, row, position)
         position = jnp.where((wanted >= 0) & (side == core), position, -1)
@@ -105,12 +109,12 @@
     queries.wait()
 
 
-def join_kernel(pieces, *rest):
-    *pieces_refs, near_ref, across_ref = rest
-    quarter = near_ref.shape[0] // pieces
-    for i, ref in enumerate(pieces_refs):
-        out_ref, at = (near_ref, i) if i < pieces else (across_ref, i - pieces)
-        out_ref[at * quarter : (at + 1) * quarter, :] = ref[...]
+def join_kernel(last_ref, *rest):
+    *pieces, _, forward_ref, across_ref = rest
+    quarter = last_ref.shape[0]
+    forward_ref[...] = last_ref[...]
+    for i, ref in enumerate(pieces):
+        across_ref[i * quarter : (i + 1) * quarter, :] = ref[...]
 
 
 def spread_terms(dest, dest_inverse, block, far, counts):
@@ -246,6 +250,9 @@
     other = lax.dynamic_slice_in_dim(database, (me ^ 3) * quarter, quarter, 0)
     near = along_all(mine, 1)[1:]
     across = along_all(other, 2)
+    ahead = jnp.concatenate(near[:-1], axis=0)
+    beside = cross(ahead, (1, 2))
+    behind = cross(ahead, (2, 1))
     twin = swap(database)
     vmem = pl.BlockSpec(memory_space=pltpu.VMEM)
     slots = jnp.arange(fanout, dtype=jnp.int32)[None, :]
@@ -253,7 +260,7 @@
     twin_wanted = swap(wanted)
     padded = lambda size: (size + 127) // 128 * 128
     span = (planes - 1) * quarter
-    widths = (rows, span, span, 2 * span)
+    widths = (rows, 3 * span - 2 * quarter, span + 2 * quarter)
     *counts, own, first_queries, near_first = pl.pallas_call(
         functools.partial(count_kernel, planes),
         out_shape=[
@@ -265,7 +272,7 @@
             jax.ShapeDtypeStruct((quarter, features), jnp.bfloat16),
         ],
         in_specs=[vmem, vmem] + [pl.BlockSpec(memory_space=pltpu.HBM)] * 2 + [vmem] * 2,
-        out_specs=[vmem] * 7,
+        out_specs=[vmem] * 6,
         scratch_shapes=[
             pltpu.VMEM((2 * wanted.shape[0], 128), jnp.int32),
             pltpu.VMEM((2 * wanted.shape[0], 128), jnp.int32),
@@ -273,23 +280,23 @@
             pltpu.SemaphoreType.DMA(()),
         ],
         compiler_params=pltpu.CompilerParams(vmem_limit_bytes=30 * MIB),
-        cost_estimate=pl.CostEstimate(flops=1<<30, bytes_accessed=4 * rows * rows, transcendentals=0),
+        cost_estimate=pl.CostEstimate(flops=1<<26, bytes_accessed=4 * rows * rows, transcendentals=0),
         name="counts",
     )(twin_wanted, wanted, database, queries, near[0], near[planes // 2 - 1])
-    near, message = pl.pallas_call(
-        functools.partial(join_kernel, planes - 1),
+    forward, message = pl.pallas_call(
+        join_kernel,
         out_shape=[
-            jax.ShapeDtypeStruct((span, features), jnp.bfloat16),
+            jax.ShapeDtypeStruct((quarter, features), jnp.bfloat16),
             jax.ShapeDtypeStruct((planes // 2 * quarter, features), jnp.bfloat16),
         ],
-        in_specs=[vmem] * (planes - 1 + planes // 2),
+        in_specs=[vmem] * (2 + planes // 2),
         out_specs=[vmem] * 2,
         compiler_params=pltpu.CompilerParams(vmem_limit_bytes=8 * MIB),
         name="join",
-    )(near_first, *near[1:], *across)
+    )(near[-1], *across, near_first)
     across = across[1:] + [along(message, 1)]
-    beside = cross(near, (1, 2))
-    behind = cross(near, (2, 1))
+    beside_last = cross(forward, (1, 2))
+    behind_last = cross(forward, (2, 1))
 
     def sums(name, counts, blocks, before=None):
         out = [jax.ShapeDtypeStruct((2 * rows, features), jnp.float32)]
@@ -309,18 +316,17 @@
         )(*operands)
 
     (total,) = sums("own_sums", counts[0], [own])
-    (total,) = sums("near_sums", counts[1], [near], total)
-    (total,) = sums("beside_sums", counts[2], [beside], total)
+    (total,) = sums("near_sums", counts[1], [*near, beside, behind], total)
 
     def late(number, dest):
         return pl.pallas_call(
             functools.partial(late_kernel, number),
             out_shape=jax.ShapeDtypeStruct((rows, features), jnp.float32),
-            in_specs=[vmem] * (4 + len(across)),
+            in_specs=[vmem] * (5 + len(across)),
             out_specs=vmem,
             compiler_params=pltpu.CompilerParams(vmem_limit_bytes=30 * MIB),
             name="late_sums",
-        )(dest, total, counts[3], *across, behind)
+        )(dest, total, counts[2], *across, beside_last, behind_last)
 
     twin_a = late(0, twin)
     own_b = swap(twin_a)

time: 50.7 us -> 48.7 us (0.961)
  waiting for transfers between devices: 13.8 us -> 9.79 us
  starting transfers between devices: 16.3 us -> 18.5 us
    ppermute x2 -> x4, waiting for transfers between devices: 4.03 us -> 1.14 us  [cross(): return lax.ppermute(value, ('pb', 'db'), pairs)]
    ppermute x8, starting transfers between devices: 11.6 us -> 13.1 us  [along(): return lax.ppermute(value, 'db', pairs)]
    ppermute x8, waiting for transfers between devices: 6.62 us -> 5.55 us  [along(): return lax.ppermute(value, 'db', pairs)]
    ppermute x2 -> x4, starting transfers between devices: 3.33 us -> 4.12 us  [cross(): return lax.ppermute(value, ('pb', 'db'), pairs)]
    pallas_call x3 -> x2, Pallas kernels: 3.36 us -> 2.92 us  [sums(): pl.pallas_call(functools.partial(sums_kernel, len(blocks)), out_shape=out...]
  transfers between devices with their start and end apart: 15 -> 17, of which waited for: 9 -> 8; matrix products, arithmetic and copies ran while one was open for 2% -> 2% of each run, Pallas kernels for 15% -> 15%
where the time goes in v2:
time: 48.7 us; the launch traced here: 48.4 us
  starting transfers between devices  18.5 us (38%)
  Pallas kernels  15.8 us (32%)
  waiting for transfers between devices  9.79 us (20%)
  local copies, waits for them, and re-layouts  2.17 us (4%)
  other arithmetic  1.38 us (3%)
  between operations  0.79 us (2%)
    ppermute x8, starting transfers between devices, along(): return lax.ppermute(value, 'db', pairs)  13.1 us
    pallas_call x1, Pallas kernels, local(): pl.pallas_call(score_kernel, out_shape=[jax.ShapeDtypeStruct((rows, featu...  7.63 us
    ppermute x8, waiting for transfers between devices, along(): return lax.ppermute(value, 'db', pairs)  5.55 us
    ppermute x4, starting transfers between devices, cross(): return lax.ppermute(value, ('pb', 'db'), pairs)  4.12 us
    ppermute x5, waiting for transfers between devices, swap(): return lax.ppermute(value, 'db', [(i, i ^ 1) for i in range(owners)])  3.1 us
    pallas_call x1, Pallas kernels, local(): pl.pallas_call(functools.partial(count_kernel, planes), out_shape=[jax.Sh...  3 us
    pallas_call x2, Pallas kernels, sums(): pl.pallas_call(functools.partial(sums_kernel, len(blocks)), out_shape=out...  2.92 us
    pallas_call x2, Pallas kernels, late(): pl.pallas_call(functools.partial(late_kernel, number), out_shape=jax.Shap...  2.19 us
  transfers between devices with their start and end apart: 17, of which 8 were waited for; matrix products, arithmetic and copies ran while one was open for 2% of the time, Pallas kernels for 15%

profile of v2, /device:TPU:0, one launch (start us, length us, event | category | flops | bytes accessed | tf_op | source)
XLA Modules:
  0.0 48.4 jit_solution(17914189053941023302)
XLA Ops:
  0.6 1.0 %constant_dynamic-slice_fusion = (bf16[64,768]{1,0:T(8,128)(2,1)S(1)}, bf16[64,768]{1,0:T(8,128)(2,1)S(1)}) fusion(bf16[256,768]{1,0:T(8,128)(2,1)} %database_ref.1, s32[]{:T(128)S(6)} %select_n.31, s32[]{:T(128)S(6)} %select_n.30), kind=kLoop, calls=%fused_computation.8 | loop fusion | bytes 393224 | tf_op jit(solution)/shard_map/dynamic_slice | solution.py:250
  1.6 4.1 %collective-permute-start.2 = (bf16[64,768]{1,0:T(8,128)(2,1)S(1)}, bf16[64,768]{1,0:T(8,128)(2,1)S(1)}, u32[]{:S(2)}, u32[]{:S(2)}) collective-permute-start(bf16[64,768]{1,0:T(8,128)(2,1)S(1)} %get-tuple-element.23), channel_id=1, source_target_pairs={{0,4},{1,5},{2,6},{3,7},{4,0},{5,1},{6,2},{7,3},{8,12},{9,13},{10,... | collective-permute-start | bytes 294920 | tf_op jit(solution)/shard_map/ppermute | solution.py:228
  5.7 1.6 %collective-permute-start.1 = (bf16[64,768]{1,0:T(8,128)(2,1)S(1)}, bf16[64,768]{1,0:T(8,128)(2,1)S(1)}, u32[]{:S(2)}, u32[]{:S(2)}) collective-permute-start(bf16[64,768]{1,0:T(8,128)(2,1)S(1)} %get-tuple-element.23), channel_id=1, source_target_pairs={{0,2},{1,3},{2,0},{3,1},{4,6},{5,7},{6,4},{7,5},{8,10},{9,11},{10,... | collective-permute-start | bytes 294920 | tf_op jit(solution)/shard_map/ppermute | solution.py:228
  7.3 0.7 %fusion = s32[256,16]{0,1:T(8,128)S(1)} fusion(s32[256,16]{0,1:T(8,128)} %param.5, s32[256]{0:T(256)} %param.6), kind=kLoop, calls=%fused_computation.3 | loop fusion | flops 8192 | bytes 33792 | tf_op jit(solution)/shard_map/jit(_where)/select_n | solution.py:259
  8.0 0.1 copy.7
  8.2 0.6 %collective-permute-start = (s32[32,128]{1,0:T(8,128)S(1)}, s32[32,128]{1,0:T(8,128)S(1)}, u32[]{:S(2)}, u32[]{:S(2)}) collective-permute-start(s32[32,128]{1,0:T(8,128)S(1)} %reshape.11.own_ref), channel_id=1, source_target_pairs={{0,1},{1,0},{2,3},{3,2},{4,5},{5,4},{6,7},{7,6},{8,9},{9,8},{10,11... | collective-permute-start | bytes 49160 | tf_op jit(solution)/shard_map/ppermute | solution.py:240
  8.8 0.3 collective-permute-start.7
  9.1 1.4 %collective-permute-done.2.far_ref.rest_1_ = bf16[64,768]{1,0:T(8,128)(2,1)S(1)} collective-permute-done((bf16[64,768]{1,0:T(8,128)(2,1)S(1)}, bf16[64,768]{1,0:T(8,128)(2,1)S(1)}, u32[]{:S(2)}, u32[]{:S(2)}) %collective-permute-start.2) | collective-permute-done | bytes 98336 | tf_op jit(solution)/shard_map/ppermute | solution.py:228
  10.5 1.2 %collective-permute-start.4 = (bf16[64,768]{1,0:T(8,128)(2,1)S(1)}, bf16[64,768]{1,0:T(8,128)(2,1)S(1)}, u32[]{:S(2)}, u32[]{:S(2)}) collective-permute-start(bf16[64,768]{1,0:T(8,128)(2,1)S(1)} %collective-permute-done.2.far_ref.rest_1_), channel_id=1, source_target_pairs={{0,2},{1,3},{2,0},{3,1},{4,6},{5,7},{6,4},{7,5},{8,10},{9,11},{10,... | collective-permute-start | bytes 294920 | tf_op jit(solution)/shard_map/ppermute | solution.py:228
  11.7 1.6 %collective-permute-start.5 = (bf16[128,768]{1,0:T(8,128)(2,1)S(1)}, bf16[128,768]{1,0:T(8,128)(2,1)S(1)}, u32[]{:S(2)}, u32[]{:S(2)}) collective-permute-start(bf16[128,768]{1,0:T(8,128)(2,1)S(1)} %constant_dynamic-update-slice_fusion), channel_id=1, source_target_pairs={{0,8},{1,17},{2,10},{3,19},{4,12},{5,21},{6,14},{7,23},{8,0},{9,25... | collective-permute-start | bytes 589832 | tf_op jit(solution)/shard_map/ppermute | solution.py:247
  13.3 1.5 %collective-permute-start.6 = (bf16[128,768]{1,0:T(8,128)(2,1)S(1)}, bf16[128,768]{1,0:T(8,128)(2,1)S(1)}, u32[]{:S(2)}, u32[]{:S(2)}) collective-permute-start(bf16[128,768]{1,0:T(8,128)(2,1)S(1)} %constant_dynamic-update-slice_fusion), channel_id=1, source_target_pairs={{0,16},{1,9},{2,18},{3,11},{4,20},{5,13},{6,22},{7,15},{8,24},{9,1... | collective-permute-start | bytes 589832 | tf_op jit(solution)/shard_map/ppermute | solution.py:247
  14.8 1.0 %copy-done = bf16[256,768]{1,0:T(8,128)(2,1)S(1)} copy-done((bf16[256,768]{1,0:T(8,128)(2,1)S(1)}, bf16[256,768]{1,0:T(8,128)(2,1)}, u32[]{:S(2)}) %copy-start) | copy-done | bytes 393240
  15.8 3.0 %counts.1 = (bf16[512,256]{1,0:T(8,128)(2,1)S(1)}, bf16[512,512]{1,0:T(8,128)(2,1)S(1)}, bf16[512,384]{1,0:T(8,128)(2,1)S(1)}, bf16[256,768]{1,0:T(8,128)(2,1)S(...) custom-call(s32[32,128]{1,0:T(8,128)S(1)} %collective-permute-done.twin_ref, ...), custom_call_target="tpu_custom_call" | custom-call | flops 67108864 | bytes 262144 | tf_op jit(solution)/shard_map/counts/pallas_call | solution.py:264
  18.8 1.4 %collective-permute-start.8 = (bf16[128,768]{1,0:T(8,128)(2,1)S(1)}, bf16[128,768]{1,0:T(8,128)(2,1)S(1)}, u32[]{:S(2)}, u32[]{:S(2)}) collective-permute-start(bf16[128,768]{1,0:T(8,128)(2,1)S(1)} %get-tuple-element.17), channel_id=1, source_target_pairs={{0,2},{1,3},{2,0},{3,1},{4,6},{5,7},{6,4},{7,5},{8,10},{9,11},{10,... | collective-permute-start | bytes 589832 | tf_op jit(solution)/shard_map/ppermute | solution.py:228
  20.2 0.5 %collective-permute-start.10 = (bf16[64,768]{1,0:T(8,128)(2,1)S(1)}, bf16[64,768]{1,0:T(8,128)(2,1)S(1)}, u32[]{:S(2)}, u32[]{:S(2)}) collective-permute-start(bf16[64,768]{1,0:T(8,128)(2,1)S(1)} %get-tuple-element.18), channel_id=1, source_target_pairs={{0,16},{1,9},{2,18},{3,11},{4,20},{5,13},{6,22},{7,15},{8,24},{9,1... | collective-permute-start | bytes 294920 | tf_op jit(solution)/shard_map/ppermute | solution.py:247
  20.7 0.5 %collective-permute-start.9 = (bf16[64,768]{1,0:T(8,128)(2,1)S(1)}, bf16[64,768]{1,0:T(8,128)(2,1)S(1)}, u32[]{:S(2)}, u32[]{:S(2)}) collective-permute-start(bf16[64,768]{1,0:T(8,128)(2,1)S(1)} %get-tuple-element.18), channel_id=1, source_target_pairs={{0,8},{1,17},{2,10},{3,19},{4,12},{5,21},{6,14},{7,23},{8,0},{9,25... | collective-permute-start | bytes 294920 | tf_op jit(solution)/shard_map/ppermute | solution.py:247
  21.3 1.1 %own_sums.1.rest_5_ = f32[512,768]{1,0:T(8,128)S(1)} custom-call(bf16[256,768]{1,0:T(8,128)(2,1)S(1)} %collective-permute-done.3.twin_ref.dest_ref, bf16[256,768]{1,0:T(8,128)(2,1)S(1)} %get-tuple-element.12.own_ref.rest_0_.dest_ref, bf16[512,256]{1,0:T(8,128)(2,1)S(1)} %get-tuple-element.14.counts_ref, ...), custom_call_target="tpu_custom_call" | custom-call | flops 67108864 | bytes 262144 | tf_op jit(solution)/shard_map/own_sums/pallas_call | solution.py:308
  22.4 1.8 %near_sums.1.early_ref = f32[512,768]{1,0:T(8,128)S(1)} custom-call(bf16[256,768]{1,0:T(8,128)(2,1)S(1)} %collective-permute-done.3.twin_ref.dest_ref, bf16[256,768]{1,0:T(8,128)(2,1)S(1)} %get-tuple-element.12.own_ref.rest_0_.dest_ref, bf16[512,512]{1,0:T(8,128)(2,1)S(1)} %get-tuple-element.13.counts_ref, ...), custom_call_target="tpu_custom_call" | custom-call | flops 67108864 | bytes 262144 | tf_op jit(solution)/shard_map/near_sums/pallas_call | solution.py:308
  24.2 0.6 %collective-permute-done.10.rest_3_ = bf16[64,768]{1,0:T(8,128)(2,1)S(1)} collective-permute-done((bf16[64,768]{1,0:T(8,128)(2,1)S(1)}, bf16[64,768]{1,0:T(8,128)(2,1)S(1)}, u32[]{:S(2)}, u32[]{:S(2)}) %collective-permute-start.10) | collective-permute-done | bytes 98336 | tf_op jit(solution)/shard_map/ppermute | solution.py:247
  24.8 0.5 %collective-permute-done.9.rest_2_ = bf16[64,768]{1,0:T(8,128)(2,1)S(1)} collective-permute-done((bf16[64,768]{1,0:T(8,128)(2,1)S(1)}, bf16[64,768]{1,0:T(8,128)(2,1)S(1)}, u32[]{:S(2)}, u32[]{:S(2)}) %collective-permute-start.9) | collective-permute-done | bytes 98336 | tf_op jit(solution)/shard_map/ppermute | solution.py:247
  25.3 1.1 %late_sums.3.twin_a_ref = f32[256,768]{1,0:T(8,128)S(1)} custom-call(bf16[256,768]{1,0:T(8,128)(2,1)S(1)} %collective-permute-done.3.twin_ref.dest_ref, f32[512,768]{1,0:T(8,128)S(1)} %near_sums.1.early_ref, bf16[512,384]{1,0:T(8,128)(2,1)S(1)} %get-tuple-element.15.counts_ref, bf16[64,768]{1,0:T(8,128)(2,1)S(1)} %collective-permute-done.7.rest_1_.rest_0_, ...), custom_call_target="tpu_custom_call" | custom-call | tf_op jit(solution)/shard_map/late_sums/pallas_call | solution.py:322
  26.5 1.1 %late_sums.2.own_a_ref = f32[256,768]{1,0:T(8,128)S(1)} custom-call(bf16[256,768]{1,0:T(8,128)(2,1)S(1)} %get-tuple-element.12.own_ref.rest_0_.dest_ref, f32[512,768]{1,0:T(8,128)S(1)} %near_sums.1.early_ref, bf16[512,384]{1,0:T(8,128)(2,1)S(1)} %get-tuple-element.15.counts_ref, bf16[64,768]{1,0:T(8,128)(2,1)S(1)} %collective-permute-done.7.rest_1_.rest_0_, ...), custom_call_target="tpu_custom_call" | custom-call | tf_op jit(solution)/shard_map/late_sums/pallas_call | solution.py:322
  27.6 0.6 %collective-permute-start.12 = (f32[256,768]{1,0:T(8,128)S(1)}, f32[256,768]{1,0:T(8,128)S(1)}, u32[]{:S(2)}, u32[]{:S(2)}) collective-permute-start(f32[256,768]{1,0:T(8,128)S(1)} %late_sums.2.own_a_ref), channel_id=1, source_target_pairs={{0,1},{1,0},{2,3},{3,2},{4,5},{5,4},{6,7},{7,6},{8,9},{9,8},{10,11... | collective-permute-start | bytes 2359304 | tf_op jit(solution)/shard_map/ppermute | solution.py:240
  28.2 0.6 %collective-permute-done.11.own_b_ref = f32[256,768]{1,0:T(8,128)S(1)} collective-permute-done((f32[256,768]{1,0:T(8,128)S(1)}, f32[256,768]{1,0:T(8,128)S(1)}, u32[]{:S(2)}, u32[]{:S(2)}) %collective-permute-start.11) | collective-permute-done | bytes 786464 | tf_op jit(solution)/shard_map/ppermute | solution.py:240
  28.8 1.3 %collective-permute-done.12.twin_b_ref = f32[256,768]{1,0:T(8,128)S(1)} collective-permute-done((f32[256,768]{1,0:T(8,128)S(1)}, f32[256,768]{1,0:T(8,128)S(1)}, u32[]{:S(2)}, u32[]{:S(2)}) %collective-permute-start.12) | collective-permute-done | bytes 786464 | tf_op jit(solution)/shard_map/ppermute | solution.py:240
  30.1 7.6 %scores.1 = (bf16[256,768]{1,0:T(8,128)(2,1)}, f32[64,128]{1,0:T(8,128)S(1)}) custom-call(f32[256,768]{1,0:T(8,128)S(1)} %late_sums.2.own_a_ref, f32[256,768]{1,0:T(8,128)S(1)} %collective-permute-done.11.own_b_ref, f32[256,768]{1,0:T(8,128)S(1)} %late_sums.3.twin_a_ref, f32[256,768]{1,0:T(8,128)S(1)} %collective-permute-done.12.twin_b_ref, ...), custom_call_target="tpu_custom_call" | custom-call | flops 6442450944 | bytes 12582912 | tf_op jit(solution)/shard_map/scores/pallas_call | solution.py:337
  37.7 3.9 %collective-permute-start.13 = (f32[64,128]{1,0:T(8,128)S(1)}, f32[64,128]{1,0:T(8,128)S(1)}, u32[]{:S(2)}, u32[]{:S(2)}) collective-permute-start(f32[64,128]{1,0:T(8,128)S(1)} %get-tuple-element.21), channel_id=1, source_target_pairs={{0,6},{1,7},{2,4},{3,5},{4,2},{5,3},{6,0},{7,1},{8,14},{9,15},{10,... | collective-permute-start | bytes 98312 | tf_op jit(solution)/shard_map/ppermute | solution.py:228
  41.7 0.6 %collective-permute-start.15 = (f32[64,128]{1,0:T(8,128)S(1)}, f32[64,128]{1,0:T(8,128)S(1)}, u32[]{:S(2)}, u32[]{:S(2)}) collective-permute-start(f32[64,128]{1,0:T(8,128)S(1)} %get-tuple-element.21), channel_id=1, source_target_pairs={{0,2},{1,3},{2,0},{3,1},{4,6},{5,7},{6,4},{7,5},{8,10},{9,11},{10,... | collective-permute-start | bytes 98312 | tf_op jit(solution)/shard_map/ppermute | solution.py:228
  42.3 1.3 %collective-permute-done.13 = f32[64,128]{1,0:T(8,128)S(1)} collective-permute-done((f32[64,128]{1,0:T(8,128)S(1)}, f32[64,128]{1,0:T(8,128)S(1)}, u32[]{:S(2)}, u32[]{:S(2)}) %collective-permute-start.13) | collective-permute-done | bytes 32800 | tf_op jit(solution)/shard_map/ppermute | solution.py:228
  43.6 2.9 %collective-permute-done.14 = f32[64,128]{1,0:T(8,128)S(1)} collective-permute-done((f32[64,128]{1,0:T(8,128)S(1)}, f32[64,128]{1,0:T(8,128)S(1)}, u32[]{:S(2)}, u32[]{:S(2)}) %collective-permute-start.14) | collective-permute-done | bytes 32800 | tf_op jit(solution)/shard_map/ppermute | solution.py:228
  46.6 1.2 %collective-permute-done.16 = f32[64,128]{1,0:T(8,128)S(1)} collective-permute-done((f32[64,128]{1,0:T(8,128)S(1)}, f32[64,128]{1,0:T(8,128)S(1)}, u32[]{:S(2)}, u32[]{:S(2)}) %collective-permute-start.16) | collective-permute-done | bytes 32800 | tf_op jit(solution)/shard_map/ppermute | solution.py:240
  47.8 0.6 %maximum_bitcast_fusion = f32[16384]{0:T(1024)} fusion(f32[64,128]{1,0:T(8,128)S(1)} %get-tuple-element.25, f32[64,128]{1,0:T(8,128)S(1)} %get-tuple-element.24), kind=kLoop, calls=%fused_computation | loop fusion | flops 16384 | bytes 131072 | tf_op jit(solution)/shard_map/reshape | solution.py:363
  (20 shorter events, 0.3 us)
Async XLA Ops:
  1.6 8.9 %collective-permute-start.2 = (bf16[64,768]{1,0:T(8,128)(2,1)S(1)}, bf16[64,768]{1,0:T(8,128)(2,1)S(1)}, u32[]{:S(2)}, u32[]{:S(2)}) collective-permute-start(bf16[64,768]{1,0:T(8,128)(2,1)S(1)} %get-tuple-element.23), channel_id=1, source_target_pairs={{0,4},{1,5},{2,6},{3,7},{4,0},{5,1},{6,2},{7,3},{8,12},{9,13},{10,... | collective-permute-start | bytes 294920 | tf_op jit(solution)/shard_map/ppermute | solution.py:228
  5.7 6.0 %collective-permute-start.1 = (bf16[64,768]{1,0:T(8,128)(2,1)S(1)}, bf16[64,768]{1,0:T(8,128)(2,1)S(1)}, u32[]{:S(2)}, u32[]{:S(2)}) collective-permute-start(bf16[64,768]{1,0:T(8,128)(2,1)S(1)} %get-tuple-element.23), channel_id=1, source_target_pairs={{0,2},{1,3},{2,0},{3,1},{4,6},{5,7},{6,4},{7,5},{8,10},{9,11},{10,... | collective-permute-start | bytes 294920 | tf_op jit(solution)/shard_map/ppermute | solution.py:228
  7.3 13.4 %collective-permute-start.3 = (bf16[256,768]{1,0:T(8,128)(2,1)}, bf16[256,768]{1,0:T(8,128)(2,1)S(1)}, u32[]{:S(2)}, u32[]{:S(2)}) collective-permute-start(bf16[256,768]{1,0:T(8,128)(2,1)} %database_ref.1), channel_id=1, source_target_pairs={{0,1},{1,0},{2,3},{3,2},{4,5},{5,4},{6,7},{7,6},{8,9},{9,8},{10,11... | collective-permute-start | bytes 1179656 | tf_op jit(solution)/shard_map/ppermute | solution.py:240
  8.2 5.0 %collective-permute-start = (s32[32,128]{1,0:T(8,128)S(1)}, s32[32,128]{1,0:T(8,128)S(1)}, u32[]{:S(2)}, u32[]{:S(2)}) collective-permute-start(s32[32,128]{1,0:T(8,128)S(1)} %reshape.11.own_ref), channel_id=1, source_target_pairs={{0,1},{1,0},{2,3},{3,2},{4,5},{5,4},{6,7},{7,6},{8,9},{9,8},{10,11... | collective-permute-start | bytes 49160 | tf_op jit(solution)/shard_map/ppermute | solution.py:240
  8.8 10.0 %collective-permute-start.7 = (bf16[64,768]{1,0:T(8,128)(2,1)S(1)}, bf16[64,768]{1,0:T(8,128)(2,1)S(1)}, u32[]{:S(2)}, u32[]{:S(2)}) collective-permute-start(bf16[64,768]{1,0:T(8,128)(2,1)S(1)} %get-tuple-element.22.rest_0_), channel_id=1, source_target_pairs={{0,4},{1,5},{2,6},{3,7},{4,0},{5,1},{6,2},{7,3},{8,12},{9,13},{10,... | collective-permute-start | bytes 294920 | tf_op jit(solution)/shard_map/ppermute | solution.py:228
  10.5 8.3 %collective-permute-start.4 = (bf16[64,768]{1,0:T(8,128)(2,1)S(1)}, bf16[64,768]{1,0:T(8,128)(2,1)S(1)}, u32[]{:S(2)}, u32[]{:S(2)}) collective-permute-start(bf16[64,768]{1,0:T(8,128)(2,1)S(1)} %collective-permute-done.2.far_ref.rest_1_), channel_id=1, source_target_pairs={{0,2},{1,3},{2,0},{3,1},{4,6},{5,7},{6,4},{7,5},{8,10},{9,11},{10,... | collective-permute-start | bytes 294920 | tf_op jit(solution)/shard_map/ppermute | solution.py:228
  11.7 10.7 %collective-permute-start.5 = (bf16[128,768]{1,0:T(8,128)(2,1)S(1)}, bf16[128,768]{1,0:T(8,128)(2,1)S(1)}, u32[]{:S(2)}, u32[]{:S(2)}) collective-permute-start(bf16[128,768]{1,0:T(8,128)(2,1)S(1)} %constant_dynamic-update-slice_fusion), channel_id=1, source_target_pairs={{0,8},{1,17},{2,10},{3,19},{4,12},{5,21},{6,14},{7,23},{8,0},{9,25... | collective-permute-start | bytes 589832 | tf_op jit(solution)/shard_map/ppermute | solution.py:247
  13.3 9.2 %collective-permute-start.6 = (bf16[128,768]{1,0:T(8,128)(2,1)S(1)}, bf16[128,768]{1,0:T(8,128)(2,1)S(1)}, u32[]{:S(2)}, u32[]{:S(2)}) collective-permute-start(bf16[128,768]{1,0:T(8,128)(2,1)S(1)} %constant_dynamic-update-slice_fusion), channel_id=1, source_target_pairs={{0,16},{1,9},{2,18},{3,11},{4,20},{5,13},{6,22},{7,15},{8,24},{9,1... | collective-permute-start | bytes 589832 | tf_op jit(solution)/shard_map/ppermute | solution.py:247
  14.8 1.0 %copy-start = (bf16[256,768]{1,0:T(8,128)(2,1)S(1)}, bf16[256,768]{1,0:T(8,128)(2,1)}, u32[]{:S(2)}) copy-start(bf16[256,768]{1,0:T(8,128)(2,1)} %database_ref.1) | copy-start | bytes 1179652
  18.8 6.5 %collective-permute-start.8 = (bf16[128,768]{1,0:T(8,128)(2,1)S(1)}, bf16[128,768]{1,0:T(8,128)(2,1)S(1)}, u32[]{:S(2)}, u32[]{:S(2)}) collective-permute-start(bf16[128,768]{1,0:T(8,128)(2,1)S(1)} %get-tuple-element.17), channel_id=1, source_target_pairs={{0,2},{1,3},{2,0},{3,1},{4,6},{5,7},{6,4},{7,5},{8,10},{9,11},{10,... | collective-permute-start | bytes 589832 | tf_op jit(solution)/shard_map/ppermute | solution.py:228
  20.2 4.6 %collective-permute-start.10 = (bf16[64,768]{1,0:T(8,128)(2,1)S(1)}, bf16[64,768]{1,0:T(8,128)(2,1)S(1)}, u32[]{:S(2)}, u32[]{:S(2)}) collective-permute-start(bf16[64,768]{1,0:T(8,128)(2,1)S(1)} %get-tuple-element.18), channel_id=1, source_target_pairs={{0,16},{1,9},{2,18},{3,11},{4,20},{5,13},{6,22},{7,15},{8,24},{9,1... | collective-permute-start | bytes 294920 | tf_op jit(solution)/shard_map/ppermute | solution.py:247
  20.7 4.6 %collective-permute-start.9 = (bf16[64,768]{1,0:T(8,128)(2,1)S(1)}, bf16[64,768]{1,0:T(8,128)(2,1)S(1)}, u32[]{:S(2)}, u32[]{:S(2)}) collective-permute-start(bf16[64,768]{1,0:T(8,128)(2,1)S(1)} %get-tuple-element.18), channel_id=1, source_target_pairs={{0,8},{1,17},{2,10},{3,19},{4,12},{5,21},{6,14},{7,23},{8,0},{9,25... | collective-permute-start | bytes 294920 | tf_op jit(solution)/shard_map/ppermute | solution.py:247
  26.4 2.4 %collective-permute-start.11 = (f32[256,768]{1,0:T(8,128)S(1)}, f32[256,768]{1,0:T(8,128)S(1)}, u32[]{:S(2)}, u32[]{:S(2)}) collective-permute-start(f32[256,768]{1,0:T(8,128)S(1)} %late_sums.3.twin_a_ref), channel_id=1, source_target_pairs={{0,1},{1,0},{2,3},{3,2},{4,5},{5,4},{6,7},{7,6},{8,9},{9,8},{10,11... | collective-permute-start | bytes 2359304 | tf_op jit(solution)/shard_map/ppermute | solution.py:240
  27.6 2.5 %collective-permute-start.12 = (f32[256,768]{1,0:T(8,128)S(1)}, f32[256,768]{1,0:T(8,128)S(1)}, u32[]{:S(2)}, u32[]{:S(2)}) collective-permute-start(f32[256,768]{1,0:T(8,128)S(1)} %late_sums.2.own_a_ref), channel_id=1, source_target_pairs={{0,1},{1,0},{2,3},{3,2},{4,5},{5,4},{6,7},{7,6},{8,9},{9,8},{10,11... | collective-permute-start | bytes 2359304 | tf_op jit(solution)/shard_map/ppermute | solution.py:240
  37.7 5.8 %collective-permute-start.13 = (f32[64,128]{1,0:T(8,128)S(1)}, f32[64,128]{1,0:T(8,128)S(1)}, u32[]{:S(2)}, u32[]{:S(2)}) collective-permute-start(f32[64,128]{1,0:T(8,128)S(1)} %get-tuple-element.21), channel_id=1, source_target_pairs={{0,6},{1,7},{2,4},{3,5},{4,2},{5,3},{6,0},{7,1},{8,14},{9,15},{10,... | collective-permute-start | bytes 98312 | tf_op jit(solution)/shard_map/ppermute | solution.py:228
  41.7 4.8 %collective-permute-start.14 = (f32[64,128]{1,0:T(8,128)S(1)}, f32[64,128]{1,0:T(8,128)S(1)}, u32[]{:S(2)}, u32[]{:S(2)}) collective-permute-start(f32[64,128]{1,0:T(8,128)S(1)} %get-tuple-element.21), channel_id=1, source_target_pairs={{0,4},{1,5},{2,6},{3,7},{4,0},{5,1},{6,2},{7,3},{8,12},{9,13},{10,... | collective-permute-start | bytes 98312 | tf_op jit(solution)/shard_map/ppermute | solution.py:228
  41.7 4.8 %collective-permute-start.15 = (f32[64,128]{1,0:T(8,128)S(1)}, f32[64,128]{1,0:T(8,128)S(1)}, u32[]{:S(2)}, u32[]{:S(2)}) collective-permute-start(f32[64,128]{1,0:T(8,128)S(1)} %get-tuple-element.21), channel_id=1, source_target_pairs={{0,2},{1,3},{2,0},{3,1},{4,6},{5,7},{6,4},{7,5},{8,10},{9,11},{10,... | collective-permute-start | bytes 98312 | tf_op jit(solution)/shard_map/ppermute | solution.py:228
  46.5 1.3 %collective-permute-start.16 = (f32[64,128]{1,0:T(8,128)S(1)}, f32[64,128]{1,0:T(8,128)S(1)}, u32[]{:S(2)}, u32[]{:S(2)}) collective-permute-start(f32[64,128]{1,0:T(8,128)S(1)} %maximum_maximum_fusion), channel_id=1, source_target_pairs={{0,1},{1,0},{2,3},{3,2},{4,5},{5,4},{6,7},{7,6},{8,9},{9,8},{10,11... | collective-permute-start | bytes 98312 | tf_op jit(solution)/shard_map/ppermute | solution.py:240

commit v3 on v2

--- a/solution.py
+++ b/solution.py
@@ -34,10 +34,10 @@
 
 
 def count_kernel(
-    planes, twin_ref, own_ref, database_ref, queries_ref, adjacent_ref, far_ref, *rest
+    planes, twin_ref, own_ref, database_ref, queries_ref, *rest
 ):
-    count_refs = rest[:-7]
-    copy_ref, held_ref, near_ref, tiles_ref, lows_ref, sem, queries_sem = rest[-7:]
+    count_refs = rest[:-6]
+    copy_ref, held_ref, tiles_ref, lows_ref, sem, queries_sem = rest[-6:]
     rows = copy_ref.shape[0]
     fanout = own_ref.shape[0] * 128 // rows
     quarter = rows // 4
@@ -49,7 +49,6 @@
     copy.start()
     queries = fetch_queries(queries_ref, held_ref, 0, queries_sem)
     queries.start()
-    near_ref[...] = adjacent_ref[...]
     me, plane, core = position_of()
     bits = rows.bit_length() - 1
     lines = own_ref.shape[0]
@@ -261,7 +260,7 @@
     padded = lambda size: (size + 127) // 128 * 128
     span = (planes - 1) * quarter
     widths = (rows, 3 * span - 2 * quarter, span + 2 * quarter)
-    *counts, own, first_queries, near_first = pl.pallas_call(
+    *counts, own, first_queries = pl.pallas_call(
         functools.partial(count_kernel, planes),
         out_shape=[
             jax.ShapeDtypeStruct((2 * rows, padded(width)), jnp.bfloat16) for width in widths
@@ -269,10 +268,9 @@
         + [
             jax.ShapeDtypeStruct((rows, features), jnp.bfloat16),
             jax.ShapeDtypeStruct((count // 4, features), jnp.bfloat16),
-            jax.ShapeDtypeStruct((quarter, features), jnp.bfloat16),
-        ],
-        in_specs=[vmem, vmem] + [pl.BlockSpec(memory_space=pltpu.HBM)] * 2 + [vmem] * 2,
-        out_specs=[vmem] * 6,
+        ],
+        in_specs=[vmem, vmem] + [pl.BlockSpec(memory_space=pltpu.HBM)] * 2,
+        out_specs=[vmem] * 5,
         scratch_shapes=[
             pltpu.VMEM((2 * wanted.shape[0], 128), jnp.int32),
             pltpu.VMEM((2 * wanted.shape[0], 128), jnp.int32),
@@ -280,9 +278,9 @@
             pltpu.SemaphoreType.DMA(()),
         ],
         compiler_params=pltpu.CompilerParams(vmem_limit_bytes=30 * MIB),
-        cost_estimate=pl.CostEstimate(flops=1<<26, bytes_accessed=4 * rows * rows, transcendentals=0),
+        cost_estimate=pl.CostEstimate(flops=1<<29, bytes_accessed=4 * rows * rows, transcendentals=0),
         name="counts",
-    )(twin_wanted, wanted, database, queries, near[0], near[planes // 2 - 1])
+    )(twin_wanted, wanted, database, queries)
     forward, message = pl.pallas_call(
         join_kernel,
         out_shape=[
@@ -293,12 +291,12 @@
         out_specs=[vmem] * 2,
         compiler_params=pltpu.CompilerParams(vmem_limit_bytes=8 * MIB),
         name="join",
-    )(near[-1], *across, near_first)
+    )(near[-1], *across, own)
     across = across[1:] + [along(message, 1)]
     beside_last = cross(forward, (1, 2))
     behind_last = cross(forward, (2, 1))
 
-    def sums(name, counts, blocks, before=None):
+    def sums(name, counts, blocks, flops, before=None):
         out = [jax.ShapeDtypeStruct((2 * rows, features), jnp.float32)]
         operands = [twin, own, counts, *blocks]
         specs = [vmem] * len(operands)
@@ -311,12 +309,12 @@
             in_specs=specs,
             out_specs=[vmem] * len(out),
             compiler_params=pltpu.CompilerParams(vmem_limit_bytes=30 * MIB),
-            cost_estimate=pl.CostEstimate(flops=1<<26, bytes_accessed=4 * rows * rows, transcendentals=0),
+            cost_estimate=pl.CostEstimate(flops=flops, bytes_accessed=4 * rows * rows, transcendentals=0),
             name=name,
         )(*operands)
 
-    (total,) = sums("own_sums", counts[0], [own])
-    (total,) = sums("near_sums", counts[1], [*near, beside, behind], total)
+    (total,) = sums("own_sums", counts[0], [own], 1<<31)
+    (total,) = sums("near_sums", counts[1], [*near, beside, behind], 1<<26, total)
 
     def late(number, dest):
         return pl.pallas_call(

time: 48.7 us -> 49.2 us (1.010)
    ppermute x4, starting transfers between devices: 4.12 us -> 6.15 us  [cross(): return lax.ppermute(value, ('pb', 'db'), pairs)]
    ppermute x8, starting transfers between devices: 13.1 us -> 11.4 us  [along(): return lax.ppermute(value, 'db', pairs)]
    ppermute x4, waiting for transfers between devices: 1.14 us -> 0.01 us  [cross(): return lax.ppermute(value, ('pb', 'db'), pairs)]
    ppermute x8, waiting for transfers between devices: 5.55 us -> 6.35 us  [along(): return lax.ppermute(value, 'db', pairs)]
    ppermute x5, waiting for transfers between devices: 3.1 us -> 3.6 us  [swap(): return lax.ppermute(value, 'db', [(i, i ^ 1) for i in range(owners)])]
  transfers between devices with their start and end apart: 17 -> 17, of which waited for: 8 -> 8; matrix products, arithmetic and copies ran while one was open for 2% -> 2% of each run, Pallas kernels for 15% -> 14%
where the time goes in v3:
time: 49.2 us; the launch traced here: 48.9 us
  starting transfers between devices  18.9 us (38%)
  Pallas kernels  15.8 us (32%)
  waiting for transfers between devices  9.96 us (20%)
  local copies, waits for them, and re-layouts  2.17 us (4%)
  other arithmetic  1.38 us (3%)
  between operations  0.79 us (2%)
    ppermute x8, starting transfers between devices, along(): return lax.ppermute(value, 'db', pairs)  11.4 us
    pallas_call x1, Pallas kernels, local(): pl.pallas_call(score_kernel, out_shape=[jax.ShapeDtypeStruct((rows, featu...  7.63 us
    ppermute x8, waiting for transfers between devices, along(): return lax.ppermute(value, 'db', pairs)  6.35 us
    ppermute x4, starting transfers between devices, cross(): return lax.ppermute(value, ('pb', 'db'), pairs)  6.15 us
    ppermute x5, waiting for transfers between devices, swap(): return lax.ppermute(value, 'db', [(i, i ^ 1) for i in range(owners)])  3.6 us
    pallas_call x1, Pallas kernels, local(): pl.pallas_call(functools.partial(count_kernel, planes), out_shape=[jax.Sh...  3 us
    pallas_call x2, Pallas kernels, sums(): pl.pallas_call(functools.partial(sums_kernel, len(blocks)), out_shape=out...  2.93 us
    pallas_call x2, Pallas kernels, late(): pl.pallas_call(functools.partial(late_kernel, number), out_shape=jax.Shap...  2.18 us
  transfers between devices with their start and end apart: 17, of which 8 were waited for; matrix products, arithmetic and copies ran while one was open for 2% of the time, Pallas kernels for 14%

profile of v3, /device:TPU:0, one launch (start us, length us, event | category | flops | bytes accessed | tf_op | source)
XLA Modules:
  0.0 48.9 jit_solution(15109503823598686984)
XLA Ops:
  0.6 1.0 %constant_dynamic-slice_fusion = (bf16[64,768]{1,0:T(8,128)(2,1)S(1)}, bf16[64,768]{1,0:T(8,128)(2,1)S(1)}) fusion(bf16[256,768]{1,0:T(8,128)(2,1)} %database_ref.1, s32[]{:T(128)S(6)} %select_n.31, s32[]{:T(128)S(6)} %select_n.30), kind=kLoop, calls=%fused_computation.8 | loop fusion | bytes 393224 | tf_op jit(solution)/shard_map/dynamic_slice | solution.py:249
  1.6 4.1 %collective-permute-start.3 = (bf16[64,768]{1,0:T(8,128)(2,1)S(1)}, bf16[64,768]{1,0:T(8,128)(2,1)S(1)}, u32[]{:S(2)}, u32[]{:S(2)}) collective-permute-start(bf16[64,768]{1,0:T(8,128)(2,1)S(1)} %get-tuple-element.21), channel_id=1, source_target_pairs={{0,4},{1,5},{2,6},{3,7},{4,0},{5,1},{6,2},{7,3},{8,12},{9,13},{10,... | collective-permute-start | bytes 294920 | tf_op jit(solution)/shard_map/ppermute | solution.py:227
  5.7 1.6 %collective-permute-start.2 = (bf16[64,768]{1,0:T(8,128)(2,1)S(1)}, bf16[64,768]{1,0:T(8,128)(2,1)S(1)}, u32[]{:S(2)}, u32[]{:S(2)}) collective-permute-start(bf16[64,768]{1,0:T(8,128)(2,1)S(1)} %get-tuple-element.21), channel_id=1, source_target_pairs={{0,2},{1,3},{2,0},{3,1},{4,6},{5,7},{6,4},{7,5},{8,10},{9,11},{10,... | collective-permute-start | bytes 294920 | tf_op jit(solution)/shard_map/ppermute | solution.py:227
  7.3 0.7 %fusion = s32[256,16]{0,1:T(8,128)S(1)} fusion(s32[256,16]{0,1:T(8,128)} %param.5, s32[256]{0:T(256)} %param.6), kind=kLoop, calls=%fused_computation.3 | loop fusion | flops 8192 | bytes 33792 | tf_op jit(solution)/shard_map/jit(_where)/select_n | solution.py:258
  8.2 0.6 %collective-permute-start = (s32[32,128]{1,0:T(8,128)S(1)}, s32[32,128]{1,0:T(8,128)S(1)}, u32[]{:S(2)}, u32[]{:S(2)}) collective-permute-start(s32[32,128]{1,0:T(8,128)S(1)} %reshape.11.own_ref), channel_id=1, source_target_pairs={{0,1},{1,0},{2,3},{3,2},{4,5},{5,4},{6,7},{7,6},{8,9},{9,8},{10,11... | collective-permute-start | bytes 49160 | tf_op jit(solution)/shard_map/ppermute | solution.py:239
  8.8 0.3 collective-permute-start.7
  9.1 0.5 %collective-permute-done.twin_ref = s32[32,128]{1,0:T(8,128)S(1)} collective-permute-done((s32[32,128]{1,0:T(8,128)S(1)}, s32[32,128]{1,0:T(8,128)S(1)}, u32[]{:S(2)}, u32[]{:S(2)}) %collective-permute-start) | collective-permute-done | bytes 16416 | tf_op jit(solution)/shard_map/ppermute | solution.py:239
  9.6 1.0 %copy-done = bf16[256,768]{1,0:T(8,128)(2,1)S(1)} copy-done((bf16[256,768]{1,0:T(8,128)(2,1)S(1)}, bf16[256,768]{1,0:T(8,128)(2,1)}, u32[]{:S(2)}) %copy-start) | copy-done | bytes 393240
  10.6 3.0 %counts.1 = (bf16[512,256]{1,0:T(8,128)(2,1)S(1)}, bf16[512,512]{1,0:T(8,128)(2,1)S(1)}, bf16[512,384]{1,0:T(8,128)(2,1)S(1)}, bf16[256,768]{1,0:T(8,128)(2,1)S(1)}, bf16[4096,768]{1,0:T(8,128)(2,1)S(1)}) custom-call(s32[32,128]{1,0:T(8,128)S(1)} %collective-permute-done.twin_ref, s32[32,128]{1,0:T(8,128)S(1)} %reshape.11.own_ref, ...), custom_call_target="tpu_custom_call" | custom-call | flops 536870912 | bytes 262144 | tf_op jit(solution)/shard_map/counts/pallas_call | solution.py:263
  13.6 0.5 %collective-permute-start.4 = (bf16[64,768]{1,0:T(8,128)(2,1)S(1)}, bf16[64,768]{1,0:T(8,128)(2,1)S(1)}, u32[]{:S(2)}, u32[]{:S(2)}) collective-permute-start(bf16[64,768]{1,0:T(8,128)(2,1)S(1)} %collective-permute-done.3.rest_1_), channel_id=1, source_target_pairs={{0,2},{1,3},{2,0},{3,1},{4,6},{5,7},{6,4},{7,5},{8,10},{9,11},{10,... | collective-permute-start | bytes 294920 | tf_op jit(solution)/shard_map/ppermute | solution.py:227
  14.2 1.6 %collective-permute-start.5 = (bf16[128,768]{1,0:T(8,128)(2,1)S(1)}, bf16[128,768]{1,0:T(8,128)(2,1)S(1)}, u32[]{:S(2)}, u32[]{:S(2)}) collective-permute-start(bf16[128,768]{1,0:T(8,128)(2,1)S(1)} %constant_dynamic-update-slice_fusion), channel_id=1, source_target_pairs={{0,8},{1,17},{2,10},{3,19},{4,12},{5,21},{6,14},{7,23},{8,0},{9,25... | collective-permute-start | bytes 589832 | tf_op jit(solution)/shard_map/ppermute | solution.py:246
  15.7 1.5 %collective-permute-start.6 = (bf16[128,768]{1,0:T(8,128)(2,1)S(1)}, bf16[128,768]{1,0:T(8,128)(2,1)S(1)}, u32[]{:S(2)}, u32[]{:S(2)}) collective-permute-start(bf16[128,768]{1,0:T(8,128)(2,1)S(1)} %constant_dynamic-update-slice_fusion), channel_id=1, source_target_pairs={{0,16},{1,9},{2,18},{3,11},{4,20},{5,13},{6,22},{7,15},{8,24},{9,1... | collective-permute-start | bytes 589832 | tf_op jit(solution)/shard_map/ppermute | solution.py:246
  17.3 1.5 %collective-permute-done.4.rest_2_.last_ref = bf16[64,768]{1,0:T(8,128)(2,1)S(1)} collective-permute-done((bf16[64,768]{1,0:T(8,128)(2,1)S(1)}, bf16[64,768]{1,0:T(8,128)(2,1)S(1)}, u32[]{:S(2)}, u32[]{:S(2)}) %collective-permute-start.4) | collective-permute-done | bytes 98336 | tf_op jit(solution)/shard_map/ppermute | solution.py:227
  18.8 1.6 %collective-permute-start.10 = (bf16[64,768]{1,0:T(8,128)(2,1)S(1)}, bf16[64,768]{1,0:T(8,128)(2,1)S(1)}, u32[]{:S(2)}, u32[]{:S(2)}) collective-permute-start(bf16[64,768]{1,0:T(8,128)(2,1)S(1)} %get-tuple-element.16), channel_id=1, source_target_pairs={{0,16},{1,9},{2,18},{3,11},{4,20},{5,13},{6,22},{7,15},{8,24},{9,1... | collective-permute-start | bytes 294920 | tf_op jit(solution)/shard_map/ppermute | solution.py:246
  20.4 1.5 %collective-permute-start.9 = (bf16[64,768]{1,0:T(8,128)(2,1)S(1)}, bf16[64,768]{1,0:T(8,128)(2,1)S(1)}, u32[]{:S(2)}, u32[]{:S(2)}) collective-permute-start(bf16[64,768]{1,0:T(8,128)(2,1)S(1)} %get-tuple-element.16), channel_id=1, source_target_pairs={{0,8},{1,17},{2,10},{3,19},{4,12},{5,21},{6,14},{7,23},{8,0},{9,25... | collective-permute-start | bytes 294920 | tf_op jit(solution)/shard_map/ppermute | solution.py:246
  21.9 0.5 collective-permute-start.8
  22.3 1.1 %own_sums.1.rest_5_ = f32[512,768]{1,0:T(8,128)S(1)} custom-call(bf16[256,768]{1,0:T(8,128)(2,1)S(1)} %collective-permute-done.1.twin_ref.dest_ref, bf16[256,768]{1,0:T(8,128)(2,1)S(1)} %get-tuple-element.11.own_ref.rest_0_.rest_2_.dest_ref, bf16[512,256]{1,0:T(8,128)(2,1)S(1)} %get-tuple-element.13.counts_ref, ...), custom_call_target="tpu_custom_call" | custom-call | flops 2147483648 | bytes 262144 | tf_op jit(solution)/shard_map/own_sums/pallas_call | solution.py:306
  23.5 1.8 %near_sums.1.early_ref = f32[512,768]{1,0:T(8,128)S(1)} custom-call(bf16[256,768]{1,0:T(8,128)(2,1)S(1)} %collective-permute-done.1.twin_ref.dest_ref, bf16[256,768]{1,0:T(8,128)(2,1)S(1)} %get-tuple-element.11.own_ref.rest_0_.rest_2_.dest_ref, bf16[512,512]{1,0:T(8,128)(2,1)S(1)} %get-tuple-element.12.counts_ref, ...), custom_call_target="tpu_custom_call" | custom-call | flops 67108864 | bytes 262144 | tf_op jit(solution)/shard_map/near_sums/pallas_call | solution.py:306
  25.3 2.4 %collective-permute-done.8.rest_1_ = bf16[128,768]{1,0:T(8,128)(2,1)S(1)} collective-permute-done((bf16[128,768]{1,0:T(8,128)(2,1)S(1)}, bf16[128,768]{1,0:T(8,128)(2,1)S(1)}, u32[]{:S(2)}, u32[]{:S(2)}) %collective-permute-start.8) | collective-permute-done | bytes 196640 | tf_op jit(solution)/shard_map/ppermute | solution.py:227
  27.6 1.1 %late_sums.3.twin_a_ref = f32[256,768]{1,0:T(8,128)S(1)} custom-call(bf16[256,768]{1,0:T(8,128)(2,1)S(1)} %collective-permute-done.1.twin_ref.dest_ref, f32[512,768]{1,0:T(8,128)S(1)} %near_sums.1.early_ref, bf16[512,384]{1,0:T(8,128)(2,1)S(1)} %get-tuple-element.14.counts_ref, bf16[64,768]{1,0:T(8,128)(2,1)S(1)} %collective-permute-done.7.rest_1_.rest_0_, ...), custom_call_target="tpu_custom_call" | custom-call | tf_op jit(solution)/shard_map/late_sums/pallas_call | solution.py:320
  28.8 1.1 %late_sums.2.own_a_ref = f32[256,768]{1,0:T(8,128)S(1)} custom-call(bf16[256,768]{1,0:T(8,128)(2,1)S(1)} %get-tuple-element.11.own_ref.rest_0_.rest_2_.dest_ref, f32[512,768]{1,0:T(8,128)S(1)} %near_sums.1.early_ref, bf16[512,384]{1,0:T(8,128)(2,1)S(1)} %get-tuple-element.14.counts_ref, bf16[64,768]{1,0:T(8,128)(2,1)S(1)} %collective-permute-done.7.rest_1_.rest_0_, ...), custom_call_target="tpu_custom_call" | custom-call | tf_op jit(solution)/shard_map/late_sums/pallas_call | solution.py:320
  29.9 0.6 %collective-permute-start.12 = (f32[256,768]{1,0:T(8,128)S(1)}, f32[256,768]{1,0:T(8,128)S(1)}, u32[]{:S(2)}, u32[]{:S(2)}) collective-permute-start(f32[256,768]{1,0:T(8,128)S(1)} %late_sums.2.own_a_ref), channel_id=1, source_target_pairs={{0,1},{1,0},{2,3},{3,2},{4,5},{5,4},{6,7},{7,6},{8,9},{9,8},{10,11... | collective-permute-start | bytes 2359304 | tf_op jit(solution)/shard_map/ppermute | solution.py:239
  30.5 0.6 %collective-permute-done.11.own_b_ref = f32[256,768]{1,0:T(8,128)S(1)} collective-permute-done((f32[256,768]{1,0:T(8,128)S(1)}, f32[256,768]{1,0:T(8,128)S(1)}, u32[]{:S(2)}, u32[]{:S(2)}) %collective-permute-start.11) | collective-permute-done | bytes 786464 | tf_op jit(solution)/shard_map/ppermute | solution.py:239
  31.1 1.3 %collective-permute-done.12.twin_b_ref = f32[256,768]{1,0:T(8,128)S(1)} collective-permute-done((f32[256,768]{1,0:T(8,128)S(1)}, f32[256,768]{1,0:T(8,128)S(1)}, u32[]{:S(2)}, u32[]{:S(2)}) %collective-permute-start.12) | collective-permute-done | bytes 786464 | tf_op jit(solution)/shard_map/ppermute | solution.py:239
  32.4 7.6 %scores.1 = (bf16[256,768]{1,0:T(8,128)(2,1)}, f32[64,128]{1,0:T(8,128)S(1)}) custom-call(f32[256,768]{1,0:T(8,128)S(1)} %late_sums.2.own_a_ref, f32[256,768]{1,0:T(8,128)S(1)} %collective-permute-done.11.own_b_ref, f32[256,768]{1,0:T(8,128)S(1)} %late_sums.3.twin_a_ref, f32[256,768]{1,0:T(8,128)S(1)} %collective-permute-done.12.twin_b_ref, ...), custom_call_target="tpu_custom_call" | custom-call | flops 6442450944 | bytes 12582912 | tf_op jit(solution)/shard_map/scores/pallas_call | solution.py:335
  40.0 1.7 %collective-permute-start.13 = (f32[64,128]{1,0:T(8,128)S(1)}, f32[64,128]{1,0:T(8,128)S(1)}, u32[]{:S(2)}, u32[]{:S(2)}) collective-permute-start(f32[64,128]{1,0:T(8,128)S(1)} %get-tuple-element.19), channel_id=1, source_target_pairs={{0,6},{1,7},{2,4},{3,5},{4,2},{5,3},{6,0},{7,1},{8,14},{9,15},{10,... | collective-permute-start | bytes 98312 | tf_op jit(solution)/shard_map/ppermute | solution.py:227
  41.7 0.3 collective-permute-start.14
  42.0 2.5 %collective-permute-start.15 = (f32[64,128]{1,0:T(8,128)S(1)}, f32[64,128]{1,0:T(8,128)S(1)}, u32[]{:S(2)}, u32[]{:S(2)}) collective-permute-start(f32[64,128]{1,0:T(8,128)S(1)} %get-tuple-element.19), channel_id=1, source_target_pairs={{0,2},{1,3},{2,0},{3,1},{4,6},{5,7},{6,4},{7,5},{8,10},{9,11},{10,... | collective-permute-start | bytes 98312 | tf_op jit(solution)/shard_map/ppermute | solution.py:227
  44.5 1.5 %collective-permute-done.13 = f32[64,128]{1,0:T(8,128)S(1)} collective-permute-done((f32[64,128]{1,0:T(8,128)S(1)}, f32[64,128]{1,0:T(8,128)S(1)}, u32[]{:S(2)}, u32[]{:S(2)}) %collective-permute-start.13) | collective-permute-done | bytes 32800 | tf_op jit(solution)/shard_map/ppermute | solution.py:227
  46.0 1.0 %collective-permute-done.14 = f32[64,128]{1,0:T(8,128)S(1)} collective-permute-done((f32[64,128]{1,0:T(8,128)S(1)}, f32[64,128]{1,0:T(8,128)S(1)}, u32[]{:S(2)}, u32[]{:S(2)}) %collective-permute-start.14) | collective-permute-done | bytes 32800 | tf_op jit(solution)/shard_map/ppermute | solution.py:227
  47.1 1.2 %collective-permute-done.16 = f32[64,128]{1,0:T(8,128)S(1)} collective-permute-done((f32[64,128]{1,0:T(8,128)S(1)}, f32[64,128]{1,0:T(8,128)S(1)}, u32[]{:S(2)}, u32[]{:S(2)}) %collective-permute-start.16) | collective-permute-done | bytes 32800 | tf_op jit(solution)/shard_map/ppermute | solution.py:239
  48.3 0.6 %maximum_bitcast_fusion = f32[16384]{0:T(1024)} fusion(f32[64,128]{1,0:T(8,128)S(1)} %get-tuple-element.23, f32[64,128]{1,0:T(8,128)S(1)} %get-tuple-element.22), kind=kLoop, calls=%fused_computation | loop fusion | flops 16384 | bytes 131072 | tf_op jit(solution)/shard_map/reshape | solution.py:361
  (20 shorter events, 0.4 us)
Async XLA Ops:
  1.6 12.0 %collective-permute-start.3 = (bf16[64,768]{1,0:T(8,128)(2,1)S(1)}, bf16[64,768]{1,0:T(8,128)(2,1)S(1)}, u32[]{:S(2)}, u32[]{:S(2)}) collective-permute-start(bf16[64,768]{1,0:T(8,128)(2,1)S(1)} %get-tuple-element.21), channel_id=1, source_target_pairs={{0,4},{1,5},{2,6},{3,7},{4,0},{5,1},{6,2},{7,3},{8,12},{9,13},{10,... | collective-permute-start | bytes 294920 | tf_op jit(solution)/shard_map/ppermute | solution.py:227
  5.7 8.5 %collective-permute-start.2 = (bf16[64,768]{1,0:T(8,128)(2,1)S(1)}, bf16[64,768]{1,0:T(8,128)(2,1)S(1)}, u32[]{:S(2)}, u32[]{:S(2)}) collective-permute-start(bf16[64,768]{1,0:T(8,128)(2,1)S(1)} %get-tuple-element.21), channel_id=1, source_target_pairs={{0,2},{1,3},{2,0},{3,1},{4,6},{5,7},{6,4},{7,5},{8,10},{9,11},{10,... | collective-permute-start | bytes 294920 | tf_op jit(solution)/shard_map/ppermute | solution.py:227
  7.3 14.6 %collective-permute-start.1 = (bf16[256,768]{1,0:T(8,128)(2,1)}, bf16[256,768]{1,0:T(8,128)(2,1)S(1)}, u32[]{:S(2)}, u32[]{:S(2)}) collective-permute-start(bf16[256,768]{1,0:T(8,128)(2,1)} %database_ref.1), channel_id=1, source_target_pairs={{0,1},{1,0},{2,3},{3,2},{4,5},{5,4},{6,7},{7,6},{8,9},{9,8},{10,11... | collective-permute-start | bytes 1179656 | tf_op jit(solution)/shard_map/ppermute | solution.py:239
  8.2 1.4 %collective-permute-start = (s32[32,128]{1,0:T(8,128)S(1)}, s32[32,128]{1,0:T(8,128)S(1)}, u32[]{:S(2)}, u32[]{:S(2)}) collective-permute-start(s32[32,128]{1,0:T(8,128)S(1)} %reshape.11.own_ref), channel_id=1, source_target_pairs={{0,1},{1,0},{2,3},{3,2},{4,5},{5,4},{6,7},{7,6},{8,9},{9,8},{10,11... | collective-permute-start | bytes 49160 | tf_op jit(solution)/shard_map/ppermute | solution.py:239
  8.8 8.5 %collective-permute-start.7 = (bf16[64,768]{1,0:T(8,128)(2,1)S(1)}, bf16[64,768]{1,0:T(8,128)(2,1)S(1)}, u32[]{:S(2)}, u32[]{:S(2)}) collective-permute-start(bf16[64,768]{1,0:T(8,128)(2,1)S(1)} %get-tuple-element.20.rest_0_), channel_id=1, source_target_pairs={{0,4},{1,5},{2,6},{3,7},{4,0},{5,1},{6,2},{7,3},{8,12},{9,13},{10,... | collective-permute-start | bytes 294920 | tf_op jit(solution)/shard_map/ppermute | solution.py:227
  9.6 1.0 %copy-start = (bf16[256,768]{1,0:T(8,128)(2,1)S(1)}, bf16[256,768]{1,0:T(8,128)(2,1)}, u32[]{:S(2)}) copy-start(bf16[256,768]{1,0:T(8,128)(2,1)} %database_ref.1) | copy-start | bytes 1179652
  13.6 5.1 %collective-permute-start.4 = (bf16[64,768]{1,0:T(8,128)(2,1)S(1)}, bf16[64,768]{1,0:T(8,128)(2,1)S(1)}, u32[]{:S(2)}, u32[]{:S(2)}) collective-permute-start(bf16[64,768]{1,0:T(8,128)(2,1)S(1)} %collective-permute-done.3.rest_1_), channel_id=1, source_target_pairs={{0,2},{1,3},{2,0},{3,1},{4,6},{5,7},{6,4},{7,5},{8,10},{9,11},{10,... | collective-permute-start | bytes 294920 | tf_op jit(solution)/shard_map/ppermute | solution.py:227
  14.2 9.3 %collective-permute-start.5 = (bf16[128,768]{1,0:T(8,128)(2,1)S(1)}, bf16[128,768]{1,0:T(8,128)(2,1)S(1)}, u32[]{:S(2)}, u32[]{:S(2)}) collective-permute-start(bf16[128,768]{1,0:T(8,128)(2,1)S(1)} %constant_dynamic-update-slice_fusion), channel_id=1, source_target_pairs={{0,8},{1,17},{2,10},{3,19},{4,12},{5,21},{6,14},{7,23},{8,0},{9,25... | collective-permute-start | bytes 589832 | tf_op jit(solution)/shard_map/ppermute | solution.py:246
  15.7 7.7 %collective-permute-start.6 = (bf16[128,768]{1,0:T(8,128)(2,1)S(1)}, bf16[128,768]{1,0:T(8,128)(2,1)S(1)}, u32[]{:S(2)}, u32[]{:S(2)}) collective-permute-start(bf16[128,768]{1,0:T(8,128)(2,1)S(1)} %constant_dynamic-update-slice_fusion), channel_id=1, source_target_pairs={{0,16},{1,9},{2,18},{3,11},{4,20},{5,13},{6,22},{7,15},{8,24},{9,1... | collective-permute-start | bytes 589832 | tf_op jit(solution)/shard_map/ppermute | solution.py:246
  18.8 6.5 %collective-permute-start.10 = (bf16[64,768]{1,0:T(8,128)(2,1)S(1)}, bf16[64,768]{1,0:T(8,128)(2,1)S(1)}, u32[]{:S(2)}, u32[]{:S(2)}) collective-permute-start(bf16[64,768]{1,0:T(8,128)(2,1)S(1)} %get-tuple-element.16), channel_id=1, source_target_pairs={{0,16},{1,9},{2,18},{3,11},{4,20},{5,13},{6,22},{7,15},{8,24},{9,1... | collective-permute-start | bytes 294920 | tf_op jit(solution)/shard_map/ppermute | solution.py:246
  20.4 4.9 %collective-permute-start.9 = (bf16[64,768]{1,0:T(8,128)(2,1)S(1)}, bf16[64,768]{1,0:T(8,128)(2,1)S(1)}, u32[]{:S(2)}, u32[]{:S(2)}) collective-permute-start(bf16[64,768]{1,0:T(8,128)(2,1)S(1)} %get-tuple-element.16), channel_id=1, source_target_pairs={{0,8},{1,17},{2,10},{3,19},{4,12},{5,21},{6,14},{7,23},{8,0},{9,25... | collective-permute-start | bytes 294920 | tf_op jit(solution)/shard_map/ppermute | solution.py:246
  21.9 5.8 %collective-permute-start.8 = (bf16[128,768]{1,0:T(8,128)(2,1)S(1)}, bf16[128,768]{1,0:T(8,128)(2,1)S(1)}, u32[]{:S(2)}, u32[]{:S(2)}) collective-permute-start(bf16[128,768]{1,0:T(8,128)(2,1)S(1)} %get-tuple-element.15), channel_id=1, source_target_pairs={{0,2},{1,3},{2,0},{3,1},{4,6},{5,7},{6,4},{7,5},{8,10},{9,11},{10,... | collective-permute-start | bytes 589832 | tf_op jit(solution)/shard_map/ppermute | solution.py:227
  28.7 2.4 %collective-permute-start.11 = (f32[256,768]{1,0:T(8,128)S(1)}, f32[256,768]{1,0:T(8,128)S(1)}, u32[]{:S(2)}, u32[]{:S(2)}) collective-permute-start(f32[256,768]{1,0:T(8,128)S(1)} %late_sums.3.twin_a_ref), channel_id=1, source_target_pairs={{0,1},{1,0},{2,3},{3,2},{4,5},{5,4},{6,7},{7,6},{8,9},{9,8},{10,11... | collective-permute-start | bytes 2359304 | tf_op jit(solution)/shard_map/ppermute | solution.py:239
  29.9 2.5 %collective-permute-start.12 = (f32[256,768]{1,0:T(8,128)S(1)}, f32[256,768]{1,0:T(8,128)S(1)}, u32[]{:S(2)}, u32[]{:S(2)}) collective-permute-start(f32[256,768]{1,0:T(8,128)S(1)} %late_sums.2.own_a_ref), channel_id=1, source_target_pairs={{0,1},{1,0},{2,3},{3,2},{4,5},{5,4},{6,7},{7,6},{8,9},{9,8},{10,11... | collective-permute-start | bytes 2359304 | tf_op jit(solution)/shard_map/ppermute | solution.py:239
  40.0 6.0 %collective-permute-start.13 = (f32[64,128]{1,0:T(8,128)S(1)}, f32[64,128]{1,0:T(8,128)S(1)}, u32[]{:S(2)}, u32[]{:S(2)}) collective-permute-start(f32[64,128]{1,0:T(8,128)S(1)} %get-tuple-element.19), channel_id=1, source_target_pairs={{0,6},{1,7},{2,4},{3,5},{4,2},{5,3},{6,0},{7,1},{8,14},{9,15},{10,... | collective-permute-start | bytes 98312 | tf_op jit(solution)/shard_map/ppermute | solution.py:227
  41.7 5.3 %collective-permute-start.14 = (f32[64,128]{1,0:T(8,128)S(1)}, f32[64,128]{1,0:T(8,128)S(1)}, u32[]{:S(2)}, u32[]{:S(2)}) collective-permute-start(f32[64,128]{1,0:T(8,128)S(1)} %get-tuple-element.19), channel_id=1, source_target_pairs={{0,4},{1,5},{2,6},{3,7},{4,0},{5,1},{6,2},{7,3},{8,12},{9,13},{10,... | collective-permute-start | bytes 98312 | tf_op jit(solution)/shard_map/ppermute | solution.py:227
  42.0 5.0 %collective-permute-start.15 = (f32[64,128]{1,0:T(8,128)S(1)}, f32[64,128]{1,0:T(8,128)S(1)}, u32[]{:S(2)}, u32[]{:S(2)}) collective-permute-start(f32[64,128]{1,0:T(8,128)S(1)} %get-tuple-element.19), channel_id=1, source_target_pairs={{0,2},{1,3},{2,0},{3,1},{4,6},{5,7},{6,4},{7,5},{8,10},{9,11},{10,... | collective-permute-start | bytes 98312 | tf_op jit(solution)/shard_map/ppermute | solution.py:227
  47.0 1.3 %collective-permute-start.16 = (f32[64,128]{1,0:T(8,128)S(1)}, f32[64,128]{1,0:T(8,128)S(1)}, u32[]{:S(2)}, u32[]{:S(2)}) collective-permute-start(f32[64,128]{1,0:T(8,128)S(1)} %maximum_maximum_fusion), channel_id=1, source_target_pairs={{0,1},{1,0},{2,3},{3,2},{4,5},{5,4},{6,7},{7,6},{8,9},{9,8},{10,11... | collective-permute-start | bytes 98312 | tf_op jit(solution)/shard_map/ppermute | solution.py:239

commit v4 on v3

--- a/solution.py
+++ b/solution.py
@@ -281,21 +281,6 @@
         cost_estimate=pl.CostEstimate(flops=1<<29, bytes_accessed=4 * rows * rows, transcendentals=0),
         name="counts",
     )(twin_wanted, wanted, database, queries)
-    forward, message = pl.pallas_call(
-        join_kernel,
-        out_shape=[
-            jax.ShapeDtypeStruct((quarter, features), jnp.bfloat16),
-            jax.ShapeDtypeStruct((planes // 2 * quarter, features), jnp.bfloat16),
-        ],
-        in_specs=[vmem] * (2 + planes // 2),
-        out_specs=[vmem] * 2,
-        compiler_params=pltpu.CompilerParams(vmem_limit_bytes=8 * MIB),
-        name="join",
-    )(near[-1], *across, own)
-    across = across[1:] + [along(message, 1)]
-    beside_last = cross(forward, (1, 2))
-    behind_last = cross(forward, (2, 1))
-
     def sums(name, counts, blocks, flops, before=None):
         out = [jax.ShapeDtypeStruct((2 * rows, features), jnp.float32)]
         operands = [twin, own, counts, *blocks]
@@ -313,7 +298,22 @@
             name=name,
         )(*operands)
 
-    (total,) = sums("own_sums", counts[0], [own], 1<<31)
+    (total,) = sums("own_sums", counts[0], [own], 1<<29)
+    forward, message = pl.pallas_call(
+        join_kernel,
+        out_shape=[
+            jax.ShapeDtypeStruct((quarter, features), jnp.bfloat16),
+            jax.ShapeDtypeStruct((planes // 2 * quarter, features), jnp.bfloat16),
+        ],
+        in_specs=[vmem] * (2 + planes // 2),
+        out_specs=[vmem] * 2,
+        compiler_params=pltpu.CompilerParams(vmem_limit_bytes=8 * MIB),
+        name="join",
+    )(near[-1], *across, total)
+    across = across[1:] + [along(message, 1)]
+    beside_last = cross(forward, (1, 2))
+    behind_last = cross(forward, (2, 1))
+
     (total,) = sums("near_sums", counts[1], [*near, beside, behind], 1<<26, total)
 
     def late(number, dest):

time: 49.2 us -> 47.7 us (0.970)
  waiting for transfers between devices: 9.96 us -> 8.44 us
    ppermute x8, waiting for transfers between devices: 6.35 us -> 3.5 us  [along(): return lax.ppermute(value, 'db', pairs)]
    ppermute x4, waiting for transfers between devices: 0.01 us -> 1.33 us  [cross(): return lax.ppermute(value, ('pb', 'db'), pairs)]
    ppermute x4, starting transfers between devices: 6.15 us -> 5.27 us  [cross(): return lax.ppermute(value, ('pb', 'db'), pairs)]
    ppermute x8, starting transfers between devices: 11.4 us -> 12.3 us  [along(): return lax.ppermute(value, 'db', pairs)]
  transfers between devices with their start and end apart: 17 -> 17, of which waited for: 8 -> 9; matrix products, arithmetic and copies ran while one was open for 2% -> 2% of each run, Pallas kernels for 14% -> 15%
where the time goes in v4:
time: 47.7 us; the launch traced here: 47.4 us
  starting transfers between devices  18.9 us (40%)
  Pallas kernels  15.8 us (33%)
  waiting for transfers between devices  8.44 us (18%)
  local copies, waits for them, and re-layouts  2.17 us (5%)
  other arithmetic  1.38 us (3%)
  between operations  0.77 us (2%)
    ppermute x8, starting transfers between devices, along(): return lax.ppermute(value, 'db', pairs)  12.3 us
    pallas_call x1, Pallas kernels, local(): pl.pallas_call(score_kernel, out_shape=[jax.ShapeDtypeStruct((rows, featu...  7.63 us
    ppermute x4, starting transfers between devices, cross(): return lax.ppermute(value, ('pb', 'db'), pairs)  5.27 us
    ppermute x5, waiting for transfers between devices, swap(): return lax.ppermute(value, 'db', [(i, i ^ 1) for i in range(owners)])  3.6 us
    ppermute x8, waiting for transfers between devices, along(): return lax.ppermute(value, 'db', pairs)  3.5 us
    pallas_call x1, Pallas kernels, local(): pl.pallas_call(functools.partial(count_kernel, planes), out_shape=[jax.Sh...  3 us
    pallas_call x2, Pallas kernels, sums(): pl.pallas_call(functools.partial(sums_kernel, len(blocks)), out_shape=out...  2.93 us
    pallas_call x2, Pallas kernels, late(): pl.pallas_call(functools.partial(late_kernel, number), out_shape=jax.Shap...  2.18 us
  transfers between devices with their start and end apart: 17, of which 9 were waited for; matrix products, arithmetic and copies ran while one was open for 2% of the time, Pallas kernels for 15%

profile of v4, /device:TPU:0, one launch (start us, length us, event | category | flops | bytes accessed | tf_op | source)
XLA Modules:
  0.0 47.4 jit_solution(8320780180336057015)
XLA Ops:
  0.6 1.0 %constant_dynamic-slice_fusion = (bf16[64,768]{1,0:T(8,128)(2,1)S(1)}, bf16[64,768]{1,0:T(8,128)(2,1)S(1)}) fusion(bf16[256,768]{1,0:T(8,128)(2,1)} %database_ref.1, s32[]{:T(128)S(6)} %select_n.31, s32[]{:T(128)S(6)} %select_n.30), kind=kLoop, calls=%fused_computation.8 | loop fusion | bytes 393224 | tf_op jit(solution)/shard_map/dynamic_slice | solution.py:249
  1.6 4.1 %collective-permute-start.3 = (bf16[64,768]{1,0:T(8,128)(2,1)S(1)}, bf16[64,768]{1,0:T(8,128)(2,1)S(1)}, u32[]{:S(2)}, u32[]{:S(2)}) collective-permute-start(bf16[64,768]{1,0:T(8,128)(2,1)S(1)} %get-tuple-element.21), channel_id=1, source_target_pairs={{0,4},{1,5},{2,6},{3,7},{4,0},{5,1},{6,2},{7,3},{8,12},{9,13},{10,... | collective-permute-start | bytes 294920 | tf_op jit(solution)/shard_map/ppermute | solution.py:227
  5.7 1.6 %collective-permute-start.2 = (bf16[64,768]{1,0:T(8,128)(2,1)S(1)}, bf16[64,768]{1,0:T(8,128)(2,1)S(1)}, u32[]{:S(2)}, u32[]{:S(2)}) collective-permute-start(bf16[64,768]{1,0:T(8,128)(2,1)S(1)} %get-tuple-element.21), channel_id=1, source_target_pairs={{0,2},{1,3},{2,0},{3,1},{4,6},{5,7},{6,4},{7,5},{8,10},{9,11},{10,... | collective-permute-start | bytes 294920 | tf_op jit(solution)/shard_map/ppermute | solution.py:227
  7.3 0.7 %fusion = s32[256,16]{0,1:T(8,128)S(1)} fusion(s32[256,16]{0,1:T(8,128)} %param.5, s32[256]{0:T(256)} %param.6), kind=kLoop, calls=%fused_computation.3 | loop fusion | flops 8192 | bytes 33792 | tf_op jit(solution)/shard_map/jit(_where)/select_n | solution.py:258
  8.2 0.6 %collective-permute-start = (s32[32,128]{1,0:T(8,128)S(1)}, s32[32,128]{1,0:T(8,128)S(1)}, u32[]{:S(2)}, u32[]{:S(2)}) collective-permute-start(s32[32,128]{1,0:T(8,128)S(1)} %reshape.11.own_ref), channel_id=1, source_target_pairs={{0,1},{1,0},{2,3},{3,2},{4,5},{5,4},{6,7},{7,6},{8,9},{9,8},{10,11... | collective-permute-start | bytes 49160 | tf_op jit(solution)/shard_map/ppermute | solution.py:239
  8.8 0.3 collective-permute-start.7
  9.1 0.5 %collective-permute-done.twin_ref = s32[32,128]{1,0:T(8,128)S(1)} collective-permute-done((s32[32,128]{1,0:T(8,128)S(1)}, s32[32,128]{1,0:T(8,128)S(1)}, u32[]{:S(2)}, u32[]{:S(2)}) %collective-permute-start) | collective-permute-done | bytes 16416 | tf_op jit(solution)/shard_map/ppermute | solution.py:239
  9.6 1.0 %copy-done = bf16[256,768]{1,0:T(8,128)(2,1)S(1)} copy-done((bf16[256,768]{1,0:T(8,128)(2,1)S(1)}, bf16[256,768]{1,0:T(8,128)(2,1)}, u32[]{:S(2)}) %copy-start) | copy-done | bytes 393240
  10.6 3.0 %counts.1 = (bf16[512,256]{1,0:T(8,128)(2,1)S(1)}, bf16[512,512]{1,0:T(8,128)(2,1)S(1)}, bf16[512,384]{1,0:T(8,128)(2,1)S(1)}, bf16[256,768]{1,0:T(8,128)(2,1)S(1)}, bf16[4096,768]{1,0:T(8,128)(2,1)S(1)}) custom-call(s32[32,128]{1,0:T(8,128)S(1)} %collective-permute-done.twin_ref, s32[32,128]{1,0:T(8,128)S(1)} %reshape.11.own_ref, ...), custom_call_target="tpu_custom_call" | custom-call | flops 536870912 | bytes 262144 | tf_op jit(solution)/shard_map/counts/pallas_call | solution.py:263
  13.6 0.5 %collective-permute-start.4 = (bf16[64,768]{1,0:T(8,128)(2,1)S(1)}, bf16[64,768]{1,0:T(8,128)(2,1)S(1)}, u32[]{:S(2)}, u32[]{:S(2)}) collective-permute-start(bf16[64,768]{1,0:T(8,128)(2,1)S(1)} %collective-permute-done.3.rest_1_), channel_id=1, source_target_pairs={{0,2},{1,3},{2,0},{3,1},{4,6},{5,7},{6,4},{7,5},{8,10},{9,11},{10,... | collective-permute-start | bytes 294920 | tf_op jit(solution)/shard_map/ppermute | solution.py:227
  14.2 1.6 %collective-permute-start.5 = (bf16[128,768]{1,0:T(8,128)(2,1)S(1)}, bf16[128,768]{1,0:T(8,128)(2,1)S(1)}, u32[]{:S(2)}, u32[]{:S(2)}) collective-permute-start(bf16[128,768]{1,0:T(8,128)(2,1)S(1)} %constant_dynamic-update-slice_fusion), channel_id=1, source_target_pairs={{0,8},{1,17},{2,10},{3,19},{4,12},{5,21},{6,14},{7,23},{8,0},{9,25... | collective-permute-start | bytes 589832 | tf_op jit(solution)/shard_map/ppermute | solution.py:246
  15.7 1.5 %collective-permute-start.6 = (bf16[128,768]{1,0:T(8,128)(2,1)S(1)}, bf16[128,768]{1,0:T(8,128)(2,1)S(1)}, u32[]{:S(2)}, u32[]{:S(2)}) collective-permute-start(bf16[128,768]{1,0:T(8,128)(2,1)S(1)} %constant_dynamic-update-slice_fusion), channel_id=1, source_target_pairs={{0,16},{1,9},{2,18},{3,11},{4,20},{5,13},{6,22},{7,15},{8,24},{9,1... | collective-permute-start | bytes 589832 | tf_op jit(solution)/shard_map/ppermute | solution.py:246
  17.3 1.1 %own_sums.1.rest_5_.rest_2_ = f32[512,768]{1,0:T(8,128)S(1)} custom-call(bf16[256,768]{1,0:T(8,128)(2,1)S(1)} %collective-permute-done.1.twin_ref.dest_ref, bf16[256,768]{1,0:T(8,128)(2,1)S(1)} %get-tuple-element.11.own_ref.rest_0_.dest_ref, bf16[512,256]{1,0:T(8,128)(2,1)S(1)} %get-tuple-element.13.counts_ref, ...), custom_call_target="tpu_custom_call" | custom-call | flops 536870912 | bytes 262144 | tf_op jit(solution)/shard_map/own_sums/pallas_call | solution.py:291
  18.8 1.3 %collective-permute-start.8 = (bf16[128,768]{1,0:T(8,128)(2,1)S(1)}, bf16[128,768]{1,0:T(8,128)(2,1)S(1)}, u32[]{:S(2)}, u32[]{:S(2)}) collective-permute-start(bf16[128,768]{1,0:T(8,128)(2,1)S(1)} %get-tuple-element.15), channel_id=1, source_target_pairs={{0,2},{1,3},{2,0},{3,1},{4,6},{5,7},{6,4},{7,5},{8,10},{9,11},{10,... | collective-permute-start | bytes 589832 | tf_op jit(solution)/shard_map/ppermute | solution.py:227
  20.1 0.7 %collective-permute-start.10 = (bf16[64,768]{1,0:T(8,128)(2,1)S(1)}, bf16[64,768]{1,0:T(8,128)(2,1)S(1)}, u32[]{:S(2)}, u32[]{:S(2)}) collective-permute-start(bf16[64,768]{1,0:T(8,128)(2,1)S(1)} %get-tuple-element.16), channel_id=1, source_target_pairs={{0,16},{1,9},{2,18},{3,11},{4,20},{5,13},{6,22},{7,15},{8,24},{9,1... | collective-permute-start | bytes 294920 | tf_op jit(solution)/shard_map/ppermute | solution.py:246
  20.8 1.5 %collective-permute-start.9 = (bf16[64,768]{1,0:T(8,128)(2,1)S(1)}, bf16[64,768]{1,0:T(8,128)(2,1)S(1)}, u32[]{:S(2)}, u32[]{:S(2)}) collective-permute-start(bf16[64,768]{1,0:T(8,128)(2,1)S(1)} %get-tuple-element.16), channel_id=1, source_target_pairs={{0,8},{1,17},{2,10},{3,19},{4,12},{5,21},{6,14},{7,23},{8,0},{9,25... | collective-permute-start | bytes 294920 | tf_op jit(solution)/shard_map/ppermute | solution.py:246
  22.3 1.8 %near_sums.1.early_ref = f32[512,768]{1,0:T(8,128)S(1)} custom-call(bf16[256,768]{1,0:T(8,128)(2,1)S(1)} %collective-permute-done.1.twin_ref.dest_ref, bf16[256,768]{1,0:T(8,128)(2,1)S(1)} %get-tuple-element.11.own_ref.rest_0_.dest_ref, bf16[512,512]{1,0:T(8,128)(2,1)S(1)} %get-tuple-element.12.counts_ref, ...), custom_call_target="tpu_custom_call" | custom-call | flops 67108864 | bytes 262144 | tf_op jit(solution)/shard_map/near_sums/pallas_call | solution.py:291
  24.1 0.6 %collective-permute-done.10.rest_3_ = bf16[64,768]{1,0:T(8,128)(2,1)S(1)} collective-permute-done((bf16[64,768]{1,0:T(8,128)(2,1)S(1)}, bf16[64,768]{1,0:T(8,128)(2,1)S(1)}, u32[]{:S(2)}, u32[]{:S(2)}) %collective-permute-start.10) | collective-permute-done | bytes 98336 | tf_op jit(solution)/shard_map/ppermute | solution.py:246
  24.7 0.7 %collective-permute-done.9.rest_2_ = bf16[64,768]{1,0:T(8,128)(2,1)S(1)} collective-permute-done((bf16[64,768]{1,0:T(8,128)(2,1)S(1)}, bf16[64,768]{1,0:T(8,128)(2,1)S(1)}, u32[]{:S(2)}, u32[]{:S(2)}) %collective-permute-start.9) | collective-permute-done | bytes 98336 | tf_op jit(solution)/shard_map/ppermute | solution.py:246
  25.4 1.1 %late_sums.3.twin_a_ref = f32[256,768]{1,0:T(8,128)S(1)} custom-call(bf16[256,768]{1,0:T(8,128)(2,1)S(1)} %collective-permute-done.1.twin_ref.dest_ref, f32[512,768]{1,0:T(8,128)S(1)} %near_sums.1.early_ref, bf16[512,384]{1,0:T(8,128)(2,1)S(1)} %get-tuple-element.14.counts_ref, bf16[64,768]{1,0:T(8,128)(2,1)S(1)} %collective-permute-done.7.rest_1_.rest_0_, ...), custom_call_target="tpu_custom_call" | custom-call | tf_op jit(solution)/shard_map/late_sums/pallas_call | solution.py:320
  26.6 1.1 %late_sums.2.own_a_ref = f32[256,768]{1,0:T(8,128)S(1)} custom-call(bf16[256,768]{1,0:T(8,128)(2,1)S(1)} %get-tuple-element.11.own_ref.rest_0_.dest_ref, f32[512,768]{1,0:T(8,128)S(1)} %near_sums.1.early_ref, bf16[512,384]{1,0:T(8,128)(2,1)S(1)} %get-tuple-element.14.counts_ref, bf16[64,768]{1,0:T(8,128)(2,1)S(1)} %collective-permute-done.7.rest_1_.rest_0_, ...), custom_call_target="tpu_custom_call" | custom-call | tf_op jit(solution)/shard_map/late_sums/pallas_call | solution.py:320
  27.7 0.6 %collective-permute-start.12 = (f32[256,768]{1,0:T(8,128)S(1)}, f32[256,768]{1,0:T(8,128)S(1)}, u32[]{:S(2)}, u32[]{:S(2)}) collective-permute-start(f32[256,768]{1,0:T(8,128)S(1)} %late_sums.2.own_a_ref), channel_id=1, source_target_pairs={{0,1},{1,0},{2,3},{3,2},{4,5},{5,4},{6,7},{7,6},{8,9},{9,8},{10,11... | collective-permute-start | bytes 2359304 | tf_op jit(solution)/shard_map/ppermute | solution.py:239
  28.3 0.6 %collective-permute-done.11.own_b_ref = f32[256,768]{1,0:T(8,128)S(1)} collective-permute-done((f32[256,768]{1,0:T(8,128)S(1)}, f32[256,768]{1,0:T(8,128)S(1)}, u32[]{:S(2)}, u32[]{:S(2)}) %collective-permute-start.11) | collective-permute-done | bytes 786464 | tf_op jit(solution)/shard_map/ppermute | solution.py:239
  28.9 1.3 %collective-permute-done.12.twin_b_ref = f32[256,768]{1,0:T(8,128)S(1)} collective-permute-done((f32[256,768]{1,0:T(8,128)S(1)}, f32[256,768]{1,0:T(8,128)S(1)}, u32[]{:S(2)}, u32[]{:S(2)}) %collective-permute-start.12) | collective-permute-done | bytes 786464 | tf_op jit(solution)/shard_map/ppermute | solution.py:239
  30.2 7.6 %scores.1 = (bf16[256,768]{1,0:T(8,128)(2,1)}, f32[64,128]{1,0:T(8,128)S(1)}) custom-call(f32[256,768]{1,0:T(8,128)S(1)} %late_sums.2.own_a_ref, f32[256,768]{1,0:T(8,128)S(1)} %collective-permute-done.11.own_b_ref, f32[256,768]{1,0:T(8,128)S(1)} %late_sums.3.twin_a_ref, f32[256,768]{1,0:T(8,128)S(1)} %collective-permute-done.12.twin_b_ref, ...), custom_call_target="tpu_custom_call" | custom-call | flops 6442450944 | bytes 12582912 | tf_op jit(solution)/shard_map/scores/pallas_call | solution.py:335
  37.8 2.8 %collective-permute-start.13 = (f32[64,128]{1,0:T(8,128)S(1)}, f32[64,128]{1,0:T(8,128)S(1)}, u32[]{:S(2)}, u32[]{:S(2)}) collective-permute-start(f32[64,128]{1,0:T(8,128)S(1)} %get-tuple-element.19), channel_id=1, source_target_pairs={{0,6},{1,7},{2,4},{3,5},{4,2},{5,3},{6,0},{7,1},{8,14},{9,15},{10,... | collective-permute-start | bytes 98312 | tf_op jit(solution)/shard_map/ppermute | solution.py:227
  40.6 0.4 collective-permute-start.14
  40.9 1.3 %collective-permute-start.15 = (f32[64,128]{1,0:T(8,128)S(1)}, f32[64,128]{1,0:T(8,128)S(1)}, u32[]{:S(2)}, u32[]{:S(2)}) collective-permute-start(f32[64,128]{1,0:T(8,128)S(1)} %get-tuple-element.19), channel_id=1, source_target_pairs={{0,2},{1,3},{2,0},{3,1},{4,6},{5,7},{6,4},{7,5},{8,10},{9,11},{10,... | collective-permute-start | bytes 98312 | tf_op jit(solution)/shard_map/ppermute | solution.py:227
  42.3 1.6 %collective-permute-done.13 = f32[64,128]{1,0:T(8,128)S(1)} collective-permute-done((f32[64,128]{1,0:T(8,128)S(1)}, f32[64,128]{1,0:T(8,128)S(1)}, u32[]{:S(2)}, u32[]{:S(2)}) %collective-permute-start.13) | collective-permute-done | bytes 32800 | tf_op jit(solution)/shard_map/ppermute | solution.py:227
  43.9 1.6 %collective-permute-done.14 = f32[64,128]{1,0:T(8,128)S(1)} collective-permute-done((f32[64,128]{1,0:T(8,128)S(1)}, f32[64,128]{1,0:T(8,128)S(1)}, u32[]{:S(2)}, u32[]{:S(2)}) %collective-permute-start.14) | collective-permute-done | bytes 32800 | tf_op jit(solution)/shard_map/ppermute | solution.py:227
  45.6 1.2 %collective-permute-done.16 = f32[64,128]{1,0:T(8,128)S(1)} collective-permute-done((f32[64,128]{1,0:T(8,128)S(1)}, f32[64,128]{1,0:T(8,128)S(1)}, u32[]{:S(2)}, u32[]{:S(2)}) %collective-permute-start.16) | collective-permute-done | bytes 32800 | tf_op jit(solution)/shard_map/ppermute | solution.py:239
  46.8 0.6 %maximum_bitcast_fusion = f32[16384]{0:T(1024)} fusion(f32[64,128]{1,0:T(8,128)S(1)} %get-tuple-element.23, f32[64,128]{1,0:T(8,128)S(1)} %get-tuple-element.22), kind=kLoop, calls=%fused_computation | loop fusion | flops 16384 | bytes 131072 | tf_op jit(solution)/shard_map/reshape | solution.py:361
  (20 shorter events, 0.8 us)
Async XLA Ops:
  1.6 12.0 %collective-permute-start.3 = (bf16[64,768]{1,0:T(8,128)(2,1)S(1)}, bf16[64,768]{1,0:T(8,128)(2,1)S(1)}, u32[]{:S(2)}, u32[]{:S(2)}) collective-permute-start(bf16[64,768]{1,0:T(8,128)(2,1)S(1)} %get-tuple-element.21), channel_id=1, source_target_pairs={{0,4},{1,5},{2,6},{3,7},{4,0},{5,1},{6,2},{7,3},{8,12},{9,13},{10,... | collective-permute-start | bytes 294920 | tf_op jit(solution)/shard_map/ppermute | solution.py:227
  5.7 8.5 %collective-permute-start.2 = (bf16[64,768]{1,0:T(8,128)(2,1)S(1)}, bf16[64,768]{1,0:T(8,128)(2,1)S(1)}, u32[]{:S(2)}, u32[]{:S(2)}) collective-permute-start(bf16[64,768]{1,0:T(8,128)(2,1)S(1)} %get-tuple-element.21), channel_id=1, source_target_pairs={{0,2},{1,3},{2,0},{3,1},{4,6},{5,7},{6,4},{7,5},{8,10},{9,11},{10,... | collective-permute-start | bytes 294920 | tf_op jit(solution)/shard_map/ppermute | solution.py:227
  7.3 10.0 %collective-permute-start.1 = (bf16[256,768]{1,0:T(8,128)(2,1)}, bf16[256,768]{1,0:T(8,128)(2,1)S(1)}, u32[]{:S(2)}, u32[]{:S(2)}) collective-permute-start(bf16[256,768]{1,0:T(8,128)(2,1)} %database_ref.1), channel_id=1, source_target_pairs={{0,1},{1,0},{2,3},{3,2},{4,5},{5,4},{6,7},{7,6},{8,9},{9,8},{10,11... | collective-permute-start | bytes 1179656 | tf_op jit(solution)/shard_map/ppermute | solution.py:239
  8.2 1.4 %collective-permute-start = (s32[32,128]{1,0:T(8,128)S(1)}, s32[32,128]{1,0:T(8,128)S(1)}, u32[]{:S(2)}, u32[]{:S(2)}) collective-permute-start(s32[32,128]{1,0:T(8,128)S(1)} %reshape.11.own_ref), channel_id=1, source_target_pairs={{0,1},{1,0},{2,3},{3,2},{4,5},{5,4},{6,7},{7,6},{8,9},{9,8},{10,11... | collective-permute-start | bytes 49160 | tf_op jit(solution)/shard_map/ppermute | solution.py:239
  8.8 9.6 %collective-permute-start.7 = (bf16[64,768]{1,0:T(8,128)(2,1)S(1)}, bf16[64,768]{1,0:T(8,128)(2,1)S(1)}, u32[]{:S(2)}, u32[]{:S(2)}) collective-permute-start(bf16[64,768]{1,0:T(8,128)(2,1)S(1)} %get-tuple-element.20.rest_0_), channel_id=1, source_target_pairs={{0,4},{1,5},{2,6},{3,7},{4,0},{5,1},{6,2},{7,3},{8,12},{9,13},{10,... | collective-permute-start | bytes 294920 | tf_op jit(solution)/shard_map/ppermute | solution.py:227
  9.6 1.0 %copy-start = (bf16[256,768]{1,0:T(8,128)(2,1)S(1)}, bf16[256,768]{1,0:T(8,128)(2,1)}, u32[]{:S(2)}) copy-start(bf16[256,768]{1,0:T(8,128)(2,1)} %database_ref.1) | copy-start | bytes 1179652
  13.6 5.1 %collective-permute-start.4 = (bf16[64,768]{1,0:T(8,128)(2,1)S(1)}, bf16[64,768]{1,0:T(8,128)(2,1)S(1)}, u32[]{:S(2)}, u32[]{:S(2)}) collective-permute-start(bf16[64,768]{1,0:T(8,128)(2,1)S(1)} %collective-permute-done.3.rest_1_), channel_id=1, source_target_pairs={{0,2},{1,3},{2,0},{3,1},{4,6},{5,7},{6,4},{7,5},{8,10},{9,11},{10,... | collective-permute-start | bytes 294920 | tf_op jit(solution)/shard_map/ppermute | solution.py:227
  14.2 8.1 %collective-permute-start.5 = (bf16[128,768]{1,0:T(8,128)(2,1)S(1)}, bf16[128,768]{1,0:T(8,128)(2,1)S(1)}, u32[]{:S(2)}, u32[]{:S(2)}) collective-permute-start(bf16[128,768]{1,0:T(8,128)(2,1)S(1)} %constant_dynamic-update-slice_fusion), channel_id=1, source_target_pairs={{0,8},{1,17},{2,10},{3,19},{4,12},{5,21},{6,14},{7,23},{8,0},{9,25... | collective-permute-start | bytes 589832 | tf_op jit(solution)/shard_map/ppermute | solution.py:246
  15.7 6.6 %collective-permute-start.6 = (bf16[128,768]{1,0:T(8,128)(2,1)S(1)}, bf16[128,768]{1,0:T(8,128)(2,1)S(1)}, u32[]{:S(2)}, u32[]{:S(2)}) collective-permute-start(bf16[128,768]{1,0:T(8,128)(2,1)S(1)} %constant_dynamic-update-slice_fusion), channel_id=1, source_target_pairs={{0,16},{1,9},{2,18},{3,11},{4,20},{5,13},{6,22},{7,15},{8,24},{9,1... | collective-permute-start | bytes 589832 | tf_op jit(solution)/shard_map/ppermute | solution.py:246
  18.8 6.7 %collective-permute-start.8 = (bf16[128,768]{1,0:T(8,128)(2,1)S(1)}, bf16[128,768]{1,0:T(8,128)(2,1)S(1)}, u32[]{:S(2)}, u32[]{:S(2)}) collective-permute-start(bf16[128,768]{1,0:T(8,128)(2,1)S(1)} %get-tuple-element.15), channel_id=1, source_target_pairs={{0,2},{1,3},{2,0},{3,1},{4,6},{5,7},{6,4},{7,5},{8,10},{9,11},{10,... | collective-permute-start | bytes 589832 | tf_op jit(solution)/shard_map/ppermute | solution.py:227
  20.1 4.6 %collective-permute-start.10 = (bf16[64,768]{1,0:T(8,128)(2,1)S(1)}, bf16[64,768]{1,0:T(8,128)(2,1)S(1)}, u32[]{:S(2)}, u32[]{:S(2)}) collective-permute-start(bf16[64,768]{1,0:T(8,128)(2,1)S(1)} %get-tuple-element.16), channel_id=1, source_target_pairs={{0,16},{1,9},{2,18},{3,11},{4,20},{5,13},{6,22},{7,15},{8,24},{9,1... | collective-permute-start | bytes 294920 | tf_op jit(solution)/shard_map/ppermute | solution.py:246
  20.8 4.6 %collective-permute-start.9 = (bf16[64,768]{1,0:T(8,128)(2,1)S(1)}, bf16[64,768]{1,0:T(8,128)(2,1)S(1)}, u32[]{:S(2)}, u32[]{:S(2)}) collective-permute-start(bf16[64,768]{1,0:T(8,128)(2,1)S(1)} %get-tuple-element.16), channel_id=1, source_target_pairs={{0,8},{1,17},{2,10},{3,19},{4,12},{5,21},{6,14},{7,23},{8,0},{9,25... | collective-permute-start | bytes 294920 | tf_op jit(solution)/shard_map/ppermute | solution.py:246
  26.5 2.4 %collective-permute-start.11 = (f32[256,768]{1,0:T(8,128)S(1)}, f32[256,768]{1,0:T(8,128)S(1)}, u32[]{:S(2)}, u32[]{:S(2)}) collective-permute-start(f32[256,768]{1,0:T(8,128)S(1)} %late_sums.3.twin_a_ref), channel_id=1, source_target_pairs={{0,1},{1,0},{2,3},{3,2},{4,5},{5,4},{6,7},{7,6},{8,9},{9,8},{10,11... | collective-permute-start | bytes 2359304 | tf_op jit(solution)/shard_map/ppermute | solution.py:239
  27.7 2.5 %collective-permute-start.12 = (f32[256,768]{1,0:T(8,128)S(1)}, f32[256,768]{1,0:T(8,128)S(1)}, u32[]{:S(2)}, u32[]{:S(2)}) collective-permute-start(f32[256,768]{1,0:T(8,128)S(1)} %late_sums.2.own_a_ref), channel_id=1, source_target_pairs={{0,1},{1,0},{2,3},{3,2},{4,5},{5,4},{6,7},{7,6},{8,9},{9,8},{10,11... | collective-permute-start | bytes 2359304 | tf_op jit(solution)/shard_map/ppermute | solution.py:239
  37.8 6.0 %collective-permute-start.13 = (f32[64,128]{1,0:T(8,128)S(1)}, f32[64,128]{1,0:T(8,128)S(1)}, u32[]{:S(2)}, u32[]{:S(2)}) collective-permute-start(f32[64,128]{1,0:T(8,128)S(1)} %get-tuple-element.19), channel_id=1, source_target_pairs={{0,6},{1,7},{2,4},{3,5},{4,2},{5,3},{6,0},{7,1},{8,14},{9,15},{10,... | collective-permute-start | bytes 98312 | tf_op jit(solution)/shard_map/ppermute | solution.py:227
  40.6 4.9 %collective-permute-start.14 = (f32[64,128]{1,0:T(8,128)S(1)}, f32[64,128]{1,0:T(8,128)S(1)}, u32[]{:S(2)}, u32[]{:S(2)}) collective-permute-start(f32[64,128]{1,0:T(8,128)S(1)} %get-tuple-element.19), channel_id=1, source_target_pairs={{0,4},{1,5},{2,6},{3,7},{4,0},{5,1},{6,2},{7,3},{8,12},{9,13},{10,... | collective-permute-start | bytes 98312 | tf_op jit(solution)/shard_map/ppermute | solution.py:227
  40.9 4.5 %collective-permute-start.15 = (f32[64,128]{1,0:T(8,128)S(1)}, f32[64,128]{1,0:T(8,128)S(1)}, u32[]{:S(2)}, u32[]{:S(2)}) collective-permute-start(f32[64,128]{1,0:T(8,128)S(1)} %get-tuple-element.19), channel_id=1, source_target_pairs={{0,2},{1,3},{2,0},{3,1},{4,6},{5,7},{6,4},{7,5},{8,10},{9,11},{10,... | collective-permute-start | bytes 98312 | tf_op jit(solution)/shard_map/ppermute | solution.py:227
  45.5 1.3 %collective-permute-start.16 = (f32[64,128]{1,0:T(8,128)S(1)}, f32[64,128]{1,0:T(8,128)S(1)}, u32[]{:S(2)}, u32[]{:S(2)}) collective-permute-start(f32[64,128]{1,0:T(8,128)S(1)} %maximum_maximum_fusion), channel_id=1, source_target_pairs={{0,1},{1,0},{2,3},{3,2},{4,5},{5,4},{6,7},{7,6},{8,9},{9,8},{10,11... | collective-permute-start | bytes 98312 | tf_op jit(solution)/shard_map/ppermute | solution.py:239

commit v5 on v4

--- a/solution.py
+++ b/solution.py
@@ -189,7 +189,7 @@
             block_ref = fetched(part - 1)
         height = block_ref.shape[0]
         step = min(1024, height)
-        tile = min(2048, height)
+        tile = min(4096, height)
         before = line_of
         line_of += height // 128
 

time: 47.7 us -> 48.9 us (1.025)
  Pallas kernels: 15.8 us -> 17 us
    pallas_call x1, Pallas kernels: 7.63 us -> 8.85 us  [local(): pl.pallas_call(score_kernel, out_shape=[jax.ShapeDtypeStruct((rows, featu...]
  transfers between devices with their start and end apart: 17 -> 17, of which waited for: 9 -> 9; matrix products, arithmetic and copies ran while one was open for 2% -> 2% of each run, Pallas kernels for 15% -> 14%
where the time goes in v5:
time: 48.9 us; the launch traced here: 48.6 us
  starting transfers between devices  18.9 us (39%)
  Pallas kernels  17 us (35%)
  waiting for transfers between devices  8.43 us (17%)
  local copies, waits for them, and re-layouts  2.17 us (4%)
  other arithmetic  1.38 us (3%)
  between operations  0.77 us (2%)
    ppermute x8, starting transfers between devices, along(): return lax.ppermute(value, 'db', pairs)  12.3 us
    pallas_call x1, Pallas kernels, local(): pl.pallas_call(score_kernel, out_shape=[jax.ShapeDtypeStruct((rows, featu...  8.85 us
    ppermute x4, starting transfers between devices, cross(): return lax.ppermute(value, ('pb', 'db'), pairs)  5.27 us
    ppermute x5, waiting for transfers between devices, swap(): return lax.ppermute(value, 'db', [(i, i ^ 1) for i in range(owners)])  3.6 us
    ppermute x8, waiting for transfers between devices, along(): return lax.ppermute(value, 'db', pairs)  3.5 us
    pallas_call x1, Pallas kernels, local(): pl.pallas_call(functools.partial(count_kernel, planes), out_shape=[jax.Sh...  3 us
    pallas_call x2, Pallas kernels, sums(): pl.pallas_call(functools.partial(sums_kernel, len(blocks)), out_shape=out...  2.93 us
    pallas_call x2, Pallas kernels, late(): pl.pallas_call(functools.partial(late_kernel, number), out_shape=jax.Shap...  2.18 us
  transfers between devices with their start and end apart: 17, of which 9 were waited for; matrix products, arithmetic and copies ran while one was open for 2% of the time, Pallas kernels for 14%

profile of v5, /device:TPU:0, one launch (start us, length us, event | category | flops | bytes accessed | tf_op | source)
XLA Modules:
  0.0 48.6 jit_solution(12420738660729684302)
XLA Ops:
  0.6 1.0 %constant_dynamic-slice_fusion = (bf16[64,768]{1,0:T(8,128)(2,1)S(1)}, bf16[64,768]{1,0:T(8,128)(2,1)S(1)}) fusion(bf16[256,768]{1,0:T(8,128)(2,1)} %database_ref.1, s32[]{:T(128)S(6)} %select_n.31, s32[]{:T(128)S(6)} %select_n.30), kind=kLoop, calls=%fused_computation.8 | loop fusion | bytes 393224 | tf_op jit(solution)/shard_map/dynamic_slice | solution.py:249
  1.6 4.1 %collective-permute-start.3 = (bf16[64,768]{1,0:T(8,128)(2,1)S(1)}, bf16[64,768]{1,0:T(8,128)(2,1)S(1)}, u32[]{:S(2)}, u32[]{:S(2)}) collective-permute-start(bf16[64,768]{1,0:T(8,128)(2,1)S(1)} %get-tuple-element.21), channel_id=1, source_target_pairs={{0,4},{1,5},{2,6},{3,7},{4,0},{5,1},{6,2},{7,3},{8,12},{9,13},{10,... | collective-permute-start | bytes 294920 | tf_op jit(solution)/shard_map/ppermute | solution.py:227
  5.7 1.6 %collective-permute-start.2 = (bf16[64,768]{1,0:T(8,128)(2,1)S(1)}, bf16[64,768]{1,0:T(8,128)(2,1)S(1)}, u32[]{:S(2)}, u32[]{:S(2)}) collective-permute-start(bf16[64,768]{1,0:T(8,128)(2,1)S(1)} %get-tuple-element.21), channel_id=1, source_target_pairs={{0,2},{1,3},{2,0},{3,1},{4,6},{5,7},{6,4},{7,5},{8,10},{9,11},{10,... | collective-permute-start | bytes 294920 | tf_op jit(solution)/shard_map/ppermute | solution.py:227
  7.3 0.7 %fusion = s32[256,16]{0,1:T(8,128)S(1)} fusion(s32[256,16]{0,1:T(8,128)} %param.5, s32[256]{0:T(256)} %param.6), kind=kLoop, calls=%fused_computation.3 | loop fusion | flops 8192 | bytes 33792 | tf_op jit(solution)/shard_map/jit(_where)/select_n | solution.py:258
  8.2 0.6 %collective-permute-start = (s32[32,128]{1,0:T(8,128)S(1)}, s32[32,128]{1,0:T(8,128)S(1)}, u32[]{:S(2)}, u32[]{:S(2)}) collective-permute-start(s32[32,128]{1,0:T(8,128)S(1)} %reshape.11.own_ref), channel_id=1, source_target_pairs={{0,1},{1,0},{2,3},{3,2},{4,5},{5,4},{6,7},{7,6},{8,9},{9,8},{10,11... | collective-permute-start | bytes 49160 | tf_op jit(solution)/shard_map/ppermute | solution.py:239
  8.8 0.3 collective-permute-start.7
  9.1 0.5 %collective-permute-done.twin_ref = s32[32,128]{1,0:T(8,128)S(1)} collective-permute-done((s32[32,128]{1,0:T(8,128)S(1)}, s32[32,128]{1,0:T(8,128)S(1)}, u32[]{:S(2)}, u32[]{:S(2)}) %collective-permute-start) | collective-permute-done | bytes 16416 | tf_op jit(solution)/shard_map/ppermute | solution.py:239
  9.6 1.0 %copy-done = bf16[256,768]{1,0:T(8,128)(2,1)S(1)} copy-done((bf16[256,768]{1,0:T(8,128)(2,1)S(1)}, bf16[256,768]{1,0:T(8,128)(2,1)}, u32[]{:S(2)}) %copy-start) | copy-done | bytes 393240
  10.6 3.0 %counts.1 = (bf16[512,256]{1,0:T(8,128)(2,1)S(1)}, bf16[512,512]{1,0:T(8,128)(2,1)S(1)}, bf16[512,384]{1,0:T(8,128)(2,1)S(1)}, bf16[256,768]{1,0:T(8,128)(2,1)S(1)}, bf16[4096,768]{1,0:T(8,128)(2,1)S(1)}) custom-call(s32[32,128]{1,0:T(8,128)S(1)} %collective-permute-done.twin_ref, s32[32,128]{1,0:T(8,128)S(1)} %reshape.11.own_ref, ...), custom_call_target="tpu_custom_call" | custom-call | flops 536870912 | bytes 262144 | tf_op jit(solution)/shard_map/counts/pallas_call | solution.py:263
  13.6 0.5 %collective-permute-start.4 = (bf16[64,768]{1,0:T(8,128)(2,1)S(1)}, bf16[64,768]{1,0:T(8,128)(2,1)S(1)}, u32[]{:S(2)}, u32[]{:S(2)}) collective-permute-start(bf16[64,768]{1,0:T(8,128)(2,1)S(1)} %collective-permute-done.3.rest_1_), channel_id=1, source_target_pairs={{0,2},{1,3},{2,0},{3,1},{4,6},{5,7},{6,4},{7,5},{8,10},{9,11},{10,... | collective-permute-start | bytes 294920 | tf_op jit(solution)/shard_map/ppermute | solution.py:227
  14.2 1.6 %collective-permute-start.5 = (bf16[128,768]{1,0:T(8,128)(2,1)S(1)}, bf16[128,768]{1,0:T(8,128)(2,1)S(1)}, u32[]{:S(2)}, u32[]{:S(2)}) collective-permute-start(bf16[128,768]{1,0:T(8,128)(2,1)S(1)} %constant_dynamic-update-slice_fusion), channel_id=1, source_target_pairs={{0,8},{1,17},{2,10},{3,19},{4,12},{5,21},{6,14},{7,23},{8,0},{9,25... | collective-permute-start | bytes 589832 | tf_op jit(solution)/shard_map/ppermute | solution.py:246
  15.7 1.5 %collective-permute-start.6 = (bf16[128,768]{1,0:T(8,128)(2,1)S(1)}, bf16[128,768]{1,0:T(8,128)(2,1)S(1)}, u32[]{:S(2)}, u32[]{:S(2)}) collective-permute-start(bf16[128,768]{1,0:T(8,128)(2,1)S(1)} %constant_dynamic-update-slice_fusion), channel_id=1, source_target_pairs={{0,16},{1,9},{2,18},{3,11},{4,20},{5,13},{6,22},{7,15},{8,24},{9,1... | collective-permute-start | bytes 589832 | tf_op jit(solution)/shard_map/ppermute | solution.py:246
  17.3 1.1 %own_sums.1.rest_5_.rest_2_ = f32[512,768]{1,0:T(8,128)S(1)} custom-call(bf16[256,768]{1,0:T(8,128)(2,1)S(1)} %collective-permute-done.1.twin_ref.dest_ref, bf16[256,768]{1,0:T(8,128)(2,1)S(1)} %get-tuple-element.11.own_ref.rest_0_.dest_ref, bf16[512,256]{1,0:T(8,128)(2,1)S(1)} %get-tuple-element.13.counts_ref, ...), custom_call_target="tpu_custom_call" | custom-call | flops 536870912 | bytes 262144 | tf_op jit(solution)/shard_map/own_sums/pallas_call | solution.py:291
  18.8 1.3 %collective-permute-start.8 = (bf16[128,768]{1,0:T(8,128)(2,1)S(1)}, bf16[128,768]{1,0:T(8,128)(2,1)S(1)}, u32[]{:S(2)}, u32[]{:S(2)}) collective-permute-start(bf16[128,768]{1,0:T(8,128)(2,1)S(1)} %get-tuple-element.15), channel_id=1, source_target_pairs={{0,2},{1,3},{2,0},{3,1},{4,6},{5,7},{6,4},{7,5},{8,10},{9,11},{10,... | collective-permute-start | bytes 589832 | tf_op jit(solution)/shard_map/ppermute | solution.py:227
  20.1 0.7 %collective-permute-start.10 = (bf16[64,768]{1,0:T(8,128)(2,1)S(1)}, bf16[64,768]{1,0:T(8,128)(2,1)S(1)}, u32[]{:S(2)}, u32[]{:S(2)}) collective-permute-start(bf16[64,768]{1,0:T(8,128)(2,1)S(1)} %get-tuple-element.16), channel_id=1, source_target_pairs={{0,16},{1,9},{2,18},{3,11},{4,20},{5,13},{6,22},{7,15},{8,24},{9,1... | collective-permute-start | bytes 294920 | tf_op jit(solution)/shard_map/ppermute | solution.py:246
  20.8 1.5 %collective-permute-start.9 = (bf16[64,768]{1,0:T(8,128)(2,1)S(1)}, bf16[64,768]{1,0:T(8,128)(2,1)S(1)}, u32[]{:S(2)}, u32[]{:S(2)}) collective-permute-start(bf16[64,768]{1,0:T(8,128)(2,1)S(1)} %get-tuple-element.16), channel_id=1, source_target_pairs={{0,8},{1,17},{2,10},{3,19},{4,12},{5,21},{6,14},{7,23},{8,0},{9,25... | collective-permute-start | bytes 294920 | tf_op jit(solution)/shard_map/ppermute | solution.py:246
  22.3 1.8 %near_sums.1.early_ref = f32[512,768]{1,0:T(8,128)S(1)} custom-call(bf16[256,768]{1,0:T(8,128)(2,1)S(1)} %collective-permute-done.1.twin_ref.dest_ref, bf16[256,768]{1,0:T(8,128)(2,1)S(1)} %get-tuple-element.11.own_ref.rest_0_.dest_ref, bf16[512,512]{1,0:T(8,128)(2,1)S(1)} %get-tuple-element.12.counts_ref, ...), custom_call_target="tpu_custom_call" | custom-call | flops 67108864 | bytes 262144 | tf_op jit(solution)/shard_map/near_sums/pallas_call | solution.py:291
  24.1 0.6 %collective-permute-done.10.rest_3_ = bf16[64,768]{1,0:T(8,128)(2,1)S(1)} collective-permute-done((bf16[64,768]{1,0:T(8,128)(2,1)S(1)}, bf16[64,768]{1,0:T(8,128)(2,1)S(1)}, u32[]{:S(2)}, u32[]{:S(2)}) %collective-permute-start.10) | collective-permute-done | bytes 98336 | tf_op jit(solution)/shard_map/ppermute | solution.py:246
  24.7 0.7 %collective-permute-done.9.rest_2_ = bf16[64,768]{1,0:T(8,128)(2,1)S(1)} collective-permute-done((bf16[64,768]{1,0:T(8,128)(2,1)S(1)}, bf16[64,768]{1,0:T(8,128)(2,1)S(1)}, u32[]{:S(2)}, u32[]{:S(2)}) %collective-permute-start.9) | collective-permute-done | bytes 98336 | tf_op jit(solution)/shard_map/ppermute | solution.py:246
  25.4 1.1 %late_sums.3.twin_a_ref = f32[256,768]{1,0:T(8,128)S(1)} custom-call(bf16[256,768]{1,0:T(8,128)(2,1)S(1)} %collective-permute-done.1.twin_ref.dest_ref, f32[512,768]{1,0:T(8,128)S(1)} %near_sums.1.early_ref, bf16[512,384]{1,0:T(8,128)(2,1)S(1)} %get-tuple-element.14.counts_ref, bf16[64,768]{1,0:T(8,128)(2,1)S(1)} %collective-permute-done.7.rest_1_.rest_0_, ...), custom_call_target="tpu_custom_call" | custom-call | tf_op jit(solution)/shard_map/late_sums/pallas_call | solution.py:320
  26.6 1.1 %late_sums.2.own_a_ref = f32[256,768]{1,0:T(8,128)S(1)} custom-call(bf16[256,768]{1,0:T(8,128)(2,1)S(1)} %get-tuple-element.11.own_ref.rest_0_.dest_ref, f32[512,768]{1,0:T(8,128)S(1)} %near_sums.1.early_ref, bf16[512,384]{1,0:T(8,128)(2,1)S(1)} %get-tuple-element.14.counts_ref, bf16[64,768]{1,0:T(8,128)(2,1)S(1)} %collective-permute-done.7.rest_1_.rest_0_, ...), custom_call_target="tpu_custom_call" | custom-call | tf_op jit(solution)/shard_map/late_sums/pallas_call | solution.py:320
  27.7 0.6 %collective-permute-start.12 = (f32[256,768]{1,0:T(8,128)S(1)}, f32[256,768]{1,0:T(8,128)S(1)}, u32[]{:S(2)}, u32[]{:S(2)}) collective-permute-start(f32[256,768]{1,0:T(8,128)S(1)} %late_sums.2.own_a_ref), channel_id=1, source_target_pairs={{0,1},{1,0},{2,3},{3,2},{4,5},{5,4},{6,7},{7,6},{8,9},{9,8},{10,11... | collective-permute-start | bytes 2359304 | tf_op jit(solution)/shard_map/ppermute | solution.py:239
  28.3 0.6 %collective-permute-done.11.own_b_ref = f32[256,768]{1,0:T(8,128)S(1)} collective-permute-done((f32[256,768]{1,0:T(8,128)S(1)}, f32[256,768]{1,0:T(8,128)S(1)}, u32[]{:S(2)}, u32[]{:S(2)}) %collective-permute-start.11) | collective-permute-done | bytes 786464 | tf_op jit(solution)/shard_map/ppermute | solution.py:239
  28.9 1.3 %collective-permute-done.12.twin_b_ref = f32[256,768]{1,0:T(8,128)S(1)} collective-permute-done((f32[256,768]{1,0:T(8,128)S(1)}, f32[256,768]{1,0:T(8,128)S(1)}, u32[]{:S(2)}, u32[]{:S(2)}) %collective-permute-start.12) | collective-permute-done | bytes 786464 | tf_op jit(solution)/shard_map/ppermute | solution.py:239
  30.2 8.8 %scores.1 = (bf16[256,768]{1,0:T(8,128)(2,1)}, f32[64,128]{1,0:T(8,128)S(1)}) custom-call(f32[256,768]{1,0:T(8,128)S(1)} %late_sums.2.own_a_ref, f32[256,768]{1,0:T(8,128)S(1)} %collective-permute-done.11.own_b_ref, f32[256,768]{1,0:T(8,128)S(1)} %late_sums.3.twin_a_ref, f32[256,768]{1,0:T(8,128)S(1)} %collective-permute-done.12.twin_b_ref, ...), custom_call_target="tpu_custom_call" | custom-call | flops 6442450944 | bytes 12582912 | tf_op jit(solution)/shard_map/scores/pallas_call | solution.py:335
  39.0 2.8 %collective-permute-start.13 = (f32[64,128]{1,0:T(8,128)S(1)}, f32[64,128]{1,0:T(8,128)S(1)}, u32[]{:S(2)}, u32[]{:S(2)}) collective-permute-start(f32[64,128]{1,0:T(8,128)S(1)} %get-tuple-element.19), channel_id=1, source_target_pairs={{0,6},{1,7},{2,4},{3,5},{4,2},{5,3},{6,0},{7,1},{8,14},{9,15},{10,... | collective-permute-start | bytes 98312 | tf_op jit(solution)/shard_map/ppermute | solution.py:227
  41.8 0.4 collective-permute-start.14
  42.2 1.3 %collective-permute-start.15 = (f32[64,128]{1,0:T(8,128)S(1)}, f32[64,128]{1,0:T(8,128)S(1)}, u32[]{:S(2)}, u32[]{:S(2)}) collective-permute-start(f32[64,128]{1,0:T(8,128)S(1)} %get-tuple-element.19), channel_id=1, source_target_pairs={{0,2},{1,3},{2,0},{3,1},{4,6},{5,7},{6,4},{7,5},{8,10},{9,11},{10,... | collective-permute-start | bytes 98312 | tf_op jit(solution)/shard_map/ppermute | solution.py:227
  43.5 1.6 %collective-permute-done.13 = f32[64,128]{1,0:T(8,128)S(1)} collective-permute-done((f32[64,128]{1,0:T(8,128)S(1)}, f32[64,128]{1,0:T(8,128)S(1)}, u32[]{:S(2)}, u32[]{:S(2)}) %collective-permute-start.13) | collective-permute-done | bytes 32800 | tf_op jit(solution)/shard_map/ppermute | solution.py:227
  45.1 1.6 %collective-permute-done.14 = f32[64,128]{1,0:T(8,128)S(1)} collective-permute-done((f32[64,128]{1,0:T(8,128)S(1)}, f32[64,128]{1,0:T(8,128)S(1)}, u32[]{:S(2)}, u32[]{:S(2)}) %collective-permute-start.14) | collective-permute-done | bytes 32800 | tf_op jit(solution)/shard_map/ppermute | solution.py:227
  46.8 1.2 %collective-permute-done.16 = f32[64,128]{1,0:T(8,128)S(1)} collective-permute-done((f32[64,128]{1,0:T(8,128)S(1)}, f32[64,128]{1,0:T(8,128)S(1)}, u32[]{:S(2)}, u32[]{:S(2)}) %collective-permute-start.16) | collective-permute-done | bytes 32800 | tf_op jit(solution)/shard_map/ppermute | solution.py:239
  48.0 0.6 %maximum_bitcast_fusion = f32[16384]{0:T(1024)} fusion(f32[64,128]{1,0:T(8,128)S(1)} %get-tuple-element.23, f32[64,128]{1,0:T(8,128)S(1)} %get-tuple-element.22), kind=kLoop, calls=%fused_computation | loop fusion | flops 16384 | bytes 131072 | tf_op jit(solution)/shard_map/reshape | solution.py:361
  (20 shorter events, 0.8 us)
Async XLA Ops:
  1.6 12.0 %collective-permute-start.3 = (bf16[64,768]{1,0:T(8,128)(2,1)S(1)}, bf16[64,768]{1,0:T(8,128)(2,1)S(1)}, u32[]{:S(2)}, u32[]{:S(2)}) collective-permute-start(bf16[64,768]{1,0:T(8,128)(2,1)S(1)} %get-tuple-element.21), channel_id=1, source_target_pairs={{0,4},{1,5},{2,6},{3,7},{4,0},{5,1},{6,2},{7,3},{8,12},{9,13},{10,... | collective-permute-start | bytes 294920 | tf_op jit(solution)/shard_map/ppermute | solution.py:227
  5.7 8.5 %collective-permute-start.2 = (bf16[64,768]{1,0:T(8,128)(2,1)S(1)}, bf16[64,768]{1,0:T(8,128)(2,1)S(1)}, u32[]{:S(2)}, u32[]{:S(2)}) collective-permute-start(bf16[64,768]{1,0:T(8,128)(2,1)S(1)} %get-tuple-element.21), channel_id=1, source_target_pairs={{0,2},{1,3},{2,0},{3,1},{4,6},{5,7},{6,4},{7,5},{8,10},{9,11},{10,... | collective-permute-start | bytes 294920 | tf_op jit(solution)/shard_map/ppermute | solution.py:227
  7.3 10.0 %collective-permute-start.1 = (bf16[256,768]{1,0:T(8,128)(2,1)}, bf16[256,768]{1,0:T(8,128)(2,1)S(1)}, u32[]{:S(2)}, u32[]{:S(2)}) collective-permute-start(bf16[256,768]{1,0:T(8,128)(2,1)} %database_ref.1), channel_id=1, source_target_pairs={{0,1},{1,0},{2,3},{3,2},{4,5},{5,4},{6,7},{7,6},{8,9},{9,8},{10,11... | collective-permute-start | bytes 1179656 | tf_op jit(solution)/shard_map/ppermute | solution.py:239
  8.2 1.4 %collective-permute-start = (s32[32,128]{1,0:T(8,128)S(1)}, s32[32,128]{1,0:T(8,128)S(1)}, u32[]{:S(2)}, u32[]{:S(2)}) collective-permute-start(s32[32,128]{1,0:T(8,128)S(1)} %reshape.11.own_ref), channel_id=1, source_target_pairs={{0,1},{1,0},{2,3},{3,2},{4,5},{5,4},{6,7},{7,6},{8,9},{9,8},{10,11... | collective-permute-start | bytes 49160 | tf_op jit(solution)/shard_map/ppermute | solution.py:239
  8.8 9.6 %collective-permute-start.7 = (bf16[64,768]{1,0:T(8,128)(2,1)S(1)}, bf16[64,768]{1,0:T(8,128)(2,1)S(1)}, u32[]{:S(2)}, u32[]{:S(2)}) collective-permute-start(bf16[64,768]{1,0:T(8,128)(2,1)S(1)} %get-tuple-element.20.rest_0_), channel_id=1, source_target_pairs={{0,4},{1,5},{2,6},{3,7},{4,0},{5,1},{6,2},{7,3},{8,12},{9,13},{10,... | collective-permute-start | bytes 294920 | tf_op jit(solution)/shard_map/ppermute | solution.py:227
  9.6 1.0 %copy-start = (bf16[256,768]{1,0:T(8,128)(2,1)S(1)}, bf16[256,768]{1,0:T(8,128)(2,1)}, u32[]{:S(2)}) copy-start(bf16[256,768]{1,0:T(8,128)(2,1)} %database_ref.1) | copy-start | bytes 1179652
  13.6 5.1 %collective-permute-start.4 = (bf16[64,768]{1,0:T(8,128)(2,1)S(1)}, bf16[64,768]{1,0:T(8,128)(2,1)S(1)}, u32[]{:S(2)}, u32[]{:S(2)}) collective-permute-start(bf16[64,768]{1,0:T(8,128)(2,1)S(1)} %collective-permute-done.3.rest_1_), channel_id=1, source_target_pairs={{0,2},{1,3},{2,0},{3,1},{4,6},{5,7},{6,4},{7,5},{8,10},{9,11},{10,... | collective-permute-start | bytes 294920 | tf_op jit(solution)/shard_map/ppermute | solution.py:227
  14.2 8.1 %collective-permute-start.5 = (bf16[128,768]{1,0:T(8,128)(2,1)S(1)}, bf16[128,768]{1,0:T(8,128)(2,1)S(1)}, u32[]{:S(2)}, u32[]{:S(2)}) collective-permute-start(bf16[128,768]{1,0:T(8,128)(2,1)S(1)} %constant_dynamic-update-slice_fusion), channel_id=1, source_target_pairs={{0,8},{1,17},{2,10},{3,19},{4,12},{5,21},{6,14},{7,23},{8,0},{9,25... | collective-permute-start | bytes 589832 | tf_op jit(solution)/shard_map/ppermute | solution.py:246
  15.7 6.6 %collective-permute-start.6 = (bf16[128,768]{1,0:T(8,128)(2,1)S(1)}, bf16[128,768]{1,0:T(8,128)(2,1)S(1)}, u32[]{:S(2)}, u32[]{:S(2)}) collective-permute-start(bf16[128,768]{1,0:T(8,128)(2,1)S(1)} %constant_dynamic-update-slice_fusion), channel_id=1, source_target_pairs={{0,16},{1,9},{2,18},{3,11},{4,20},{5,13},{6,22},{7,15},{8,24},{9,1... | collective-permute-start | bytes 589832 | tf_op jit(solution)/shard_map/ppermute | solution.py:246
  18.8 6.7 %collective-permute-start.8 = (bf16[128,768]{1,0:T(8,128)(2,1)S(1)}, bf16[128,768]{1,0:T(8,128)(2,1)S(1)}, u32[]{:S(2)}, u32[]{:S(2)}) collective-permute-start(bf16[128,768]{1,0:T(8,128)(2,1)S(1)} %get-tuple-element.15), channel_id=1, source_target_pairs={{0,2},{1,3},{2,0},{3,1},{4,6},{5,7},{6,4},{7,5},{8,10},{9,11},{10,... | collective-permute-start | bytes 589832 | tf_op jit(solution)/shard_map/ppermute | solution.py:227
  20.1 4.6 %collective-permute-start.10 = (bf16[64,768]{1,0:T(8,128)(2,1)S(1)}, bf16[64,768]{1,0:T(8,128)(2,1)S(1)}, u32[]{:S(2)}, u32[]{:S(2)}) collective-permute-start(bf16[64,768]{1,0:T(8,128)(2,1)S(1)} %get-tuple-element.16), channel_id=1, source_target_pairs={{0,16},{1,9},{2,18},{3,11},{4,20},{5,13},{6,22},{7,15},{8,24},{9,1... | collective-permute-start | bytes 294920 | tf_op jit(solution)/shard_map/ppermute | solution.py:246
  20.8 4.6 %collective-permute-start.9 = (bf16[64,768]{1,0:T(8,128)(2,1)S(1)}, bf16[64,768]{1,0:T(8,128)(2,1)S(1)}, u32[]{:S(2)}, u32[]{:S(2)}) collective-permute-start(bf16[64,768]{1,0:T(8,128)(2,1)S(1)} %get-tuple-element.16), channel_id=1, source_target_pairs={{0,8},{1,17},{2,10},{3,19},{4,12},{5,21},{6,14},{7,23},{8,0},{9,25... | collective-permute-start | bytes 294920 | tf_op jit(solution)/shard_map/ppermute | solution.py:246
  26.5 2.4 %collective-permute-start.11 = (f32[256,768]{1,0:T(8,128)S(1)}, f32[256,768]{1,0:T(8,128)S(1)}, u32[]{:S(2)}, u32[]{:S(2)}) collective-permute-start(f32[256,768]{1,0:T(8,128)S(1)} %late_sums.3.twin_a_ref), channel_id=1, source_target_pairs={{0,1},{1,0},{2,3},{3,2},{4,5},{5,4},{6,7},{7,6},{8,9},{9,8},{10,11... | collective-permute-start | bytes 2359304 | tf_op jit(solution)/shard_map/ppermute | solution.py:239
  27.7 2.5 %collective-permute-start.12 = (f32[256,768]{1,0:T(8,128)S(1)}, f32[256,768]{1,0:T(8,128)S(1)}, u32[]{:S(2)}, u32[]{:S(2)}) collective-permute-start(f32[256,768]{1,0:T(8,128)S(1)} %late_sums.2.own_a_ref), channel_id=1, source_target_pairs={{0,1},{1,0},{2,3},{3,2},{4,5},{5,4},{6,7},{7,6},{8,9},{9,8},{10,11... | collective-permute-start | bytes 2359304 | tf_op jit(solution)/shard_map/ppermute | solution.py:239
  39.0 6.0 %collective-permute-start.13 = (f32[64,128]{1,0:T(8,128)S(1)}, f32[64,128]{1,0:T(8,128)S(1)}, u32[]{:S(2)}, u32[]{:S(2)}) collective-permute-start(f32[64,128]{1,0:T(8,128)S(1)} %get-tuple-element.19), channel_id=1, source_target_pairs={{0,6},{1,7},{2,4},{3,5},{4,2},{5,3},{6,0},{7,1},{8,14},{9,15},{10,... | collective-permute-start | bytes 98312 | tf_op jit(solution)/shard_map/ppermute | solution.py:227
  41.8 4.9 %collective-permute-start.14 = (f32[64,128]{1,0:T(8,128)S(1)}, f32[64,128]{1,0:T(8,128)S(1)}, u32[]{:S(2)}, u32[]{:S(2)}) collective-permute-start(f32[64,128]{1,0:T(8,128)S(1)} %get-tuple-element.19), channel_id=1, source_target_pairs={{0,4},{1,5},{2,6},{3,7},{4,0},{5,1},{6,2},{7,3},{8,12},{9,13},{10,... | collective-permute-start | bytes 98312 | tf_op jit(solution)/shard_map/ppermute | solution.py:227
  42.2 4.5 %collective-permute-start.15 = (f32[64,128]{1,0:T(8,128)S(1)}, f32[64,128]{1,0:T(8,128)S(1)}, u32[]{:S(2)}, u32[]{:S(2)}) collective-permute-start(f32[64,128]{1,0:T(8,128)S(1)} %get-tuple-element.19), channel_id=1, source_target_pairs={{0,2},{1,3},{2,0},{3,1},{4,6},{5,7},{6,4},{7,5},{8,10},{9,11},{10,... | collective-permute-start | bytes 98312 | tf_op jit(solution)/shard_map/ppermute | solution.py:227
  46.7 1.3 %collective-permute-start.16 = (f32[64,128]{1,0:T(8,128)S(1)}, f32[64,128]{1,0:T(8,128)S(1)}, u32[]{:S(2)}, u32[]{:S(2)}) collective-permute-start(f32[64,128]{1,0:T(8,128)S(1)} %maximum_maximum_fusion), channel_id=1, source_target_pairs={{0,1},{1,0},{2,3},{3,2},{4,5},{5,4},{6,7},{7,6},{8,9},{9,8},{10,11... | collective-permute-start | bytes 98312 | tf_op jit(solution)/shard_map/ppermute | solution.py:239
